TPU v7x, 512 devices: a whole 4x8x8 slice. The times are simulated.
512 devices in a mesh: req: 128 (over y, z, core), mp: 4 (over x).
Axes of the slice: x: 4, y: 8, z: 8, core: 2. Of those that a mesh axis runs over, the one named last changes fastest.
Arguments:
- cand_feats: bfloat16 [65536, 1024], P('req', 'mp'), may hold values from -6 to 6
- cand_perm: int32 [128, 512], P('req'), may hold values from 0 to 511, each once within a row
- w_in: bfloat16 [1024, 4, 1024], P(None, None, 'mp'), may hold values from -0.1875 to 0.1875
- w_out: bfloat16 [1024, 1024], P('mp'), may hold values from -0.1875 to 0.1875
- cache_k: bfloat16 [4096, 32, 1024], P('req', None, 'mp'), may hold values from -6 to 6
- cache_v: bfloat16 [4096, 32, 1024], P('req', None, 'mp'), may hold values from -1.5 to 1.5
- hist_len: int32 [128], P('req'), may hold values from 1 to 4096, as said below
- hist_home: int32 [128], replicated, may hold values from 0 to 127
- hist_slot: int32 [128, 128], replicated, may hold values from 0 to 31
- hist_mask: int32 [128, 4, 128], P('req'), may hold values 0 or 1
Outputs:
- scored: bfloat16 [65536, 1024], P('req', 'mp')
Inputs may be any that keep to these rules, and one draw needn't show every extreme that they name: `cand_perm`: each row is a permutation of 0 to 511. `hist_len`: some request has a history of 4096 events.
All inputs are finite; a program needn't handle non-finite values. No bound on the sum of `hist_mask` on one device may be relied on, other than what follows from the above.
Results may differ from a plain program's by a relative error of at most 0.0067.
Values may be sent and summed in bfloat16 or wider, within the bound.
No kernel may reach another device: no remote copies, remote signals or barrier semaphores. Data moves between devices by JAX's collectives and lax.ppermute only.
A program may use at most 64 MiB of HBM per device.

v0:
```python
import jax
import jax.numpy as jnp
from jax import lax
from jax.sharding import PartitionSpec as P

HEADS = 8
DH = 128
BLK = 32
MAXBLK = 128
GROUP = 128


EPS = 1e-05


def local(
    cand_feats, cand_perm, w_in, w_out, cache_k, cache_v, hist_len, hist_home, hist_slot, hist_mask
):
    shards = lax.axis_size("req")
    own_index = lax.axis_index("req")
    columns = cand_feats.shape[1]
    cand_slot = cand_feats.shape[0] // shards
    arrived = lax.all_to_all(
        cand_feats.reshape(shards, cand_slot, columns),
        "req",
        split_axis=0,
        concat_axis=0,
        tiled=True,
    )
    arrived = arrived.reshape(shards * cand_slot, columns)
    own_rows = jnp.take(arrived, cand_perm[0], axis=0)
    full_rows = lax.all_gather(own_rows, "mp", axis=1, tiled=True)
    cand_count = full_rows.shape[0]
    features = full_rows.astype(jnp.float32)
    centred = features - jnp.mean(features, axis=1, keepdims=True)
    spread = jnp.mean(centred * centred, axis=1, keepdims=True)
    normed = (centred * lax.rsqrt(spread + EPS)).astype(jnp.bfloat16)
    local_width = w_in.shape[2]
    parts = jax.nn.silu(
        jnp.dot(
            normed, w_in.reshape(w_in.shape[0], 4 * local_width), preferred_element_type=jnp.float32
        )
    ).astype(jnp.bfloat16)
    parts = parts.reshape(cand_count, 4, local_width)
    gate_u, value_v, query_q, key_k = (parts[:, 0], parts[:, 1], parts[:, 2], parts[:, 3])
    rounds_here = MAXBLK // shards
    offsets = (own_index - hist_home) % shards
    wanted = offsets[:, None] + jnp.arange(rounds_here, dtype=jnp.int32)[None, :] * shards
    slots = jnp.take_along_axis(hist_slot, wanted, axis=1)
    send_keys = jnp.take(cache_k, slots, axis=0)
    send_values = jnp.take(cache_v, slots, axis=0)
    key_count = MAXBLK * BLK
    own_len = hist_len[0]
    got_keys, got_values = (
        lax.all_to_all(send_keys, "req", split_axis=0, concat_axis=0, tiled=True),
        lax.all_to_all(send_values, "req", split_axis=0, concat_axis=0, tiled=True),
    )
    live_keys = (jnp.arange(key_count, dtype=jnp.int32) < own_len).astype(jnp.float32)
    home_block = hist_home[own_index]
    block_order = jnp.arange(MAXBLK, dtype=jnp.int32)
    source = (home_block + block_order % shards) % shards
    round_at = block_order // shards
    hist_keys = got_keys[source, round_at].reshape(key_count, local_width)
    hist_values = got_values[source, round_at].reshape(key_count, local_width)
    block_mask = jnp.repeat(hist_mask[0].astype(jnp.float32), BLK, axis=1) * live_keys[None, :]
    score_scale = DH ** (-0.5)
    outputs = []
    for head_index in range(local_width // DH):
        lo_col = head_index * DH
        q_head = query_q[:, lo_col : lo_col + DH]
        scores = (
            lax.dot_general(
                q_head,
                hist_keys[:, lo_col : lo_col + DH],
                (((1,), (1,)), ((), ())),
                preferred_element_type=jnp.float32,
            )
            * score_scale
        )
        weights = (
            jax.nn.silu(scores).reshape(cand_count // GROUP, GROUP, key_count)
            * block_mask[:, None, :]
        )
        weights = weights.reshape(cand_count, key_count).astype(jnp.bfloat16)
        own_score = (
            jnp.sum(
                q_head.astype(jnp.float32) * key_k[:, lo_col : lo_col + DH].astype(jnp.float32),
                axis=1,
                keepdims=True,
            )
            * score_scale
        )
        own_term = jax.nn.silu(own_score) * value_v[:, lo_col : lo_col + DH].astype(jnp.float32)
        outputs.append(
            jnp.dot(
                weights, hist_values[:, lo_col : lo_col + DH], preferred_element_type=jnp.float32
            )
            + own_term
        )
    attn = jnp.concatenate(outputs, axis=1)
    width_all = HEADS * DH
    row_total = lax.psum(jnp.sum(attn, axis=1, keepdims=True), "mp")
    attn_mean = row_total / width_all
    attn_centred = attn - attn_mean
    square_total = lax.psum(jnp.sum(attn_centred * attn_centred, axis=1, keepdims=True), "mp")
    attn_spread = square_total / width_all
    hidden = (attn_centred * lax.rsqrt(attn_spread + EPS) * gate_u.astype(jnp.float32)).astype(
        jnp.bfloat16
    )
    mixed = lax.psum_scatter(
        lax.dot_general(
            w_out, hidden, (((0,), (1,)), ((), ())), preferred_element_type=jnp.float32
        ),
        "mp",
        scatter_dimension=0,
        tiled=True,
    ).T
    return (own_rows.astype(jnp.float32) + mixed).astype(jnp.bfloat16)


def solution(mesh):
    in_specs = (
        P("req", "mp"),
        P("req", None),
        P(None, None, "mp"),
        P("mp", None),
        P("req", None, "mp"),
        P("req", None, "mp"),
        P("req"),
        P(),
        P(),
        P("req", None, None),
    )
    out_specs = P("req", "mp")
    return jax.shard_map(local, mesh=mesh, in_specs=in_specs, out_specs=out_specs, check_vma=False)
```

profile of v0, /device:TPU:1, one launch (start us, length us, event | category | flops | bytes accessed | tf_op | source)
XLA Modules:
  0.0 250.5 jit_solution(4905341339986023290)
XLA Ops:
  8.3 18.4 %all-to-all-start = ((bf16[128,4,256]{2,1,0:T(4,128)(2,1)}), bf16[128,4,256]{2,1,0:T(4,128)(2,1)S(1)}, u32[]{:S(2)}, u32[]{:S(2)}) async-start(bf16[128,4,256]{2,1,0:T(4,128)(2,1)} %reshape.284), calls=%async_computation | async-start | bytes 524288 | tf_op jit(solution)/shard_map/all_to_all | solution.py:23
  27.4 1.9 gather_fusion.3
  31.8 2.0 gather_fusion.4
  33.8 4.0 %bitcast_select_fusion = (bf16[128,1,32,256]{3,2,1,0:T(8,128)(2,1)}, bf16[128,1,32,256]{3,2,1,0:T(8,128)(2,1)}) fusion(bf16[128,32,256]{2,1,0:T(8,128)(2,1)S(1)} %gather_fusion.5, pred[128]{0:T(512)(128)(4,1)S(1)} %and_bitcast_fusion, bf16[128,32,256]{2,1,0:T(8,128)(2,1)} %gather_fusion.4), kind=kLoop, calls=%fused_computation.16 | loop fusion | flops 2097152 | bytes 8388736 | tf_op jit(solution)/shard_map/jit(_take)/select_n | solution.py:51
  37.9 3.1 %all-to-all-done = bf16[128,4,256]{2,1,0:T(4,128)(2,1)S(1)} async-done(((bf16[128,4,256]{2,1,0:T(4,128)(2,1)}), bf16[128,4,256]{2,1,0:T(4,128)(2,1)S(1)}, u32[]{:S(2)}, u32[]{:S(2)}) %all-to-all-start) | async-done | bytes 262176 | tf_op jit(solution)/shard_map/all_to_all | solution.py:23
  41.0 10.8 %all-to-all-start.1 = ((bf16[128,1,32,256]{3,2,1,0:T(8,128)(2,1)}), bf16[128,1,32,256]{3,2,1,0:T(8,128)(2,1)S(1)}, u32[]{:S(2)}, u32[]{:S(2)}) async-start(bf16[128,1,32,256]{3,2,1,0:T(8,128)(2,1)} %get-tuple-element.13), calls=%async_computation.1 | async-start | bytes 4194304 | tf_op jit(solution)/shard_map/all_to_all | solution.py:55
  51.8 52.1 %all-to-all-done.1 = bf16[128,1,32,256]{3,2,1,0:T(8,128)(2,1)S(1)} async-done(((bf16[128,1,32,256]{3,2,1,0:T(8,128)(2,1)}), bf16[128,1,32,256]{3,2,1,0:T(8,128)(2,1)S(1)}, u32[]{:S(2)}, u32[]{:S(2)}) %all-to-all-start.1) | async-done | bytes 2097184 | tf_op jit(solution)/shard_map/all_to_all | solution.py:55
  105.2 8.2 %all-to-all-start.2 = ((bf16[128,1,32,256]{3,2,1,0:T(8,128)(2,1)}), bf16[128,1,32,256]{3,2,1,0:T(8,128)(2,1)}, u32[]{:S(2)}, u32[]{:S(2)}) async-start(bf16[128,1,32,256]{3,2,1,0:T(8,128)(2,1)} %get-tuple-element.12), calls=%async_computation.2 | async-start | bytes 4194304 | tf_op jit(solution)/shard_map/all_to_all | solution.py:56
  113.7 2.0 gather_fusion
  120.9 26.9 %all-gather.2.cloned.1.call-done = bf16[512,1024]{1,0:T(8,128)(2,1)} async-done(((bf16[512,256]{1,0:T(8,128)(2,1)}), bf16[512,1024]{1,0:T(8,128)(2,1)}) %all-gather.2.cloned.1.call-update) | async-done | bytes 1048592 | tf_op jit(solution)/shard_map/all_gather | solution.py:32
  151.0 3.2 %multiply_convert_fusion = bf16[512,1024]{1,0:T(8,128)(2,1)S(1)} fusion(bf16[1024,1024]{1,0:T(8,128)(2,1)} %bitcast.79, bf16[512,1024]{1,0:T(8,128)(2,1)S(1)} %copy-done.6, f32[512]{0:T(512)S(1)} %add_rsqrt_fusion.1, f32[512]{0:T(512)S(1)} %broadcast_multiply_fusion.2), kind=kOutput, calls=%fused_computation.18 | convolution fusion | flops 1078460416 | bytes 4198400 | tf_op jit(solution)/shard_map/dot_general | solution.py:40
  154.9 2.5 %fusion.36 = (bf16[512,1,256]{2,1,0:T(2,128)(2,1)}, bf16[512,1,256]{2,1,0:T(2,128)(2,1)S(1)}, bf16[512,1,256]{2,1,0:T(2,128)(2,1)}, bf16[512,1,256]{2,1,0:T(2,128)(2,1)}) fusion(bf16[512,4,256]{2,1,0:T(4,128)(2,1)S(1)} %reshape.287), kind=kLoop, calls=%fused_computation.89 | loop fusion | bytes 2097152 | tf_op jit(solution)/shard_map/slice | solution.py:45
  157.5 2.0 copy.25
  163.9 2.0 gather_fusion.1
  165.9 5.7 %fusion.1 = bf16[512,4096]{1,0:T(8,128)(2,1)} fusion(f32[4,4096]{1,0:T(4,128)S(1)} %broadcast_multiply_fusion, bf16[4096,256]{1,0:T(8,128)(2,1)} %bitcast.73, bf16[512,256]{1,0:T(8,128)(2,1)S(1)} %bitcast.76), kind=kOutput, calls=%fused_computation.9 | convolution fusion | flops 551550976 | bytes 5439488 | tf_op jit(solution)/shard_map/dot_general | solution.py:72
  171.6 4.4 %fusion = bf16[512,4096]{1,0:T(8,128)(2,1)} fusion(f32[4,4096]{1,0:T(4,128)S(1)} %broadcast_multiply_fusion, bf16[4096,256]{1,0:T(8,128)(2,1)S(1)} %bitcast.74, bf16[512,256]{1,0:T(8,128)(2,1)S(1)} %bitcast.77), kind=kOutput, calls=%fused_computation.8 | convolution fusion | flops 551550976 | bytes 5439488 | tf_op jit(solution)/shard_map/dot_general | solution.py:72
  176.0 2.3 gather_fusion.2
  178.3 3.9 %fusion.38 = (f32[512]{0:T(512)S(1)}, f32[512,128]{0,1:T(8,128)S(1)}) fusion(bf16[512,256]{0,1:T(8,128)(2,1)S(1)} %bitcast.80, f32[512]{0:T(512)S(1)} %get-tuple-element.18, bf16[512,4096]{1,0:T(8,128)(2,1)} %fusion.1, bf16[4096,256]{1,0:T(8,128)(2,1)S(1)} %bitcast.71), kind=kOutput, calls=%fused_computation.91 | convolution fusion | flops 537132544 | bytes 5640192 | tf_op jit(solution)/shard_map/dot_general | solution.py:95
  182.2 2.4 fusion.37
  184.7 7.8 %psum.14 = f32[512,1]{0,1:T(1,128)S(1)} all-reduce(f32[512,1]{0,1:T(1,128)S(1)} %bitcast.87), channel_id=1, replica_groups=mesh['req'=128,'mp'=4] {'mp'}, use_global_device_ids=true, to_apply=%region_6.8 | all-reduce | flops 512 | bytes 4096 | tf_op jit(solution)/shard_map/psum | solution.py:102
  192.6 6.0 %psum.15 = f32[512,1]{0,1:T(1,128)S(1)} all-reduce(f32[512,1]{0,1:T(1,128)S(1)} %bitcast.85), channel_id=1, replica_groups=mesh['req'=128,'mp'=4] {'mp'}, use_global_device_ids=true, to_apply=%region_8.10 | all-reduce | flops 512 | bytes 4096 | tf_op jit(solution)/shard_map/psum | solution.py:105
  198.6 3.0 %convolution_bitcast_fusion = f32[1024,512]{0,1:T(8,128)} fusion(bf16[256,1024]{1,0:T(8,128)(2,1)} %param.15, f32[512,128]{0,1:T(8,128)S(1)} %get-tuple-element.17, f32[512,128]{0,1:T(8,128)S(1)} %get-tuple-element.15, bf16[512,1,256]{0,2,1:T(8,128)(2,1)} %copy.25, f32[512]{0:T(512)S(1)} %bitcast.89, f32[512]{0:T(512)S(1)} %bitcast.84), kind=kOutput, calls=%fused_computation.19 | convolution fusion | flops 269221888 | bytes 3411968 | tf_op jit(solution)/shard_map/dot_general | solution.py:111
  201.6 40.2 %reduce-scatter.2.cloned.1.call-done = f32[256,512]{0,1:T(8,128)} async-done(((f32[1024,512]{0,1:T(8,128)}), f32[256,512]{0,1:T(8,128)}) %reduce-scatter.2.cloned.1.call-update) | async-done | bytes 524304 | tf_op jit(solution)/shard_map/reduce_scatter | solution.py:110
  241.8 1.9 fusion.17
  (65 shorter events, 19.4 us)
Async XLA Ops:
  6.5 24.2 %copy-start = (bf16[32,32,256]{2,1,0:T(8,128)(2,1)S(1)}, bf16[32,32,256]{2,1,0:T(8,128)(2,1)}, u32[]{:S(2)}) copy-start(bf16[32,32,256]{2,1,0:T(8,128)(2,1)} %param.17) | copy-start | bytes 1572868
  8.3 32.7 %all-to-all-start = ((bf16[128,4,256]{2,1,0:T(4,128)(2,1)}), bf16[128,4,256]{2,1,0:T(4,128)(2,1)S(1)}, u32[]{:S(2)}, u32[]{:S(2)}) async-start(bf16[128,4,256]{2,1,0:T(4,128)(2,1)} %reshape.284), calls=%async_computation | async-start | bytes 524288 | tf_op jit(solution)/shard_map/all_to_all | solution.py:23
  30.8 1.0 copy-start.4
  41.0 10.8 %copy-start.9 = (s32[1,512]{1,0:T(1,128)S(1)}, s32[1,512]{1,0:T(1,128)}, u32[]{:S(2)}) copy-start(s32[1,512]{1,0:T(1,128)} %param.13) | copy-start | bytes 6148
  41.0 62.9 %all-to-all-start.1 = ((bf16[128,1,32,256]{3,2,1,0:T(8,128)(2,1)}), bf16[128,1,32,256]{3,2,1,0:T(8,128)(2,1)S(1)}, u32[]{:S(2)}, u32[]{:S(2)}) async-start(bf16[128,1,32,256]{3,2,1,0:T(8,128)(2,1)} %get-tuple-element.13), calls=%async_computation.1 | async-start | bytes 4194304 | tf_op jit(solution)/shard_map/all_to_all | solution.py:55
  103.9 1.3 copy-start.2
  105.2 70.8 %all-to-all-start.2 = ((bf16[128,1,32,256]{3,2,1,0:T(8,128)(2,1)}), bf16[128,1,32,256]{3,2,1,0:T(8,128)(2,1)}, u32[]{:S(2)}, u32[]{:S(2)}) async-start(bf16[128,1,32,256]{3,2,1,0:T(8,128)(2,1)} %get-tuple-element.12), calls=%async_computation.2 | async-start | bytes 4194304 | tf_op jit(solution)/shard_map/all_to_all | solution.py:56
  113.5 3.9 %copy-start.11 = (s32[128]{0:T(128)S(1)}, s32[128]{0:T(128)}, u32[]{:S(2)}) copy-start(s32[128]{0:T(128)} %param.19) | copy-start | bytes 1540
  113.5 4.6 %copy-start.10 = (s32[1,4,128]{2,1,0:T(4,128)S(1)}, s32[1,4,128]{2,1,0:T(4,128)}, u32[]{:S(2)}) copy-start(s32[1,4,128]{2,1,0:T(4,128)} %param.21) | copy-start | bytes 6148
  113.5 34.3 %all-gather.2.cloned.1.call-start = ((), (), s32[]{:S(2)}) async-start(), calls=%async_computation.4 | async-start | bytes 1310720 | tf_op jit(solution)/shard_map/all_gather | solution.py:32
  113.6 4.8 %copy-start.7 = (bf16[1024,4,256]{2,1,0:T(4,128)(2,1)S(1)}, bf16[1024,4,256]{2,1,0:T(4,128)(2,1)}, u32[]{:S(2)}) copy-start(bf16[1024,4,256]{2,1,0:T(4,128)(2,1)} %param.14) | copy-start | bytes 6291460
  116.5 125.3 %reduce-scatter.2.cloned.1.call-start = ((), (), s32[]{:S(2)}) async-start(), calls=%async_computation.5 | async-start | bytes 2621440 | tf_op jit(solution)/shard_map/reduce_scatter | solution.py:110
  147.8 3.2 %copy-start.6 = (bf16[512,1024]{1,0:T(8,128)(2,1)S(1)}, bf16[512,1024]{1,0:T(8,128)(2,1)}, u32[]{:S(2)}) copy-start(bf16[512,1024]{1,0:T(8,128)(2,1)} %all-gather.2.cloned.1.call-done) | copy-start | bytes 3145732
  157.5 6.4 %copy-start.3 = (bf16[128,1,32,256]{3,2,1,0:T(8,128)(2,1)S(1)}, bf16[128,1,32,256]{3,2,1,0:T(8,128)(2,1)}, u32[]{:S(2)}) copy-start(bf16[128,1,32,256]{3,2,1,0:T(8,128)(2,1)} %copy-done.2) | copy-start | bytes 6291460
  162.6 15.7 %copy-start.8 = (bf16[512,1,256]{0,2,1:T(8,128)(2,1)}, bf16[512,1,256]{0,2,1:T(8,128)(2,1)S(1)}, u32[]{:S(2)}) copy-start(bf16[512,1,256]{0,2,1:T(8,128)(2,1)S(1)} %copy.24) | copy-start | bytes 786436
  165.9 5.7 %copy-start.5 = (bf16[128,32,256]{2,1,0:T(8,128)(2,1)S(1)}, bf16[128,32,256]{2,1,0:T(8,128)(2,1)}, u32[]{:S(2)}) copy-start(bf16[128,32,256]{2,1,0:T(8,128)(2,1)} %gather_fusion.1) | copy-start | bytes 6291460
  178.3 3.9 %copy-start.1 = (bf16[512,4096]{1,0:T(8,128)(2,1)S(1)}, bf16[512,4096]{1,0:T(8,128)(2,1)}, u32[]{:S(2)}) copy-start(bf16[512,4096]{1,0:T(8,128)(2,1)} %fusion) | copy-start | bytes 12582916
Sparse Core Ops, SparseCore 0:
  116.6 31.1 all-gather.1
  201.7 40.0 reduce-scatter.1
where the time goes:
time: 251 us; the launch traced here: 250 us
  waiting for transfers between devices  122 us (49%)
  starting transfers between devices  37.7 us (15%)
  local copies, waits for them, and re-layouts  25.6 us (10%)
  matrix products  22.6 us (9%)
  between operations  14.4 us (6%)
  other arithmetic  14.1 us (6%)
  blocking collectives  13.8 us (5%)
    all_to_all x1, waiting for transfers between devices, local(): lax.all_to_all(send_keys, 'req', split_axis=0, concat_axis=0, tiled=True)  52.1 us
    reduce_scatter x1, waiting for transfers between devices, local(): lax.psum_scatter(lax.dot_general(w_out, hidden, (((0,), (1,)), ((), ())),...  40.2 us
    all_gather x1, waiting for transfers between devices, local(): full_rows = lax.all_gather(own_rows, 'mp', axis=1, tiled=True)  26.9 us
    all_to_all x1, starting transfers between devices, local(): lax.all_to_all(cand_feats.reshape(shards, cand_slot, columns), 'req', spl...  18.4 us
    all_to_all x1, starting transfers between devices, local(): lax.all_to_all(send_keys, 'req', split_axis=0, concat_axis=0, tiled=True)  10.8 us
    dot_general x2, matrix products, local(): lax.dot_general(q_head, hist_keys[:, lo_col:lo_col + DH], (((1,), (1,)),...  10.1 us
    unnamed x30, local copies, waits for them, and re-layouts  8.64 us
    all_to_all x1, starting transfers between devices, local(): lax.all_to_all(send_values, 'req', split_axis=0, concat_axis=0, tiled=True)  8.25 us
  transfers between devices with their start and end apart: 5, of which 4 were waited for; matrix products, arithmetic and copies ran while one was open for 18% of the time, Pallas kernels for 0%

commit v1 on v0

v1 whole, which is shorter than its diff:
```python
import functools

import jax
import jax.numpy as jnp
from jax import lax
from jax.experimental import pallas as pl
from jax.experimental.pallas import tpu as pltpu
from jax.sharding import PartitionSpec as P

HEADS = 8
DH = 128
BLK = 32
MAXBLK = 128
GROUP = 128
EPS = 1e-05
VMEM = 48 * 1024 * 1024


def cost(flops, nbytes, trans=0):
    return pl.CostEstimate(flops=flops, bytes_accessed=nbytes, transcendentals=trans)


def pack_kernel(slots, cache, *refs):
    extra, out = (refs[0], refs[1]) if len(refs) == 2 else (None, refs[0])
    per = out.shape[0]
    base = pl.program_id(0) * per
    for i in range(per):
        slot = slots[base + i]
        block = cache[slot]
        out[i, :BLK, :] = block[:, :DH]
        out[i, BLK : 2 * BLK, :] = block[:, DH:]
    if extra is not None:
        out[:, 2 * BLK :, :] = extra[...]


def pack(slots, cache, extra=None):
    shards = slots.shape[0]
    per = 16
    rows = 2 * BLK + (0 if extra is None else extra.shape[1])
    in_specs = [pl.BlockSpec(cache.shape, lambda i, s: (0, 0, 0))]
    args = [cache]
    if extra is not None:
        in_specs.append(pl.BlockSpec((per, extra.shape[1], DH), lambda i, s: (i, 0, 0)))
        args.append(extra)
    return pl.pallas_call(
        pack_kernel,
        out_shape=jax.ShapeDtypeStruct((shards, rows, DH), cache.dtype),
        grid_spec=pltpu.PrefetchScalarGridSpec(
            num_scalar_prefetch=1,
            grid=(shards // per,),
            in_specs=in_specs,
            out_specs=pl.BlockSpec((per, rows, DH), lambda i, s: (i, 0, 0)),
        ),
        compiler_params=pltpu.CompilerParams(vmem_limit_bytes=VMEM),
        cost_estimate=cost(0, 2 * shards * rows * DH * 2),
        name="pack",
    )(slots, *args)


def project_kernel(rows, w, gate, query, own):
    features = rows[...].astype(jnp.float32)
    centred = features - jnp.mean(features, axis=1, keepdims=True)
    spread = jnp.mean(centred * centred, axis=1, keepdims=True)
    normed = (centred * lax.rsqrt(spread + EPS)).astype(jnp.bfloat16)
    width = gate.shape[1]

    def part(i):
        x = jnp.dot(
            normed, w[:, i * width : (i + 1) * width], preferred_element_type=jnp.float32
        )
        half = 0.5 * x
        return (half + half * jnp.tanh(half)).astype(jnp.bfloat16)

    gate[...] = part(0)
    value = part(1).astype(jnp.float32)
    q = part(2)
    query[...] = q
    key = part(3).astype(jnp.float32)
    product = q.astype(jnp.float32) * key
    for h in range(width // DH):
        cols = slice(h * DH, (h + 1) * DH)
        half = jnp.sum(product[:, cols], axis=1, keepdims=True) * (0.5 * DH**-0.5)
        own[:, cols] = (half + half * jnp.tanh(half)) * value[:, cols]


def project(rows, w, width):
    cands, depth = rows.shape
    step = 128
    block = lambda n: pl.BlockSpec((step, n), lambda i: (i, 0))
    return pl.pallas_call(
        project_kernel,
        out_shape=(
            jax.ShapeDtypeStruct((cands, width), jnp.bfloat16),
            jax.ShapeDtypeStruct((cands, width), jnp.bfloat16),
            jax.ShapeDtypeStruct((cands, width), jnp.float32),
        ),
        grid=(cands // step,),
        in_specs=[block(depth), pl.BlockSpec(w.shape, lambda i: (0, 0))],
        out_specs=(block(width), block(width), block(width)),
        compiler_params=pltpu.CompilerParams(vmem_limit_bytes=VMEM),
        cost_estimate=cost(2 * cands * depth * 4 * width, 6 << 20, cands * 4 * width),
        name="project",
    )(rows, w)


def weights_kernel(query, keys, mask, out):
    sources = keys.shape[0]
    n = sources * BLK
    for h in range(query.shape[1] // DH):
        k = keys[:, h * BLK : (h + 1) * BLK, :].reshape(n, DH)
        for g in range(query.shape[0] // GROUP):
            rows = slice(g * GROUP, (g + 1) * GROUP)
            s = lax.dot_general(
                query[rows, h * DH : (h + 1) * DH],
                k,
                (((1,), (1,)), ((), ())),
                preferred_element_type=jnp.float32,
            )
            half = s * mask[g : g + 1, :]
            out[h, rows, :] = (half + half * jnp.tanh(half)).astype(jnp.bfloat16)


def attention_weights(query, got, mask):
    shards = got.shape[0]
    cands, width = query.shape
    heads = width // DH
    per = 16
    return pl.pallas_call(
        weights_kernel,
        out_shape=jax.ShapeDtypeStruct((heads, cands, shards * BLK), jnp.bfloat16),
        grid=(shards // per,),
        in_specs=[
            pl.BlockSpec((cands, width), lambda i: (0, 0)),
            pl.BlockSpec((per, 2 * BLK, DH), lambda i: (i, 0, 0)),
            pl.BlockSpec((mask.shape[0], per * BLK), lambda i: (0, i)),
        ],
        out_specs=pl.BlockSpec((heads, cands, per * BLK), lambda i: (0, 0, i)),
        compiler_params=pltpu.CompilerParams(vmem_limit_bytes=VMEM),
        cost_estimate=cost(
            2 * cands * shards * BLK * width, 12 << 20, heads * cands * shards * BLK
        ),
        name="weights",
    )(query, got, mask)


def values_kernel(weights, values, own, out, total):
    step = pl.program_id(0)
    n = values.shape[0] * BLK

    @pl.when(step == 0)
    def _():
        total[...] = own[...]

    for h in range(weights.shape[0]):
        v = values[:, h * BLK : (h + 1) * BLK, :].reshape(n, DH)
        total[:, h * DH : (h + 1) * DH] += jnp.dot(
            weights[h], v, preferred_element_type=jnp.float32
        )

    @pl.when(step == pl.num_programs(0) - 1)
    def _():
        done = total[...].astype(jnp.bfloat16)
        for i in range(out.shape[0]):
            out[i] = done


def weighted_values(weights, got, own, copies):
    shards = got.shape[0]
    heads, cands, _ = weights.shape
    width = own.shape[1]
    per = 16
    return pl.pallas_call(
        values_kernel,
        out_shape=jax.ShapeDtypeStruct((copies, cands, width), jnp.bfloat16),
        grid=(shards // per,),
        in_specs=[
            pl.BlockSpec((heads, cands, per * BLK), lambda i: (0, 0, i)),
            pl.BlockSpec((per, 2 * BLK, DH), lambda i: (i, 0, 0)),
            pl.BlockSpec((cands, width), lambda i: (0, 0)),
        ],
        out_specs=pl.BlockSpec((copies, cands, width), lambda i: (0, 0, 0)),
        scratch_shapes=[pltpu.VMEM((cands, width), jnp.float32)],
        compiler_params=pltpu.CompilerParams(vmem_limit_bytes=VMEM),
        cost_estimate=cost(2 * cands * shards * BLK * width, 12 << 20),
        name="values",
    )(weights, got, own)


def finish_kernel(attn, gate, w, rows, out):
    parts, _, width = attn.shape
    pieces = [attn[i].astype(jnp.float32) for i in range(parts)]
    total = parts * width
    mean = sum(jnp.sum(p, axis=1, keepdims=True) for p in pieces) / total
    centred = [p - mean for p in pieces]
    spread = sum(jnp.sum(c * c, axis=1, keepdims=True) for c in centred) / total
    scale = lax.rsqrt(spread + EPS)
    result = rows[...].astype(jnp.float32)
    for i in range(parts):
        hidden = (centred[i] * scale * gate[i].astype(jnp.float32)).astype(jnp.bfloat16)
        result += jnp.dot(
            hidden, w[i * width : (i + 1) * width, :], preferred_element_type=jnp.float32
        )
    out[...] = result.astype(out.dtype)


def finish(attn, gate, w, rows):
    parts, cands, width = attn.shape
    step = 128
    stack = pl.BlockSpec((parts, step, width), lambda i: (0, i, 0))
    flat = pl.BlockSpec((step, rows.shape[1]), lambda i: (i, 0))
    return pl.pallas_call(
        finish_kernel,
        out_shape=jax.ShapeDtypeStruct(rows.shape, jnp.bfloat16),
        grid=(cands // step,),
        in_specs=[stack, stack, pl.BlockSpec(w.shape, lambda i: (0, 0)), flat],
        out_specs=flat,
        compiler_params=pltpu.CompilerParams(vmem_limit_bytes=VMEM),
        cost_estimate=cost(2 * cands * parts * width * rows.shape[1], 3 << 20),
        name="finish",
    )(attn, gate, w, rows)


def local(
    cand_feats, cand_perm, w_in, w_out, cache_k, cache_v, hist_len, hist_home, hist_slot, hist_mask
):
    shards = lax.axis_size("req")
    split = lax.axis_size("mp")
    me = lax.axis_index("req")
    part = lax.axis_index("mp")
    columns = cand_feats.shape[1]
    cand_slot = cand_feats.shape[0] // shards
    cands = cand_perm.shape[1]
    width = w_in.shape[2]

    wanted = (me - hist_home) % shards
    places = jnp.arange(MAXBLK, dtype=jnp.int32)
    slots = jnp.sum(jnp.where(places[None, :] == wanted[:, None], hist_slot, 0), axis=1)

    halves = columns // DH
    cand_rows = (
        cand_feats.reshape(shards, cand_slot, halves, DH)
        .transpose(0, 2, 1, 3)
        .reshape(shards, cand_slot * halves, DH)
    )
    exchange = functools.partial(
        lax.all_to_all, axis_name="req", split_axis=0, concat_axis=0, tiled=True
    )
    got_keys = exchange(pack(slots, cache_k, cand_rows))
    got_values = exchange(pack(slots, cache_v))

    own_out = lax.dynamic_slice_in_dim(
        lax.all_gather(w_out, "mp", axis=0, tiled=True), part * columns, columns, axis=1
    )

    home = hist_home[me]
    order = (jnp.arange(shards, dtype=jnp.int32) - home) % shards
    seen = jnp.take(hist_mask[0], order, axis=1, mode="clip").astype(jnp.float32)
    inside = order[:, None] * BLK + jnp.arange(BLK, dtype=jnp.int32)[None, :] < hist_len[0]
    mask = seen[:, :, None] * jnp.where(inside, 0.5 * DH**-0.5, 0.0)[None]
    mask = mask.reshape(hist_mask.shape[1], shards * BLK)

    arrived = (
        got_keys[:, 2 * BLK :, :]
        .reshape(shards, halves, cand_slot, DH)
        .transpose(0, 2, 1, 3)
        .reshape(cands, columns)
    )
    own_rows = jnp.take(arrived, cand_perm[0], axis=0, mode="clip")
    full_rows = lax.all_gather(own_rows, "mp", axis=1, tiled=True)
    gate, query, own = project(full_rows, w_in.reshape(w_in.shape[0], 4 * width), width)
    gates = lax.all_gather(gate, "mp", axis=0, tiled=False)

    weights = attention_weights(query, got_keys, mask)
    attn = weighted_values(weights, got_values, own, split)
    attn = lax.all_to_all(attn, "mp", split_axis=0, concat_axis=0, tiled=True)
    return finish(attn, gates, own_out, own_rows)


def solution(mesh):
    in_specs = (
        P("req", "mp"),
        P("req", None),
        P(None, None, "mp"),
        P("mp", None),
        P("req", None, "mp"),
        P("req", None, "mp"),
        P("req"),
        P(),
        P(),
        P("req", None, None),
    )
    out_specs = P("req", "mp")
    return jax.shard_map(local, mesh=mesh, in_specs=in_specs, out_specs=out_specs, check_vma=False)
```

time: 251 us -> 203 us (0.81)
  Pallas kernels: 0 us -> 23.7 us
  matrix products: 22.6 us -> 0 us
  blocking collectives: 13.8 us -> 0 us
  other arithmetic: 14.1 us -> 2.98 us
  waiting for transfers between devices: 122 us -> 112 us
  local copies, waits for them, and re-layouts: 25.6 us -> 18.3 us
  starting transfers between devices: 37.7 us -> 31.5 us
    all_to_all x3, waiting for transfers between devices: 55.2 us -> 97 us  [the longest x1 57.5 us: local(): got_keys = exchange(pack(slots, cache_k, cand_rows))]
    reduce_scatter x1 -> x0, waiting for transfers between devices: 40.2 us -> none  [local(): lax.psum_scatter(lax.dot_general(w_out, hidden, (((0,), (1,)), ((), ())),...]
    pallas_call x0 -> x6, Pallas kernels: none -> 23.7 us  [the longest x1 8.76 us: weighted_values(): pl.pallas_call(values_kernel, out_shape=jax.ShapeDtypeStruct((copies, can...]
    dot_general x6 -> x0, matrix products: 22.6 us -> none  [the longest x2 10.1 us: local(): lax.dot_general(q_head, hist_keys[:, lo_col:lo_col + DH], (((1,), (1,)),...]
    all_gather x1, waiting for transfers between devices: 26.9 us -> 6.41 us  [local(): full_rows = lax.all_gather(own_rows, 'mp', axis=1, tiled=True)]
    psum x2 -> x0, blocking collectives: 13.8 us -> none  [the longest x1 7.79 us: local(): row_total = lax.psum(jnp.sum(attn, axis=1, keepdims=True), 'mp')]
    gather x6 -> x2, local copies, waits for them, and re-layouts: 10.9 us -> 3.23 us  [the longest x1 2.58 us: local(): own_rows = jnp.take(arrived, cand_perm[0], axis=0, mode='clip')]
    all_gather x0 -> x2, waiting for transfers between devices: none -> 7.34 us  [the longest x1 7.34 us: local(): gates = lax.all_gather(gate, 'mp', axis=0, tiled=False)]
  transfers between devices with their start and end apart: 5 -> 6, of which waited for: 4 -> 5; matrix products, arithmetic and copies ran while one was open for 18% -> 4% of each run, Pallas kernels for 0% -> 10%
where the time goes in v1:
time: 203 us; the launch traced here: 202 us
  waiting for transfers between devices  112 us (55%)
  starting transfers between devices  31.5 us (16%)
  Pallas kernels  23.7 us (12%)
  local copies, waits for them, and re-layouts  18.3 us (9%)
  between operations  14 us (7%)
  other arithmetic  2.98 us (1%)
    all_to_all x1, waiting for transfers between devices, local(): got_keys = exchange(pack(slots, cache_k, cand_rows))  57.5 us
    all_to_all x1, waiting for transfers between devices, local(): got_values = exchange(pack(slots, cache_v))  24 us
    all_to_all x1, starting transfers between devices, local(): got_keys = exchange(pack(slots, cache_k, cand_rows))  18.6 us
    all_to_all x1, waiting for transfers between devices, local(): attn = lax.all_to_all(attn, 'mp', split_axis=0, concat_axis=0, tiled=True)  15.6 us
    unnamed x25, local copies, waits for them, and re-layouts  11.4 us
    pallas_call x1, Pallas kernels, weighted_values(): pl.pallas_call(values_kernel, out_shape=jax.ShapeDtypeStruct((copies, can...  8.76 us
    all_to_all x1, starting transfers between devices, local(): got_values = exchange(pack(slots, cache_v))  8.67 us
    all_gather x1, waiting for transfers between devices, local(): gates = lax.all_gather(gate, 'mp', axis=0, tiled=False)  7.34 us
  transfers between devices with their start and end apart: 6, of which 5 were waited for; matrix products, arithmetic and copies ran while one was open for 4% of the time, Pallas kernels for 10%

profile of v1, /device:TPU:1, one launch (start us, length us, event | category | flops | bytes accessed | tf_op | source)
XLA Modules:
  0.0 201.9 jit_solution(10346140210508508138)
XLA Ops:
  6.5 1.0 reshape.88
  8.3 1.0 select_reduce_fusion.slots
  9.3 1.0 copy-done.5
  10.4 1.0 pack.2
  11.4 1.4 copy-done
  12.8 18.6 %all-to-all-start = ((bf16[128,72,128]{2,1,0:T(8,128)(2,1)}), bf16[128,72,128]{2,1,0:T(8,128)(2,1)S(1)}, u32[]{:S(2)}, u32[]{:S(2)}) async-start(bf16[128,72,128]{2,1,0:T(8,128)(2,1)} %copy-done), calls=%async_computation | async-start | bytes 4718592 | tf_op jit(solution)/shard_map/all_to_all | solution.py:248
  31.5 57.5 %all-to-all-done.keys = bf16[128,72,128]{2,1,0:T(8,128)(2,1)S(1)} async-done(((bf16[128,72,128]{2,1,0:T(8,128)(2,1)}), bf16[128,72,128]{2,1,0:T(8,128)(2,1)S(1)}, u32[]{:S(2)}, u32[]{:S(2)}) %all-to-all-start) | async-done | bytes 2359328 | tf_op jit(solution)/shard_map/all_to_all | solution.py:248
  89.2 2.6 %gather_fusion = bf16[512,256]{1,0:T(8,128)(2,1)} fusion(bf16[512,256]{1,0:T(8,128)(2,1)S(1)} %bitcast.28, s32[1024]{0:T(1024)S(1)} %pad_clamp_fusion.1), kind=kCustom, calls=%fused_computation | custom fusion | bytes 526336 | tf_op jit(solution)/shard_map/jit(_take)/gather | solution.py:268
  92.8 1.3 copy-done.1
  94.1 8.7 %all-to-all-start.1 = ((bf16[128,64,128]{2,1,0:T(8,128)(2,1)}), bf16[128,64,128]{2,1,0:T(8,128)(2,1)}, u32[]{:S(2)}, u32[]{:S(2)}) async-start(bf16[128,64,128]{2,1,0:T(8,128)(2,1)} %copy-done.1), calls=%async_computation.1 | async-start | bytes 4194304 | tf_op jit(solution)/shard_map/all_to_all | solution.py:249
  107.6 3.4 %copy.20 = bf16[128,8,4,256]{3,1,2,0:T(8,128)(2,1)} copy(bf16[128,8,4,256]{3,2,1,0:T(4,128)(2,1)} %bitcast.29) | data formatting | bytes 4194304
  111.0 6.4 %all-gather.8.cloned.1.call-done.rows = bf16[512,1024]{1,0:T(8,128)(2,1)} async-done(((bf16[512,256]{1,0:T(8,128)(2,1)}), bf16[512,1024]{1,0:T(8,128)(2,1)}) %all-gather.8.cloned.1.call-update) | async-done | bytes 1048592 | tf_op jit(solution)/shard_map/all_gather | solution.py:269
  117.4 1.6 copy-done.3
  119.0 1.2 copy-done.7
  120.3 3.5 %project.1 = (bf16[512,256]{1,0:T(8,128)(2,1)}, bf16[512,256]{1,0:T(8,128)(2,1)S(1)}, f32[512,256]{1,0:T(8,128)S(1)}) custom-call(bf16[512,1024]{1,0:T(8,128)(2,1)S(1)} %copy-done.7, bf16[1024,1024]{1,0:T(8,128)(2,1)S(1)} %bitcast.25), custom_call_target="tpu_custom_call" | custom-call | flops 1073741824 | bytes 6291456 | tf_op jit(solution)/shard_map/project/pallas_call | solution.py:90
  123.8 6.8 %weights.1 = bf16[2,512,4096]{2,1,0:T(8,128)(2,1)} custom-call(bf16[512,256]{1,0:T(8,128)(2,1)S(1)} %get-tuple-element.8.query, bf16[128,72,128]{2,1,0:T(8,128)(2,1)S(1)} %all-to-all-done.keys, f32[4,4096]{1,0:T(4,128)S(1)} %broadcast_multiply_fusion.mask), custom_call_target="tpu_custom_call" | custom-call | flops 1073741824 | bytes 12582912 | tf_op jit(solution)/shard_map/weights/pallas_call | solution.py:128
  130.6 24.0 %all-to-all-done.1.values = bf16[128,64,128]{2,1,0:T(8,128)(2,1)} async-done(((bf16[128,64,128]{2,1,0:T(8,128)(2,1)}), bf16[128,64,128]{2,1,0:T(8,128)(2,1)}, u32[]{:S(2)}, u32[]{:S(2)}) %all-to-all-start.1) | async-done | bytes 2097184 | tf_op jit(solution)/shard_map/all_to_all | solution.py:249
  154.6 8.8 %values.1 = bf16[4,512,256]{2,1,0:T(8,128)(2,1)} custom-call(bf16[2,512,4096]{2,1,0:T(8,128)(2,1)} %weights.1, bf16[128,64,128]{2,1,0:T(8,128)(2,1)} %all-to-all-done.1.values, f32[512,256]{1,0:T(8,128)S(1)} %get-tuple-element.9.own), custom_call_target="tpu_custom_call" | custom-call | flops 1073741824 | bytes 12582912 | tf_op jit(solution)/shard_map/values/pallas_call | solution.py:172
  163.4 4.1 %all-to-all-start.2 = ((bf16[4,512,256]{2,1,0:T(8,128)(2,1)}), bf16[4,512,256]{2,1,0:T(8,128)(2,1)S(1)}, u32[]{:S(2)}, u32[]{:S(2)}) async-start(bf16[4,512,256]{2,1,0:T(8,128)(2,1)} %values.1), calls=%async_computation.2 | async-start | bytes 2097152 | tf_op jit(solution)/shard_map/all_to_all | solution.py:275
  167.5 1.1 constant_dynamic-slice_fusion.w
  168.6 15.6 %all-to-all-done.2.attn = bf16[4,512,256]{2,1,0:T(8,128)(2,1)S(1)} async-done(((bf16[4,512,256]{2,1,0:T(8,128)(2,1)}), bf16[4,512,256]{2,1,0:T(8,128)(2,1)S(1)}, u32[]{:S(2)}, u32[]{:S(2)}) %all-to-all-start.2) | async-done | bytes 1048608 | tf_op jit(solution)/shard_map/all_to_all | solution.py:275
  184.2 7.3 %all-gather.10.cloned.1.call-done = bf16[2048,256]{1,0:T(8,128)(2,1)} async-done(((bf16[512,256]{1,0:T(8,128)(2,1)}), bf16[2048,256]{1,0:T(8,128)(2,1)}) %all-gather.10.cloned.1.call-update) | async-done | bytes 1048592 | tf_op jit(solution)/shard_map/all_gather | solution.py:271
  191.5 1.2 copy-done.4
  192.7 2.6 %finish.1 = bf16[512,256]{1,0:T(8,128)(2,1)} custom-call(bf16[4,512,256]{2,1,0:T(8,128)(2,1)S(1)} %all-to-all-done.2.attn, bf16[4,512,256]{2,1,0:T(8,128)(2,1)S(1)} %bitcast.26, bf16[1024,256]{1,0:T(8,128)(2,1)S(1)} %constant_dynamic-slice_fusion.w, bf16[512,256]{1,0:T(8,128)(2,1)S(1)} %copy-done.2), custom_call_target="tpu_custom_call" | custom-call | flops 268435456 | bytes 3145728 | tf_op jit(solution)/shard_map/finish/pallas_call | solution.py:211
  (46 shorter events, 6.2 us)
Async XLA Ops:
  9.3 1.1 copy-start.5
  11.4 1.4 copy-start
  12.8 18.6 %copy-start.8 = (s32[1,512]{1,0:T(1,128)S(1)}, s32[1,512]{1,0:T(1,128)}, u32[]{:S(2)}) copy-start(s32[1,512]{1,0:T(1,128)} %param.11) | copy-start | bytes 6148
  12.8 76.1 %all-to-all-start = ((bf16[128,72,128]{2,1,0:T(8,128)(2,1)}), bf16[128,72,128]{2,1,0:T(8,128)(2,1)S(1)}, u32[]{:S(2)}, u32[]{:S(2)}) async-start(bf16[128,72,128]{2,1,0:T(8,128)(2,1)} %copy-done), calls=%async_computation | async-start | bytes 4718592 | tf_op jit(solution)/shard_map/all_to_all | solution.py:248
  31.4 86.0 %all-gather.8.cloned.1.call-start = ((), (), s32[]{:S(2)}) async-start(), calls=%async_computation.4 | async-start | bytes 1310720 | tf_op jit(solution)/shard_map/all_gather | solution.py:269
  31.5 60.4 %copy-start.6 = (bf16[32,32,256]{2,1,0:T(8,128)(2,1)S(1)}, bf16[32,32,256]{2,1,0:T(8,128)(2,1)}, u32[]{:S(2)}) copy-start(bf16[32,32,256]{2,1,0:T(8,128)(2,1)} %cache.3) | copy-start | bytes 1572868
  92.8 1.3 copy-start.1
  94.1 9.5 %copy-start.10 = (s32[128]{0:T(128)S(1)}, s32[128]{0:T(128)}, u32[]{:S(2)}) copy-start(s32[128]{0:T(128)} %param.17) | copy-start | bytes 1540
  94.1 10.1 %copy-start.9 = (s32[1,4,128]{2,1,0:T(4,128)S(1)}, s32[1,4,128]{2,1,0:T(4,128)}, u32[]{:S(2)}) copy-start(s32[1,4,128]{2,1,0:T(4,128)} %param.19) | copy-start | bytes 6148
  94.1 60.5 %all-to-all-start.1 = ((bf16[128,64,128]{2,1,0:T(8,128)(2,1)}), bf16[128,64,128]{2,1,0:T(8,128)(2,1)}, u32[]{:S(2)}, u32[]{:S(2)}) async-start(bf16[128,64,128]{2,1,0:T(8,128)(2,1)} %copy-done.1), calls=%async_computation.1 | async-start | bytes 4194304 | tf_op jit(solution)/shard_map/all_to_all | solution.py:249
  102.8 64.7 %all-gather.6.cloned.1.call-start = ((), (), s32[]{:S(2)}) async-start(), calls=%async_computation.3 | async-start | bytes 2621440 | tf_op jit(solution)/shard_map/all_gather | solution.py:252
  103.6 87.9 %all-gather.10.cloned.1.call-start = ((), (), s32[]{:S(2)}) async-start(), calls=%async_computation.5 | async-start | bytes 1310720 | tf_op jit(solution)/shard_map/all_gather | solution.py:271
  117.4 1.6 copy-start.3
  119.0 1.2 copy-start.7
  163.4 28.1 %copy-start.2 = (bf16[512,256]{1,0:T(8,128)(2,1)S(1)}, bf16[512,256]{1,0:T(8,128)(2,1)}, u32[]{:S(2)}) copy-start(bf16[512,256]{1,0:T(8,128)(2,1)} %gather_fusion) | copy-start | bytes 786436
  163.4 20.8 %all-to-all-start.2 = ((bf16[4,512,256]{2,1,0:T(8,128)(2,1)}), bf16[4,512,256]{2,1,0:T(8,128)(2,1)S(1)}, u32[]{:S(2)}, u32[]{:S(2)}) async-start(bf16[4,512,256]{2,1,0:T(8,128)(2,1)} %values.1), calls=%async_computation.2 | async-start | bytes 2097152 | tf_op jit(solution)/shard_map/all_to_all | solution.py:275
  191.5 1.2 copy-start.4
Sparse Core Ops, SparseCore 0:
  91.9 25.4 all-gather.7
  119.5 38.0 all-gather.5
  159.7 31.7 all-gather.9

commit v2 on v1

v2 whole, which is shorter than its diff:
```python
import functools

import jax
import jax.numpy as jnp
from jax import lax
from jax.experimental import pallas as pl
from jax.experimental.pallas import tpu as pltpu
from jax.sharding import PartitionSpec as P

HEADS = 8
DH = 128
BLK = 32
MAXBLK = 128
GROUP = 128
EPS = 1e-05
VMEM = 28 * 1024 * 1024
WHOLE = pl.BlockSpec(memory_space=pltpu.VMEM)
IN_HBM = pl.BlockSpec(memory_space=pltpu.HBM)


def hbm(x):
    return pltpu.with_memory_space_constraint(x, pltpu.HBM)


def cost(flops, nbytes, trans=0):
    return pl.CostEstimate(flops=flops, bytes_accessed=nbytes, transcendentals=trans)


def pack_kernel(slots, cache, *refs):
    out, held, made, load_sem, store_sem = refs[-5:]
    load = pltpu.make_async_copy(cache, held, load_sem)
    load.start()
    load.wait()
    shards, rows, _ = made.shape
    per = shards // store_sem.shape[0]
    stores = []
    for c in range(store_sem.shape[0]):
        chunk = pl.ds(c * per, per)
        for r in range(c * per, (c + 1) * per):
            block = held[slots[r]]
            made[r, :BLK, :] = block[:, :DH]
            made[r, BLK : 2 * BLK, :] = block[:, DH:]
        if rows > 2 * BLK:
            made[chunk, 2 * BLK :, :] = refs[0][chunk]
        stores.append(pltpu.make_async_copy(made.at[chunk], out.at[chunk], store_sem.at[c]))
        stores[-1].start()
    for store in stores:
        store.wait()


def pack(slots, cache, extra=None, after=()):
    shards = slots.shape[0]
    rows = 2 * BLK + (0 if extra is None else extra.shape[1])
    in_specs, args = [IN_HBM], [hbm(cache)]
    if extra is not None:
        in_specs.append(WHOLE)
        args.append(extra)
    in_specs += [pl.BlockSpec(memory_space=pl.ANY)] * len(after)
    out_shape = (shards, rows, DH)
    return pl.pallas_call(
        pack_kernel,
        out_shape=pltpu.HBM(out_shape, cache.dtype),
        in_specs=[pl.BlockSpec(memory_space=pltpu.SMEM)] + in_specs,
        out_specs=IN_HBM,
        scratch_shapes=[
            pltpu.VMEM(cache.shape, cache.dtype),
            pltpu.VMEM(out_shape, cache.dtype),
            pltpu.SemaphoreType.DMA,
            pltpu.SemaphoreType.DMA((4,)),
        ],
        compiler_params=pltpu.CompilerParams(vmem_limit_bytes=VMEM),
        cost_estimate=cost(0, 2 * shards * rows * DH * 2),
        name="pack",
    )(slots, *args, *after)


def silu(half):
    return half + half * jnp.tanh(half)


def project_kernel(part, r0, r1, r2, r3, w, g1, g2, g3, gates, query, own, normed):
    pieces = [r[...].astype(jnp.float32) for r in (r0, r1, r2, r3)]
    split = len(pieces)
    width = r0.shape[1]
    total = split * width
    mean = sum(jnp.sum(p, axis=1, keepdims=True) for p in pieces) / total
    centred = [p - mean for p in pieces]
    spread = sum(jnp.sum(c * c, axis=1, keepdims=True) for c in centred) / total
    scale = lax.rsqrt(spread + EPS)
    for d in range(split):
        at = pl.multiple_of(lax.rem(part[0] + (split - d), split) * width, width)
        normed[:, pl.ds(at, width)] = (centred[d] * scale).astype(jnp.bfloat16)
    x = normed[...]

    def times(matrix):
        return silu(0.5 * jnp.dot(x, matrix, preferred_element_type=jnp.float32)).astype(
            jnp.bfloat16
        )

    gates[0] = times(w[:, :width])
    for d, g in ((1, g1), (2, g2), (3, g3)):
        gates[d] = times(g[...])
    value = times(w[:, width : 2 * width]).astype(jnp.float32)
    q = times(w[:, 2 * width : 3 * width])
    query[...] = q
    key = times(w[:, 3 * width :]).astype(jnp.float32)
    product = q.astype(jnp.float32) * key
    for h in range(width // DH):
        cols = slice(h * DH, (h + 1) * DH)
        half = jnp.sum(product[:, cols], axis=1, keepdims=True) * (0.5 * DH**-0.5)
        own[:, cols] = silu(half) * value[:, cols]


def project(part, rows, w, gate_w):
    cands, width = rows[0].shape
    split = len(rows)
    depth = split * width
    step = 128
    block = pl.BlockSpec((step, width), lambda i, s: (i, 0))
    whole = lambda a: pl.BlockSpec(a.shape, lambda i, s: (0, 0))
    return pl.pallas_call(
        project_kernel,
        out_shape=(
            jax.ShapeDtypeStruct((split, cands, width), jnp.bfloat16),
            jax.ShapeDtypeStruct((cands, width), jnp.bfloat16),
            jax.ShapeDtypeStruct((cands, width), jnp.float32),
        ),
        grid_spec=pltpu.PrefetchScalarGridSpec(
            num_scalar_prefetch=1,
            grid=(cands // step,),
            in_specs=[block] * split + [whole(w)] + [whole(g) for g in gate_w],
            out_specs=(
                pl.BlockSpec((split, step, width), lambda i, s: (0, i, 0)),
                block,
                block,
            ),
            scratch_shapes=[pltpu.VMEM((step, depth), jnp.bfloat16)],
        ),
        compiler_params=pltpu.CompilerParams(vmem_limit_bytes=VMEM),
        cost_estimate=cost(2 * cands * depth * 7 * width, 8 << 20, cands * 7 * width),
        name="project",
    )(part, *rows, w, *gate_w)


def weights_kernel(query, keys, mask, out):
    sources = keys.shape[0]
    n = sources * BLK
    for h in range(query.shape[1] // DH):
        k = keys[:, h * BLK : (h + 1) * BLK, :].reshape(n, DH)
        for g in range(query.shape[0] // GROUP):
            rows = slice(g * GROUP, (g + 1) * GROUP)
            s = lax.dot_general(
                query[rows, h * DH : (h + 1) * DH],
                k,
                (((1,), (1,)), ((), ())),
                preferred_element_type=jnp.float32,
            )
            out[0, h, rows, :] = silu(s * mask[g : g + 1, :]).astype(jnp.bfloat16)


def attention_weights(query, got, mask):
    shards = got.shape[0]
    cands, width = query.shape
    heads = width // DH
    per = 16
    return pl.pallas_call(
        weights_kernel,
        out_shape=pltpu.HBM((shards // per, heads, cands, per * BLK), jnp.bfloat16),
        grid=(shards // per,),
        in_specs=[
            pl.BlockSpec((cands, width), lambda i: (0, 0)),
            pl.BlockSpec((per, 2 * BLK, DH), lambda i: (i, 0, 0)),
            pl.BlockSpec((mask.shape[0], per * BLK), lambda i: (0, i)),
        ],
        out_specs=pl.BlockSpec((1, heads, cands, per * BLK), lambda i: (i, 0, 0, 0)),
        compiler_params=pltpu.CompilerParams(vmem_limit_bytes=VMEM),
        cost_estimate=cost(
            2 * cands * shards * BLK * width, 12 << 20, heads * cands * shards * BLK
        ),
        name="weights",
    )(query, got, mask)


def values_kernel(weights, values, own, out, w, v, held, total, w_sem, v_sem, own_sem):
    steps, heads, cands, n = weights.shape
    per = n // BLK
    copies = out.shape[0]
    loads = []
    for c in range(steps):
        chunk = pl.ds(c * per, per)
        loads.append(
            [pltpu.make_async_copy(values.at[chunk], v.at[chunk], v_sem.at[c])]
            + [
                pltpu.make_async_copy(weights.at[c, h], w.at[c, h], w_sem.at[c, h])
                for h in range(heads)
            ]
        )
        for load in loads[-1]:
            load.start()
    last = pltpu.make_async_copy(own, held, own_sem)
    last.start()
    for c in range(steps):
        for load in loads[c]:
            load.wait()
        if c == steps - 1:
            last.wait()
        for h in range(heads):
            cols = slice(h * DH, (h + 1) * DH)
            part = jnp.dot(
                w[c, h],
                v[c * per : (c + 1) * per, h * BLK : (h + 1) * BLK, :].reshape(n, DH),
                preferred_element_type=jnp.float32,
            )
            if c == 0:
                total[:, cols] = part
            elif c < steps - 1:
                total[:, cols] += part
            else:
                done = (total[:, cols] + part + held[:, cols]).astype(jnp.bfloat16)
                for i in range(copies):
                    out[i, :, cols] = done


def weighted_values(weights, got, own, copies):
    shards = got.shape[0]
    steps, heads, cands, _ = weights.shape
    width = own.shape[1]
    return pl.pallas_call(
        values_kernel,
        out_shape=jax.ShapeDtypeStruct((copies, cands, width), jnp.bfloat16),
        in_specs=[IN_HBM, IN_HBM, IN_HBM],
        out_specs=WHOLE,
        scratch_shapes=[
            pltpu.VMEM(weights.shape, weights.dtype),
            pltpu.VMEM(got.shape, got.dtype),
            pltpu.VMEM(own.shape, own.dtype),
            pltpu.VMEM((cands, width), jnp.float32),
            pltpu.SemaphoreType.DMA((steps, heads)),
            pltpu.SemaphoreType.DMA((steps,)),
            pltpu.SemaphoreType.DMA,
        ],
        compiler_params=pltpu.CompilerParams(vmem_limit_bytes=VMEM),
        cost_estimate=cost(2 * cands * shards * BLK * width, 12 << 20),
        name="values",
    )(hbm(weights), hbm(got), hbm(own))


def finish_kernel(part, attn, gates, w0, w1, w2, w3, rows, out):
    split, _, width = attn.shape
    step = out.shape[0]
    here = pl.ds(pl.multiple_of(pl.program_id(0) * step, step), step)
    pieces = [
        attn[lax.rem(part[0] + (split - d), split), here, :].astype(jnp.float32)
        for d in range(split)
    ]
    total = split * width
    mean = jnp.sum(sum(pieces), axis=1, keepdims=True) / total
    centred = [p - mean for p in pieces]
    spread = jnp.sum(sum(c * c for c in centred), axis=1, keepdims=True) / total
    scale = lax.rsqrt(spread + EPS)
    result = rows[here, :].astype(jnp.float32)
    for d, w in enumerate((w0, w1, w2, w3)):
        hidden = (centred[d] * scale * gates[d, here, :].astype(jnp.float32)).astype(jnp.bfloat16)
        result += jnp.dot(hidden, w[...], preferred_element_type=jnp.float32)
    out[...] = result.astype(out.dtype)


def finish(part, attn, gates, ws, rows):
    split, cands, width = attn.shape
    step = 128
    return pl.pallas_call(
        finish_kernel,
        out_shape=jax.ShapeDtypeStruct(rows.shape, jnp.bfloat16),
        grid_spec=pltpu.PrefetchScalarGridSpec(
            num_scalar_prefetch=1,
            grid=(cands // step,),
            in_specs=[WHOLE] * (3 + len(ws)),
            out_specs=pl.BlockSpec((step, rows.shape[1]), lambda i, s: (i, 0)),
        ),
        compiler_params=pltpu.CompilerParams(vmem_limit_bytes=VMEM),
        cost_estimate=cost(2 * cands * split * width * rows.shape[1], 3 << 20),
        name="finish",
    )(part, attn, gates, *ws, rows)


def local(
    cand_feats, cand_perm, w_in, w_out, cache_k, cache_v, hist_len, hist_home, hist_slot, hist_mask
):
    shards = lax.axis_size("req")
    split = lax.axis_size("mp")
    me = lax.axis_index("req")
    part = lax.axis_index("mp")
    parts = part.astype(jnp.int32).reshape(1)
    columns = cand_feats.shape[1]
    cand_slot = cand_feats.shape[0] // shards
    cands = cand_perm.shape[1]
    width = w_in.shape[2]

    def back(x, d):
        return lax.ppermute(x, "mp", [(i, (i + d) % split) for i in range(split)])

    behind = me - hist_home
    wanted = jnp.where(behind < 0, behind + shards, behind)
    places = jnp.arange(MAXBLK, dtype=jnp.int32)
    slots = jnp.sum(jnp.where(places[None, :] == wanted[:, None], hist_slot, 0), axis=1)

    halves = columns // DH
    cand_rows = (
        cand_feats.reshape(shards, cand_slot, halves, DH)
        .transpose(0, 2, 1, 3)
        .reshape(shards, cand_slot * halves, DH)
    )
    exchange = functools.partial(
        lax.all_to_all, axis_name="req", split_axis=0, concat_axis=0, tiled=True
    )
    got_keys = exchange(pack(slots, cache_k, extra=cand_rows))

    w_gate = w_in[:, 0, :]
    gate_w = [back(w_gate, d) for d in range(1, split)]
    own_out = []
    for d in range(split):
        piece = lax.dynamic_slice_in_dim(w_out, (part + d) % split * columns, columns, axis=1)
        own_out.append(back(piece, d) if d else piece)

    home = hist_home[me]
    order = (jnp.arange(shards, dtype=jnp.int32) - home) % shards
    seen = jnp.take(hist_mask[0], order, axis=1, mode="clip").astype(jnp.float32)
    inside = order[:, None] * BLK + jnp.arange(BLK, dtype=jnp.int32)[None, :] < hist_len[0]
    mask = seen[:, :, None] * jnp.where(inside, 0.5 * DH**-0.5, 0.0)[None]
    mask = mask.reshape(hist_mask.shape[1], shards * BLK)

    w_flat = w_in.reshape(w_in.shape[0], 4 * width)
    ready = [*gate_w, *own_out, mask, w_flat]
    got_values = exchange(pack(slots, cache_v, after=ready))

    arrived = (
        got_keys[:, 2 * BLK :, :]
        .reshape(shards, halves, cand_slot, DH)
        .transpose(0, 2, 1, 3)
        .reshape(cands, columns)
    )
    own_rows = jnp.take(arrived, cand_perm[0], axis=0, mode="clip")
    rows = [own_rows] + [back(own_rows, d) for d in range(1, split)]
    gates, query, own = project(parts, rows, w_flat, gate_w)

    weights = attention_weights(query, got_keys, mask)
    attn = weighted_values(weights, got_values, own, split)
    attn = lax.all_to_all(attn, "mp", split_axis=0, concat_axis=0, tiled=True)
    return finish(parts, attn, gates, own_out, own_rows)


def solution(mesh):
    in_specs = (
        P("req", "mp"),
        P("req", None),
        P(None, None, "mp"),
        P("mp", None),
        P("req", None, "mp"),
        P("req", None, "mp"),
        P("req"),
        P(),
        P(),
        P("req", None, None),
    )
    out_specs = P("req", "mp")
    return jax.shard_map(local, mesh=mesh, in_specs=in_specs, out_specs=out_specs, check_vma=False)
```

time: 203 us -> 171 us (0.84)
  waiting for transfers between devices: 112 us -> 32.4 us
  starting transfers between devices: 31.5 us -> 54.8 us
  blocking collectives: 0 us -> 18.1 us
  between operations: 14 us -> 1.06 us
  local copies, waits for them, and re-layouts: 18.3 us -> 29.9 us
  Pallas kernels: 23.7 us -> 27.7 us
  other arithmetic: 2.98 us -> 5.86 us
    all_to_all x3 -> x2, waiting for transfers between devices: 97 us -> 19.4 us  [the longest x1 10.4 us: local(): got_values = exchange(pack(slots, cache_v, after=ready))]
    ppermute x0 -> x9, starting transfers between devices: none -> 27.9 us  [back(): return lax.ppermute(x, 'mp', [(i, (i + d) % split) for i in range(split)])]
    all_to_all x0 -> x1, blocking collectives: none -> 18.1 us  [local(): attn = lax.all_to_all(attn, 'mp', split_axis=0, concat_axis=0, tiled=True)]
    all_gather x3 -> x0, waiting for transfers between devices: 13.7 us -> none  [the longest x1 7.34 us: local(): gates = lax.all_gather(gate, 'mp', axis=0, tiled=False)]
    ppermute x0 -> x9, waiting for transfers between devices: none -> 13 us  [back(): return lax.ppermute(x, 'mp', [(i, (i + d) % split) for i in range(split)])]
    pallas_call x4, Pallas kernels: 12.3 us -> 18.2 us  [the longest x1 6.63 us: attention_weights(): pl.pallas_call(weights_kernel, out_shape=pltpu.HBM((shards // per, heads,...]
    all_to_all x3 -> x2, starting transfers between devices: 31.4 us -> 27 us  [the longest x1 18.4 us: local(): got_keys = exchange(pack(slots, cache_k, extra=cand_rows))]
    add x4, local copies, waits for them, and re-layouts: 0.24 us -> 4.4 us  [local(): order[:, None] * BLK + jnp.arange(BLK, dtype=jnp.int32)[None, :]]
  transfers between devices with their start and end apart: 6 -> 11, of which waited for: 5 -> 5; matrix products, arithmetic and copies ran while one was open for 4% -> 15% of each run, Pallas kernels for 10% -> 9%
where the time goes in v2:
time: 171 us; the launch traced here: 170 us
  starting transfers between devices  54.8 us (32%)
  waiting for transfers between devices  32.4 us (19%)
  local copies, waits for them, and re-layouts  29.9 us (17%)
  Pallas kernels  27.7 us (16%)
  blocking collectives  18.1 us (11%)
  other arithmetic  5.86 us (3%)
    ppermute x9, starting transfers between devices, back(): return lax.ppermute(x, 'mp', [(i, (i + d) % split) for i in range(split)])  27.9 us
    all_to_all x1, starting transfers between devices, local(): got_keys = exchange(pack(slots, cache_k, extra=cand_rows))  18.4 us
    all_to_all x1, blocking collectives, local(): attn = lax.all_to_all(attn, 'mp', split_axis=0, concat_axis=0, tiled=True)  18.1 us
    ppermute x9, waiting for transfers between devices, back(): return lax.ppermute(x, 'mp', [(i, (i + d) % split) for i in range(split)])  13 us
    unnamed x38, local copies, waits for them, and re-layouts  12 us
    all_to_all x1, waiting for transfers between devices, local(): got_values = exchange(pack(slots, cache_v, after=ready))  10.4 us
    all_to_all x1, waiting for transfers between devices, local(): got_keys = exchange(pack(slots, cache_k, extra=cand_rows))  9.03 us
    all_to_all x1, starting transfers between devices, local(): got_values = exchange(pack(slots, cache_v, after=ready))  8.54 us
  transfers between devices with their start and end apart: 11, of which 5 were waited for; matrix products, arithmetic and copies ran while one was open for 15% of the time, Pallas kernels for 9%

profile of v2, /device:TPU:1, one launch (start us, length us, event | category | flops | bytes accessed | tf_op | source)
XLA Modules:
  0.0 169.9 jit_solution(7549310710770965838)
XLA Ops:
  2.8 3.2 %pack.2 = bf16[128,72,128]{2,1,0:T(8,128)(2,1)} custom-call(s32[128]{0:T(128)S(1)} %select_reduce_fusion.slots, bf16[32,32,256]{2,1,0:T(8,128)(2,1)} %cache.2, bf16[128,8,128]{2,1,0:T(8,128)(2,1)S(1)} %bitcast.30), custom_call_target="tpu_custom_call" | custom-call | bytes 4718592 | tf_op jit(solution)/shard_map/pack/pallas_call | solution.py:60
  5.9 18.4 %all-to-all-start = ((bf16[128,72,128]{2,1,0:T(8,128)(2,1)}), bf16[128,72,128]{2,1,0:T(8,128)(2,1)S(1)}, u32[]{:S(2)}, u32[]{:S(2)}) async-start(bf16[128,72,128]{2,1,0:T(8,128)(2,1)} %pack.2), calls=%async_computation | async-start | bytes 4718592 | tf_op jit(solution)/shard_map/all_to_all | solution.py:316
  24.4 2.3 %slice.7 = bf16[1024,1,256]{2,1,0:T(2,128)(2,1)S(1)} slice(bf16[1024,4,256]{2,1,0:T(4,128)(2,1)} %param.12), slice={[0:1024], [0:1], [0:256]} | slice | bytes 1048576 | tf_op jit(solution)/shard_map/slice | solution.py:318
  27.6 4.4 %collective-permute-start.5 = (bf16[1024,256]{1,0:T(8,128)(2,1)}, bf16[1024,256]{1,0:T(8,128)(2,1)S(1)}, u32[]{:S(2)}, u32[]{:S(2)}) collective-permute-start(bf16[1024,256]{1,0:T(8,128)(2,1)} %bitcast.25), channel_id=1, source_target_pairs={{0,3},{1,0},{2,1},{3,2},{4,7},{5,4},{6,5},{7,6},{8,11},{9,8},{10,9... | collective-permute-start | bytes 1572872 | tf_op jit(solution)/shard_map/ppermute | solution.py:300
  32.0 2.4 %collective-permute-start.4 = (bf16[1024,256]{1,0:T(8,128)(2,1)}, bf16[1024,256]{1,0:T(8,128)(2,1)S(1)}, u32[]{:S(2)}, u32[]{:S(2)}) collective-permute-start(bf16[1024,256]{1,0:T(8,128)(2,1)} %bitcast.25), channel_id=1, source_target_pairs={{0,2},{1,3},{2,0},{3,1},{4,6},{5,7},{6,4},{7,5},{8,10},{9,11},{10,... | collective-permute-start | bytes 1572872 | tf_op jit(solution)/shard_map/ppermute | solution.py:300
  34.5 2.5 %collective-permute-start.3 = (bf16[1024,256]{1,0:T(8,128)(2,1)}, bf16[1024,256]{1,0:T(8,128)(2,1)}, u32[]{:S(2)}, u32[]{:S(2)}) collective-permute-start(bf16[1024,256]{1,0:T(8,128)(2,1)} %bitcast.25), channel_id=1, source_target_pairs={{0,1},{1,2},{2,3},{3,0},{4,5},{5,6},{6,7},{7,4},{8,9},{9,10},{10,1... | collective-permute-start | bytes 1572872 | tf_op jit(solution)/shard_map/ppermute | solution.py:300
  38.9 4.0 %collective-permute-start.8 = (bf16[256,256]{1,0:T(8,128)(2,1)}, bf16[256,256]{1,0:T(8,128)(2,1)}, u32[]{:S(2)}, u32[]{:S(2)}) collective-permute-start(bf16[256,256]{1,0:T(8,128)(2,1)} %get-tuple-element.11), channel_id=1, source_target_pairs={{0,3},{1,0},{2,1},{3,2},{4,7},{5,4},{6,5},{7,6},{8,11},{9,8},{10,9... | collective-permute-start | bytes 393224 | tf_op jit(solution)/shard_map/ppermute | solution.py:300
  50.1 2.1 %gather_fusion.1 = s32[128,4]{1,0:T(8,128)} fusion(s32[4,128]{0,1:T(8,128)} %bitcast.35, s32[1024]{0:T(1024)S(1)} %pad_clamp_fusion), kind=kCustom, calls=%fused_computation.1 | custom fusion | bytes 4608 | tf_op jit(solution)/shard_map/jit(_take)/gather | solution.py:327
  60.1 3.1 %collective-permute-start.7 = (bf16[256,256]{1,0:T(8,128)(2,1)}, bf16[256,256]{1,0:T(8,128)(2,1)S(1)}, u32[]{:S(2)}, u32[]{:S(2)}) collective-permute-start(bf16[256,256]{1,0:T(8,128)(2,1)} %get-tuple-element.14), channel_id=1, source_target_pairs={{0,2},{1,3},{2,0},{3,1},{4,6},{5,7},{6,4},{7,5},{8,10},{9,11},{10,... | collective-permute-start | bytes 393224 | tf_op jit(solution)/shard_map/ppermute | solution.py:300
  64.1 2.1 %copy.23 = bf16[128,8,4,256]{3,1,2,0:T(8,128)(2,1)S(1)} copy(bf16[128,8,4,256]{3,2,1,0:T(4,128)(2,1)} %bitcast.32) | data formatting | bytes 4194304
  67.8 3.1 %pack.3 = bf16[128,64,128]{2,1,0:T(8,128)(2,1)} custom-call(s32[128]{0:T(128)S(1)} %select_reduce_fusion.slots, bf16[32,32,256]{2,1,0:T(8,128)(2,1)} %cache.3, bf16[1024,256]{1,0:T(8,128)(2,1)} %collective-permute-done.3.g1.refs_0_, bf16[1024,256]{1,0:T(8,128)(2,1)S(1)} %collective-permute-done.4.g2.refs_1_, ...), custom_call_target="tpu_custom_call" | custom-call | bytes 4194304 | tf_op jit(solution)/shard_map/pack/pallas_call | solution.py:60
  72.9 9.0 %all-to-all-done.keys = bf16[128,72,128]{2,1,0:T(8,128)(2,1)S(1)} async-done(((bf16[128,72,128]{2,1,0:T(8,128)(2,1)}), bf16[128,72,128]{2,1,0:T(8,128)(2,1)S(1)}, u32[]{:S(2)}, u32[]{:S(2)}) %all-to-all-start) | async-done | bytes 2359328 | tf_op jit(solution)/shard_map/all_to_all | solution.py:316
  81.9 8.5 %all-to-all-start.1 = ((bf16[128,64,128]{2,1,0:T(8,128)(2,1)}), bf16[128,64,128]{2,1,0:T(8,128)(2,1)}, u32[]{:S(2)}, u32[]{:S(2)}) async-start(bf16[128,64,128]{2,1,0:T(8,128)(2,1)} %pack.3), calls=%async_computation.1 | async-start | bytes 4194304 | tf_op jit(solution)/shard_map/all_to_all | solution.py:334
  92.7 4.4 %collective-permute-start.2 = (bf16[512,256]{1,0:T(8,128)(2,1)S(1)}, bf16[512,256]{1,0:T(8,128)(2,1)S(1)}, u32[]{:S(2)}, u32[]{:S(2)}) collective-permute-start(bf16[512,256]{1,0:T(8,128)(2,1)S(1)} %gather_fusion), channel_id=1, source_target_pairs={{0,3},{1,0},{2,1},{3,2},{4,7},{5,4},{6,5},{7,6},{8,11},{9,8},{10,9... | collective-permute-start | bytes 786440 | tf_op jit(solution)/shard_map/ppermute | solution.py:300
  97.1 2.4 %collective-permute-start.1 = (bf16[512,256]{1,0:T(8,128)(2,1)S(1)}, bf16[512,256]{1,0:T(8,128)(2,1)S(1)}, u32[]{:S(2)}, u32[]{:S(2)}) collective-permute-start(bf16[512,256]{1,0:T(8,128)(2,1)S(1)} %gather_fusion), channel_id=1, source_target_pairs={{0,2},{1,3},{2,0},{3,1},{4,6},{5,7},{6,4},{7,5},{8,10},{9,11},{10,... | collective-permute-start | bytes 786440 | tf_op jit(solution)/shard_map/ppermute | solution.py:300
  99.6 2.7 %collective-permute-start = (bf16[512,256]{1,0:T(8,128)(2,1)S(1)}, bf16[512,256]{1,0:T(8,128)(2,1)S(1)}, u32[]{:S(2)}, u32[]{:S(2)}) collective-permute-start(bf16[512,256]{1,0:T(8,128)(2,1)S(1)} %gather_fusion), channel_id=1, source_target_pairs={{0,1},{1,2},{2,3},{3,0},{4,5},{5,6},{6,7},{7,4},{8,9},{9,10},{10,1... | collective-permute-start | bytes 786440 | tf_op jit(solution)/shard_map/ppermute | solution.py:300
  103.0 4.2 %collective-permute-done.1.r2 = bf16[512,256]{1,0:T(8,128)(2,1)S(1)} collective-permute-done((bf16[512,256]{1,0:T(8,128)(2,1)S(1)}, bf16[512,256]{1,0:T(8,128)(2,1)S(1)}, u32[]{:S(2)}, u32[]{:S(2)}) %collective-permute-start.1) | collective-permute-done | bytes 262176 | tf_op jit(solution)/shard_map/ppermute | solution.py:300
  107.2 7.2 %collective-permute-done.r1 = bf16[512,256]{1,0:T(8,128)(2,1)S(1)} collective-permute-done((bf16[512,256]{1,0:T(8,128)(2,1)S(1)}, bf16[512,256]{1,0:T(8,128)(2,1)S(1)}, u32[]{:S(2)}, u32[]{:S(2)}) %collective-permute-start) | collective-permute-done | bytes 262176 | tf_op jit(solution)/shard_map/ppermute | solution.py:300
  119.1 5.3 %project.1 = (bf16[4,512,256]{2,1,0:T(8,128)(2,1)S(1)}, bf16[512,256]{1,0:T(8,128)(2,1)S(1)}, f32[512,256]{1,0:T(8,128)S(1)}) custom-call(s32[1]{0:T(128)} %bitcast.part, bf16[512,256]{1,0:T(8,128)(2,1)S(1)} %copy-done.3, bf16[512,256]{1,0:T(8,128)(2,1)S(1)} %collective-permute-done.r1, bf16[512,256]{1,0:T(8,128)(2,1)S(1)} %collective-permute-done.1.r2, ...), custom_call_target="tpu_custom_call" | custom-call | flops 1879048192 | bytes 8388608 | tf_op jit(solution)/shard_map/project/pallas_call | solution.py:121
  125.2 6.6 %weights.1 = bf16[8,2,512,512]{3,2,1,0:T(8,128)(2,1)} custom-call(bf16[512,256]{1,0:T(8,128)(2,1)S(1)} %get-tuple-element.8.query, bf16[128,72,128]{2,1,0:T(8,128)(2,1)S(1)} %all-to-all-done.keys, f32[4,4096]{1,0:T(4,128)S(1)} %copy-done.6), custom_call_target="tpu_custom_call" | custom-call | flops 1073741824 | bytes 12582912 | tf_op jit(solution)/shard_map/weights/pallas_call | solution.py:166
  131.9 10.4 %all-to-all-done.1.values = bf16[128,64,128]{2,1,0:T(8,128)(2,1)} async-done(((bf16[128,64,128]{2,1,0:T(8,128)(2,1)}), bf16[128,64,128]{2,1,0:T(8,128)(2,1)}, u32[]{:S(2)}, u32[]{:S(2)}) %all-to-all-start.1) | async-done | bytes 2097184 | tf_op jit(solution)/shard_map/all_to_all | solution.py:334
  142.3 5.9 %values.1 = bf16[4,512,256]{2,1,0:T(8,128)(2,1)S(1)} custom-call(bf16[8,2,512,512]{3,2,1,0:T(8,128)(2,1)} %weights.1, bf16[128,64,128]{2,1,0:T(8,128)(2,1)} %all-to-all-done.1.values, f32[512,256]{1,0:T(8,128)} %copy-done.7), custom_call_target="tpu_custom_call" | custom-call | flops 1073741824 | bytes 12582912 | tf_op jit(solution)/shard_map/values/pallas_call | solution.py:228
  148.2 18.1 %all_to_all.15.attn = bf16[4,512,256]{2,1,0:T(8,128)(2,1)S(1)} all-to-all(bf16[4,512,256]{2,1,0:T(8,128)(2,1)S(1)} %values.1), channel_id=1, replica_groups=mesh['req'=128,'mp'=4] {'mp'}, dimensions={0} | all-to-all | bytes 2097152 | tf_op jit(solution)/shard_map/all_to_all | solution.py:348
  166.4 3.6 %finish.1 = bf16[512,256]{1,0:T(8,128)(2,1)} custom-call(s32[1]{0:T(128)} %bitcast.part, bf16[4,512,256]{2,1,0:T(8,128)(2,1)S(1)} %all_to_all.15.attn, bf16[4,512,256]{2,1,0:T(8,128)(2,1)S(1)} %get-tuple-element.10.gates, bf16[256,256]{1,0:T(8,128)(2,1)S(1)} %get-tuple-element.13.refs_3_.w0, bf16[256,256]{1,0:T(8,128)(2,1)} %collective-permute-done.6.refs_4_.w1, ...), custom_call_target="tpu_custom_call" | custom-call | flops 268435456 | bytes 3145728 | tf_op jit(solution)/shard_map/finish/pallas_call | solution.py:271
  (68 shorter events, 32.8 us)
Async XLA Ops:
  5.9 76.0 %all-to-all-start = ((bf16[128,72,128]{2,1,0:T(8,128)(2,1)}), bf16[128,72,128]{2,1,0:T(8,128)(2,1)S(1)}, u32[]{:S(2)}, u32[]{:S(2)}) async-start(bf16[128,72,128]{2,1,0:T(8,128)(2,1)} %pack.2), calls=%async_computation | async-start | bytes 4718592 | tf_op jit(solution)/shard_map/all_to_all | solution.py:316
  24.4 21.1 %copy-start.16 = (s32[128]{0:T(128)S(1)}, s32[128]{0:T(128)}, u32[]{:S(2)}) copy-start(s32[128]{0:T(128)} %param.17) | copy-start | bytes 1540
  24.4 24.4 %copy-start.14 = (s32[1,4,128]{2,1,0:T(4,128)S(1)}, s32[1,4,128]{2,1,0:T(4,128)}, u32[]{:S(2)}) copy-start(s32[1,4,128]{2,1,0:T(4,128)} %param.19) | copy-start | bytes 6148
  27.6 40.1 %collective-permute-start.5 = (bf16[1024,256]{1,0:T(8,128)(2,1)}, bf16[1024,256]{1,0:T(8,128)(2,1)S(1)}, u32[]{:S(2)}, u32[]{:S(2)}) collective-permute-start(bf16[1024,256]{1,0:T(8,128)(2,1)} %bitcast.25), channel_id=1, source_target_pairs={{0,3},{1,0},{2,1},{3,2},{4,7},{5,4},{6,5},{7,6},{8,11},{9,8},{10,9... | collective-permute-start | bytes 1572872 | tf_op jit(solution)/shard_map/ppermute | solution.py:300
  32.0 35.8 %collective-permute-start.4 = (bf16[1024,256]{1,0:T(8,128)(2,1)}, bf16[1024,256]{1,0:T(8,128)(2,1)S(1)}, u32[]{:S(2)}, u32[]{:S(2)}) collective-permute-start(bf16[1024,256]{1,0:T(8,128)(2,1)} %bitcast.25), channel_id=1, source_target_pairs={{0,2},{1,3},{2,0},{3,1},{4,6},{5,7},{6,4},{7,5},{8,10},{9,11},{10,... | collective-permute-start | bytes 1572872 | tf_op jit(solution)/shard_map/ppermute | solution.py:300
  34.5 33.3 %collective-permute-start.3 = (bf16[1024,256]{1,0:T(8,128)(2,1)}, bf16[1024,256]{1,0:T(8,128)(2,1)}, u32[]{:S(2)}, u32[]{:S(2)}) collective-permute-start(bf16[1024,256]{1,0:T(8,128)(2,1)} %bitcast.25), channel_id=1, source_target_pairs={{0,1},{1,2},{2,3},{3,0},{4,5},{5,6},{6,7},{7,4},{8,9},{9,10},{10,1... | collective-permute-start | bytes 1572872 | tf_op jit(solution)/shard_map/ppermute | solution.py:300
  38.9 21.1 %collective-permute-start.8 = (bf16[256,256]{1,0:T(8,128)(2,1)}, bf16[256,256]{1,0:T(8,128)(2,1)}, u32[]{:S(2)}, u32[]{:S(2)}) collective-permute-start(bf16[256,256]{1,0:T(8,128)(2,1)} %get-tuple-element.11), channel_id=1, source_target_pairs={{0,3},{1,0},{2,1},{3,2},{4,7},{5,4},{6,5},{7,6},{8,11},{9,8},{10,9... | collective-permute-start | bytes 393224 | tf_op jit(solution)/shard_map/ppermute | solution.py:300
  42.9 23.3 %collective-permute-start.6 = (bf16[256,256]{1,0:T(8,128)(2,1)}, bf16[256,256]{1,0:T(8,128)(2,1)}, u32[]{:S(2)}, u32[]{:S(2)}) collective-permute-start(bf16[256,256]{1,0:T(8,128)(2,1)} %get-tuple-element.12), channel_id=1, source_target_pairs={{0,1},{1,2},{2,3},{3,0},{4,5},{5,6},{6,7},{7,4},{8,9},{9,10},{10,1... | collective-permute-start | bytes 393224 | tf_op jit(solution)/shard_map/ppermute | solution.py:300
  60.1 7.7 %collective-permute-start.7 = (bf16[256,256]{1,0:T(8,128)(2,1)}, bf16[256,256]{1,0:T(8,128)(2,1)S(1)}, u32[]{:S(2)}, u32[]{:S(2)}) collective-permute-start(bf16[256,256]{1,0:T(8,128)(2,1)} %get-tuple-element.14), channel_id=1, source_target_pairs={{0,2},{1,3},{2,0},{3,1},{4,6},{5,7},{6,4},{7,5},{8,10},{9,11},{10,... | collective-permute-start | bytes 393224 | tf_op jit(solution)/shard_map/ppermute | solution.py:300
  64.1 3.7 %copy-start.5 = (f32[4,4096]{1,0:T(4,128)}, f32[4,4096]{1,0:T(4,128)S(1)}, u32[]{:S(2)}) copy-start(f32[4,4096]{1,0:T(4,128)S(1)} %broadcast_multiply_fusion.mask.refs_7_) | copy-start | bytes 196612
  67.8 3.1 %copy-start.8 = (bf16[1024,256]{1,0:T(8,128)(2,1)}, bf16[1024,256]{1,0:T(8,128)(2,1)S(1)}, u32[]{:S(2)}) copy-start(bf16[1024,256]{1,0:T(8,128)(2,1)S(1)} %collective-permute-done.5.g3.refs_2_) | copy-start | bytes 1572868
  67.8 3.1 %copy-start.10 = (bf16[1024,256]{1,0:T(8,128)(2,1)}, bf16[1024,256]{1,0:T(8,128)(2,1)S(1)}, u32[]{:S(2)}) copy-start(bf16[1024,256]{1,0:T(8,128)(2,1)S(1)} %collective-permute-done.4.g2.refs_1_) | copy-start | bytes 1572868
  70.9 1.3 copy-start
  72.9 17.6 %copy-start.15 = (s32[1,512]{1,0:T(1,128)S(1)}, s32[1,512]{1,0:T(1,128)}, u32[]{:S(2)}) copy-start(s32[1,512]{1,0:T(1,128)} %param.11) | copy-start | bytes 6148
  81.9 60.3 %all-to-all-start.1 = ((bf16[128,64,128]{2,1,0:T(8,128)(2,1)}), bf16[128,64,128]{2,1,0:T(8,128)(2,1)}, u32[]{:S(2)}, u32[]{:S(2)}) async-start(bf16[128,64,128]{2,1,0:T(8,128)(2,1)} %pack.3), calls=%async_computation.1 | async-start | bytes 4194304 | tf_op jit(solution)/shard_map/all_to_all | solution.py:334
  92.7 10.2 %collective-permute-start.2 = (bf16[512,256]{1,0:T(8,128)(2,1)S(1)}, bf16[512,256]{1,0:T(8,128)(2,1)S(1)}, u32[]{:S(2)}, u32[]{:S(2)}) collective-permute-start(bf16[512,256]{1,0:T(8,128)(2,1)S(1)} %gather_fusion), channel_id=1, source_target_pairs={{0,3},{1,0},{2,1},{3,2},{4,7},{5,4},{6,5},{7,6},{8,11},{9,8},{10,9... | collective-permute-start | bytes 786440 | tf_op jit(solution)/shard_map/ppermute | solution.py:300
  97.1 10.1 %collective-permute-start.1 = (bf16[512,256]{1,0:T(8,128)(2,1)S(1)}, bf16[512,256]{1,0:T(8,128)(2,1)S(1)}, u32[]{:S(2)}, u32[]{:S(2)}) collective-permute-start(bf16[512,256]{1,0:T(8,128)(2,1)S(1)} %gather_fusion), channel_id=1, source_target_pairs={{0,2},{1,3},{2,0},{3,1},{4,6},{5,7},{6,4},{7,5},{8,10},{9,11},{10,... | collective-permute-start | bytes 786440 | tf_op jit(solution)/shard_map/ppermute | solution.py:300
  99.6 14.9 %collective-permute-start = (bf16[512,256]{1,0:T(8,128)(2,1)S(1)}, bf16[512,256]{1,0:T(8,128)(2,1)S(1)}, u32[]{:S(2)}, u32[]{:S(2)}) collective-permute-start(bf16[512,256]{1,0:T(8,128)(2,1)S(1)} %gather_fusion), channel_id=1, source_target_pairs={{0,1},{1,2},{2,3},{3,0},{4,5},{5,6},{6,7},{7,4},{8,9},{9,10},{10,1... | collective-permute-start | bytes 786440 | tf_op jit(solution)/shard_map/ppermute | solution.py:300
  114.4 1.6 copy-start.1
  117.0 1.0 copy-start.9
  118.0 1.0 copy-start.11
  119.1 6.2 %copy-start.6 = (f32[4,4096]{1,0:T(4,128)S(1)}, f32[4,4096]{1,0:T(4,128)}, u32[]{:S(2)}) copy-start(f32[4,4096]{1,0:T(4,128)} %copy-done.5) | copy-start | bytes 196612
  148.2 18.2 %copy-start.4 = (bf16[512,256]{1,0:T(8,128)(2,1)S(1)}, bf16[512,256]{1,0:T(8,128)(2,1)}, u32[]{:S(2)}) copy-start(bf16[512,256]{1,0:T(8,128)(2,1)} %copy-done.2) | copy-start | bytes 786436
  148.2 18.1 %copy-start.13 = (bf16[256,256]{1,0:T(8,128)(2,1)S(1)}, bf16[256,256]{1,0:T(8,128)(2,1)}, u32[]{:S(2)}) copy-start(bf16[256,256]{1,0:T(8,128)(2,1)} %copy-done.12) | copy-start | bytes 393220
  (4 other events, 3.1 us)

commit v3 on v2

--- a/solution.py
+++ b/solution.py
@@ -12,6 +12,7 @@
 BLK = 32
 MAXBLK = 128
 GROUP = 128
+CSLOT = 4
 EPS = 1e-05
 VMEM = 28 * 1024 * 1024
 WHOLE = pl.BlockSpec(memory_space=pltpu.VMEM)
@@ -26,69 +27,113 @@
     return pl.CostEstimate(flops=flops, bytes_accessed=nbytes, transcendentals=trans)
 
 
-def pack_kernel(slots, cache, *refs):
-    out, held, made, load_sem, store_sem = refs[-5:]
-    load = pltpu.make_async_copy(cache, held, load_sem)
-    load.start()
-    load.wait()
+def spread_rows(rows_in):
+    count, columns = rows_in.shape
+    halves = columns // DH
+    x = jnp.concatenate([rows_in[:, h * DH : (h + 1) * DH] for h in range(halves)], axis=0)
+    shape = (halves * count, halves * count)
+    at = lax.broadcasted_iota(jnp.int32, shape, 0)
+    source = lax.broadcasted_iota(jnp.int32, shape, 1)
+    group, inner = at // (CSLOT * halves), at % (CSLOT * halves)
+    wanted = (inner // CSLOT) * count + group * CSLOT + inner % CSLOT
+    pick = jnp.where(source == wanted, 1.0, 0.0).astype(jnp.bfloat16)
+    return jnp.dot(pick, x, preferred_element_type=jnp.float32).astype(rows_in.dtype)
+
+
+def pack_kernel(home_in, table_in, cache, *refs):
+    out, home, table, held, made, cand, index_sem, load_sem, store_sem = refs[-9:]
+    indices = [
+        pltpu.make_async_copy(home_in, home, index_sem.at[0]),
+        pltpu.make_async_copy(table_in, table, index_sem.at[1]),
+    ]
+    parts = load_sem.shape[0]
+    size = cache.shape[0] // parts
+    blocks = []
+    for i in range(parts):
+        at = pl.ds(i * size, size)
+        blocks.append(pltpu.make_async_copy(cache.at[at], held.at[at], load_sem.at[i]))
+    for load in indices:
+        load.start()
     shards, rows, _ = made.shape
+    if rows > 2 * BLK:
+        extra = pltpu.make_async_copy(refs[0], cand, index_sem.at[2])
+        extra.start()
+    for load in blocks:
+        load.start()
+    if rows > 2 * BLK:
+        extra.wait()
+        step = 32
+        for b in range(0, cand.shape[0], step):
+            x = spread_rows(cand[b : b + step, :])
+            n = step // CSLOT
+            made[b // CSLOT : b // CSLOT + n, 2 * BLK :, :] = x.reshape(n, rows - 2 * BLK, DH)
+    for load in indices + blocks:
+        load.wait()
+    me = lax.axis_index("req")
     per = shards // store_sem.shape[0]
     stores = []
     for c in range(store_sem.shape[0]):
         chunk = pl.ds(c * per, per)
         for r in range(c * per, (c + 1) * per):
-            block = held[slots[r]]
+            behind = me - home[r]
+            block = held[table[r, jnp.where(behind < 0, behind + shards, behind)]]
             made[r, :BLK, :] = block[:, :DH]
             made[r, BLK : 2 * BLK, :] = block[:, DH:]
-        if rows > 2 * BLK:
-            made[chunk, 2 * BLK :, :] = refs[0][chunk]
         stores.append(pltpu.make_async_copy(made.at[chunk], out.at[chunk], store_sem.at[c]))
         stores[-1].start()
     for store in stores:
         store.wait()
 
 
-def pack(slots, cache, extra=None, after=()):
-    shards = slots.shape[0]
-    rows = 2 * BLK + (0 if extra is None else extra.shape[1])
-    in_specs, args = [IN_HBM], [hbm(cache)]
-    if extra is not None:
-        in_specs.append(WHOLE)
-        args.append(extra)
-    in_specs += [pl.BlockSpec(memory_space=pl.ANY)] * len(after)
+def pack(home, table, cache, cand=None, after=()):
+    shards = home.shape[0]
+    rows = 2 * BLK
+    args = [hbm(home), hbm(table), hbm(cache)]
+    held_cand = (16, DH)
+    if cand is not None:
+        rows += cand.shape[0] * cand.shape[1] // (DH * shards)
+        args.append(hbm(cand))
+        held_cand = cand.shape
+    in_specs = [IN_HBM] * len(args) + [pl.BlockSpec(memory_space=pl.ANY)] * len(after)
     out_shape = (shards, rows, DH)
     return pl.pallas_call(
         pack_kernel,
         out_shape=pltpu.HBM(out_shape, cache.dtype),
-        in_specs=[pl.BlockSpec(memory_space=pltpu.SMEM)] + in_specs,
+        in_specs=in_specs,
         out_specs=IN_HBM,
         scratch_shapes=[
+            pltpu.SMEM(home.shape, jnp.int32),
+            pltpu.SMEM(table.shape, jnp.int32),
             pltpu.VMEM(cache.shape, cache.dtype),
             pltpu.VMEM(out_shape, cache.dtype),
-            pltpu.SemaphoreType.DMA,
+            pltpu.VMEM(held_cand, cache.dtype),
+            pltpu.SemaphoreType.DMA((3,)),
+            pltpu.SemaphoreType.DMA((4,)),
             pltpu.SemaphoreType.DMA((4,)),
         ],
         compiler_params=pltpu.CompilerParams(vmem_limit_bytes=VMEM),
         cost_estimate=cost(0, 2 * shards * rows * DH * 2),
         name="pack",
-    )(slots, *args, *after)
+    )(*args, *after)
 
 
 def silu(half):
     return half + half * jnp.tanh(half)
 
 
-def project_kernel(part, r0, r1, r2, r3, w, g1, g2, g3, gates, query, own, normed):
+def project_kernel(r0, r1, r2, r3, w, g1, g2, g3, gates, query, own, normed):
     pieces = [r[...].astype(jnp.float32) for r in (r0, r1, r2, r3)]
     split = len(pieces)
     width = r0.shape[1]
     total = split * width
+    part = lax.axis_index("mp")
+    place = [lax.rem(part + (split - d), split) for d in range(split)]
     mean = sum(jnp.sum(p, axis=1, keepdims=True) for p in pieces) / total
     centred = [p - mean for p in pieces]
     spread = sum(jnp.sum(c * c, axis=1, keepdims=True) for c in centred) / total
     scale = lax.rsqrt(spread + EPS)
     for d in range(split):
-        at = pl.multiple_of(lax.rem(part[0] + (split - d), split) * width, width)
+        at = pl.multiple_of(place[d] * width, width)
         normed[:, pl.ds(at, width)] = (centred[d] * scale).astype(jnp.bfloat16)
     x = normed[...]
 
@@ -97,9 +142,9 @@
             jnp.bfloat16
         )
 
-    gates[0] = times(w[:, :width])
+    gates[place[0]] = times(w[:, :width])
     for d, g in ((1, g1), (2, g2), (3, g3)):
-        gates[d] = times(g[...])
+        gates[place[d]] = times(g[...])
     value = times(w[:, width : 2 * width]).astype(jnp.float32)
     q = times(w[:, 2 * width : 3 * width])
     query[...] = q
@@ -111,35 +156,32 @@
         own[:, cols] = silu(half) * value[:, cols]
 
 
-def project(part, rows, w, gate_w):
+def project(rows, w, gate_w):
     cands, width = rows[0].shape
     split = len(rows)
     depth = split * width
     step = 128
-    block = pl.BlockSpec((step, width), lambda i, s: (i, 0))
-    whole = lambda a: pl.BlockSpec(a.shape, lambda i, s: (0, 0))
+    block = pl.BlockSpec((step, width), lambda i: (i, 0))
+    whole = lambda a: pl.BlockSpec(a.shape, lambda i: (0, 0))
     return pl.pallas_call(
         project_kernel,
         out_shape=(
             jax.ShapeDtypeStruct((split, cands, width), jnp.bfloat16),
             jax.ShapeDtypeStruct((cands, width), jnp.bfloat16),
-            jax.ShapeDtypeStruct((cands, width), jnp.float32),
+            pltpu.HBM((cands, width), jnp.float32),
         ),
-        grid_spec=pltpu.PrefetchScalarGridSpec(
-            num_scalar_prefetch=1,
-            grid=(cands // step,),
-            in_specs=[block] * split + [whole(w)] + [whole(g) for g in gate_w],
-            out_specs=(
-                pl.BlockSpec((split, step, width), lambda i, s: (0, i, 0)),
-                block,
-                block,
-            ),
-            scratch_shapes=[pltpu.VMEM((step, depth), jnp.bfloat16)],
+        grid=(cands // step,),
+        in_specs=[block] * split + [whole(w)] + [whole(g) for g in gate_w],
+        out_specs=(
+            pl.BlockSpec((split, step, width), lambda i: (0, i, 0)),
+            block,
+            block,
         ),
+        scratch_shapes=[pltpu.VMEM((step, depth), jnp.bfloat16)],
         compiler_params=pltpu.CompilerParams(vmem_limit_bytes=VMEM),
         cost_estimate=cost(2 * cands * depth * 7 * width, 8 << 20, cands * 7 * width),
         name="project",
-    )(part, *rows, w, *gate_w)
+    )(*[hbm(r) for r in rows], hbm(w), *[hbm(g) for g in gate_w])
 
 
 def weights_kernel(query, keys, mask, out):
@@ -245,42 +287,52 @@
     )(hbm(weights), hbm(got), hbm(own))
 
 
-def finish_kernel(part, attn, gates, w0, w1, w2, w3, rows, out):
-    split, _, width = attn.shape
-    step = out.shape[0]
-    here = pl.ds(pl.multiple_of(pl.program_id(0) * step, step), step)
-    pieces = [
-        attn[lax.rem(part[0] + (split - d), split), here, :].astype(jnp.float32)
-        for d in range(split)
-    ]
+def finish_kernel(attn, gates, w, rows, out, made, sems):
+    split, cands, width = attn.shape
     total = split * width
-    mean = jnp.sum(sum(pieces), axis=1, keepdims=True) / total
-    centred = [p - mean for p in pieces]
-    spread = jnp.sum(sum(c * c for c in centred), axis=1, keepdims=True) / total
-    scale = lax.rsqrt(spread + EPS)
-    result = rows[here, :].astype(jnp.float32)
-    for d, w in enumerate((w0, w1, w2, w3)):
-        hidden = (centred[d] * scale * gates[d, here, :].astype(jnp.float32)).astype(jnp.bfloat16)
-        result += jnp.dot(hidden, w[...], preferred_element_type=jnp.float32)
-    out[...] = result.astype(out.dtype)
-
-
-def finish(part, attn, gates, ws, rows):
+    count = sems.shape[0]
+    step = cands // count
+    stores = []
+    for b in range(count):
+        here = slice(b * step, (b + 1) * step)
+        pieces = [attn[i, here, :].astype(jnp.float32) for i in range(split)]
+        mean = jnp.sum(sum(pieces), axis=1, keepdims=True) / total
+        centred = [p - mean for p in pieces]
+        spread = jnp.sum(sum(c * c for c in centred), axis=1, keepdims=True) / total
+        scale = lax.rsqrt(spread + EPS)
+        hidden = jnp.concatenate(
+            [
+                (centred[i] * scale * gates[i, here, :].astype(jnp.float32)).astype(jnp.bfloat16)
+                for i in range(split)
+            ],
+            axis=1,
+        )
+        result = rows[here, :].astype(jnp.float32) + jnp.dot(
+            hidden, w[...], preferred_element_type=jnp.float32
+        )
+        made[here, :] = result.astype(made.dtype)
+        at = pl.ds(b * step, step)
+        stores.append(pltpu.make_async_copy(made.at[at], out.at[at], sems.at[b]))
+        stores[-1].start()
+    for store in stores:
+        store.wait()
+
+
+def finish(attn, gates, w, rows):
     split, cands, width = attn.shape
-    step = 128
     return pl.pallas_call(
         finish_kernel,
-        out_shape=jax.ShapeDtypeStruct(rows.shape, jnp.bfloat16),
-        grid_spec=pltpu.PrefetchScalarGridSpec(
-            num_scalar_prefetch=1,
-            grid=(cands // step,),
-            in_specs=[WHOLE] * (3 + len(ws)),
-            out_specs=pl.BlockSpec((step, rows.shape[1]), lambda i, s: (i, 0)),
-        ),
+        out_shape=pltpu.HBM(rows.shape, jnp.bfloat16),
+        in_specs=[WHOLE] * 4,
+        out_specs=IN_HBM,
+        scratch_shapes=[
+            pltpu.VMEM(rows.shape, jnp.bfloat16),
+            pltpu.SemaphoreType.DMA((4,)),
+        ],
         compiler_params=pltpu.CompilerParams(vmem_limit_bytes=VMEM),
         cost_estimate=cost(2 * cands * split * width * rows.shape[1], 3 << 20),
         name="finish",
-    )(part, attn, gates, *ws, rows)
+    )(attn, gates, w, rows)
 
 
 def local(
@@ -290,8 +342,8 @@
     split = lax.axis_size("mp")
     me = lax.axis_index("req")
     part = lax.axis_index("mp")
-    parts = part.astype(jnp.int32).reshape(1)
     columns = cand_feats.shape[1]
+    halves = columns // DH
     cand_slot = cand_feats.shape[0] // shards
     cands = cand_perm.shape[1]
     width = w_in.shape[2]
@@ -299,21 +351,10 @@
     def back(x, d):
         return lax.ppermute(x, "mp", [(i, (i + d) % split) for i in range(split)])
 
-    behind = me - hist_home
-    wanted = jnp.where(behind < 0, behind + shards, behind)
-    places = jnp.arange(MAXBLK, dtype=jnp.int32)
-    slots = jnp.sum(jnp.where(places[None, :] == wanted[:, None], hist_slot, 0), axis=1)
-
-    halves = columns // DH
-    cand_rows = (
-        cand_feats.reshape(shards, cand_slot, halves, DH)
-        .transpose(0, 2, 1, 3)
-        .reshape(shards, cand_slot * halves, DH)
-    )
     exchange = functools.partial(
         lax.all_to_all, axis_name="req", split_axis=0, concat_axis=0, tiled=True
     )
-    got_keys = exchange(pack(slots, cache_k, extra=cand_rows))
+    got_keys = exchange(pack(hist_home, hist_slot, cache_k, cand=cand_feats))
 
     w_gate = w_in[:, 0, :]
     gate_w = [back(w_gate, d) for d in range(1, split)]
@@ -321,6 +362,9 @@
     for d in range(split):
         piece = lax.dynamic_slice_in_dim(w_out, (part + d) % split * columns, columns, axis=1)
         own_out.append(back(piece, d) if d else piece)
+    backs = (part - jnp.arange(split, dtype=jnp.int32)) % split
+    own_out = jnp.take(jnp.stack(own_out), backs, axis=0, mode="clip")
+    own_out = own_out.reshape(split * columns, columns)
 
     home = hist_home[me]
     order = (jnp.arange(shards, dtype=jnp.int32) - home) % shards
@@ -330,8 +374,8 @@
     mask = mask.reshape(hist_mask.shape[1], shards * BLK)
 
     w_flat = w_in.reshape(w_in.shape[0], 4 * width)
-    ready = [*gate_w, *own_out, mask, w_flat]
-    got_values = exchange(pack(slots, cache_v, after=ready))
+    ready = [*gate_w, own_out, mask, w_flat]
+    got_values = exchange(pack(hist_home, hist_slot, cache_v, after=ready))
 
     arrived = (
         got_keys[:, 2 * BLK :, :]
@@ -341,12 +385,12 @@
     )
     own_rows = jnp.take(arrived, cand_perm[0], axis=0, mode="clip")
     rows = [own_rows] + [back(own_rows, d) for d in range(1, split)]
-    gates, query, own = project(parts, rows, w_flat, gate_w)
+    gates, query, own = project(rows, w_flat, gate_w)
 
     weights = attention_weights(query, got_keys, mask)
     attn = weighted_values(weights, got_values, own, split)
     attn = lax.all_to_all(attn, "mp", split_axis=0, concat_axis=0, tiled=True)
-    return finish(parts, attn, gates, own_out, own_rows)
+    return finish(attn, gates, own_out, own_rows)
 
 
 def solution(mesh):

time: 171 us -> 168 us (0.982)
  waiting for transfers between devices: 32.4 us -> 47.8 us
  local copies, waits for them, and re-layouts: 29.9 us -> 15.5 us
  other arithmetic: 5.86 us -> 2.14 us
    ppermute x9, waiting for transfers between devices: 13 us -> 29.2 us  [back(): return lax.ppermute(x, 'mp', [(i, (i + d) % split) for i in range(split)])]
    add x4, local copies, waits for them, and re-layouts: 4.4 us -> 0.25 us  [local(): order[:, None] * BLK + jnp.arange(BLK, dtype=jnp.int32)[None, :]]
    unnamed x38 -> x32, local copies, waits for them, and re-layouts: 12 us -> 7.86 us
    all_to_all x2, starting transfers between devices: 27 us -> 29.9 us  [the longest x1 18.4 us: local(): got_keys = exchange(pack(hist_home, hist_slot, cache_k, cand=cand_feats))]
    mul x2, local copies, waits for them, and re-layouts: 2.56 us -> 0.29 us  [local(): mask = seen[:, :, None] * jnp.where(inside, 0.5 * DH ** (-0.5), 0.0)[None]]
    ppermute x9, starting transfers between devices: 27.9 us -> 25.6 us  [back(): return lax.ppermute(x, 'mp', [(i, (i + d) % split) for i in range(split)])]
    pallas_call x1, Pallas kernels: 3.57 us -> 1.62 us  [finish(): pl.pallas_call(finish_kernel, out_shape=pltpu.HBM(rows.shape, jnp.bfloat1...]
    dynamic_slice x1 -> x0, local copies, waits for them, and re-layouts: 1.88 us -> none  [local(): lax.dynamic_slice_in_dim(w_out, (part + d) % split * columns, columns, ax...]
  transfers between devices with their start and end apart: 11 -> 11, of which waited for: 5 -> 7; matrix products, arithmetic and copies ran while one was open for 15% -> 9% of each run, Pallas kernels for 9% -> 10%
where the time goes in v3:
time: 168 us; the launch traced here: 167 us
  starting transfers between devices  55.5 us (33%)
  waiting for transfers between devices  47.8 us (28%)
  Pallas kernels  28.4 us (17%)
  blocking collectives  16.8 us (10%)
  local copies, waits for them, and re-layouts  15.5 us (9%)
  other arithmetic  2.14 us (1%)
    ppermute x9, waiting for transfers between devices, back(): return lax.ppermute(x, 'mp', [(i, (i + d) % split) for i in range(split)])  29.2 us
    ppermute x9, starting transfers between devices, back(): return lax.ppermute(x, 'mp', [(i, (i + d) % split) for i in range(split)])  25.6 us
    all_to_all x1, starting transfers between devices, local(): got_keys = exchange(pack(hist_home, hist_slot, cache_k, cand=cand_feats))  18.4 us
    all_to_all x1, blocking collectives, local(): attn = lax.all_to_all(attn, 'mp', split_axis=0, concat_axis=0, tiled=True)  16.8 us
    all_to_all x1, waiting for transfers between devices, local(): got_values = exchange(pack(hist_home, hist_slot, cache_v, after=ready))  14.9 us
    all_to_all x1, starting transfers between devices, local(): got_values = exchange(pack(hist_home, hist_slot, cache_v, after=ready))  11.5 us
    unnamed x32, local copies, waits for them, and re-layouts  7.86 us
    pallas_call x1, Pallas kernels, project(): pl.pallas_call(project_kernel, out_shape=(jax.ShapeDtypeStruct((split, ca...  7.1 us
  transfers between devices with their start and end apart: 11, of which 7 were waited for; matrix products, arithmetic and copies ran while one was open for 9% of the time, Pallas kernels for 10%

profile of v3, /device:TPU:1, one launch (start us, length us, event | category | flops | bytes accessed | tf_op | source)
XLA Modules:
  0.0 167.4 jit_solution(16436725492603665844)
XLA Ops:
  0.0 3.5 %pack.2 = bf16[128,72,128]{2,1,0:T(8,128)(2,1)} custom-call(s32[128]{0:T(128)} %home_in.3, s32[128,128]{1,0:T(8,128)} %table_in.3, bf16[32,32,256]{2,1,0:T(8,128)(2,1)} %cache.2, bf16[512,256]{1,0:T(8,128)(2,1)} %refs_0_.1), custom_call_target="tpu_custom_call" | custom-call | bytes 4718592 | tf_op jit(solution)/shard_map/pack/pallas_call | solution.py:99
  3.6 18.4 %all-to-all-start = ((bf16[128,72,128]{2,1,0:T(8,128)(2,1)}), bf16[128,72,128]{2,1,0:T(8,128)(2,1)S(1)}, u32[]{:S(2)}, u32[]{:S(2)}) async-start(bf16[128,72,128]{2,1,0:T(8,128)(2,1)} %pack.2), calls=%async_computation | async-start | bytes 4718592 | tf_op jit(solution)/shard_map/all_to_all | solution.py:357
  22.0 2.4 %slice.7 = bf16[1024,1,256]{2,1,0:T(2,128)(2,1)S(1)} slice(bf16[1024,4,256]{2,1,0:T(4,128)(2,1)} %param.12), slice={[0:1024], [0:1], [0:256]} | slice | bytes 1048576 | tf_op jit(solution)/shard_map/slice | solution.py:359
  25.3 4.4 %collective-permute-start.5 = (bf16[1024,256]{1,0:T(8,128)(2,1)}, bf16[1024,256]{1,0:T(8,128)(2,1)}, u32[]{:S(2)}, u32[]{:S(2)}) collective-permute-start(bf16[1024,256]{1,0:T(8,128)(2,1)} %bitcast.29), channel_id=1, source_target_pairs={{0,3},{1,0},{2,1},{3,2},{4,7},{5,4},{6,5},{7,6},{8,11},{9,8},{10,9... | collective-permute-start | bytes 1572872 | tf_op jit(solution)/shard_map/ppermute | solution.py:352
  29.7 2.4 %collective-permute-start.4 = (bf16[1024,256]{1,0:T(8,128)(2,1)}, bf16[1024,256]{1,0:T(8,128)(2,1)}, u32[]{:S(2)}, u32[]{:S(2)}) collective-permute-start(bf16[1024,256]{1,0:T(8,128)(2,1)} %bitcast.29), channel_id=1, source_target_pairs={{0,2},{1,3},{2,0},{3,1},{4,6},{5,7},{6,4},{7,5},{8,10},{9,11},{10,... | collective-permute-start | bytes 1572872 | tf_op jit(solution)/shard_map/ppermute | solution.py:352
  32.1 2.5 %collective-permute-start.3 = (bf16[1024,256]{1,0:T(8,128)(2,1)}, bf16[1024,256]{1,0:T(8,128)(2,1)}, u32[]{:S(2)}, u32[]{:S(2)}) collective-permute-start(bf16[1024,256]{1,0:T(8,128)(2,1)} %bitcast.29), channel_id=1, source_target_pairs={{0,1},{1,2},{2,3},{3,0},{4,5},{5,6},{6,7},{7,4},{8,9},{9,10},{10,1... | collective-permute-start | bytes 1572872 | tf_op jit(solution)/shard_map/ppermute | solution.py:352
  35.4 3.4 %collective-permute-start.6 = (bf16[256,256]{1,0:T(8,128)(2,1)S(1)}, bf16[256,256]{1,0:T(8,128)(2,1)S(1)}, u32[]{:S(2)}, u32[]{:S(2)}) collective-permute-start(bf16[256,256]{1,0:T(8,128)(2,1)S(1)} %get-tuple-element.12), channel_id=1, source_target_pairs={{0,1},{1,2},{2,3},{3,0},{4,5},{5,6},{6,7},{7,4},{8,9},{9,10},{10,1... | collective-permute-start | bytes 393224 | tf_op jit(solution)/shard_map/ppermute | solution.py:352
  38.9 3.1 %collective-permute-start.8 = (bf16[256,256]{1,0:T(8,128)(2,1)S(1)}, bf16[256,256]{1,0:T(8,128)(2,1)S(1)}, u32[]{:S(2)}, u32[]{:S(2)}) collective-permute-start(bf16[256,256]{1,0:T(8,128)(2,1)S(1)} %get-tuple-element.13), channel_id=1, source_target_pairs={{0,3},{1,0},{2,1},{3,2},{4,7},{5,4},{6,5},{7,6},{8,11},{9,8},{10,9... | collective-permute-start | bytes 393224 | tf_op jit(solution)/shard_map/ppermute | solution.py:352
  45.7 15.4 %collective-permute-done.6 = bf16[256,256]{1,0:T(8,128)(2,1)S(1)} collective-permute-done((bf16[256,256]{1,0:T(8,128)(2,1)S(1)}, bf16[256,256]{1,0:T(8,128)(2,1)S(1)}, u32[]{:S(2)}, u32[]{:S(2)}) %collective-permute-start.6) | collective-permute-done | bytes 131104 | tf_op jit(solution)/shard_map/ppermute | solution.py:352
  61.2 2.4 %collective-permute-start.7 = (bf16[256,256]{1,0:T(8,128)(2,1)S(1)}, bf16[256,256]{1,0:T(8,128)(2,1)S(1)}, u32[]{:S(2)}, u32[]{:S(2)}) collective-permute-start(bf16[256,256]{1,0:T(8,128)(2,1)S(1)} %get-tuple-element.14), channel_id=1, source_target_pairs={{0,2},{1,3},{2,0},{3,1},{4,6},{5,7},{6,4},{7,5},{8,10},{9,11},{10,... | collective-permute-start | bytes 393224 | tf_op jit(solution)/shard_map/ppermute | solution.py:352
  63.6 3.4 %copy.21 = bf16[128,8,4,256]{3,1,2,0:T(8,128)(2,1)} copy(bf16[128,8,4,256]{3,2,1,0:T(4,128)(2,1)} %bitcast.37) | data formatting | bytes 4194304
  67.1 2.0 %collective-permute-done.7 = bf16[256,256]{1,0:T(8,128)(2,1)S(1)} collective-permute-done((bf16[256,256]{1,0:T(8,128)(2,1)S(1)}, bf16[256,256]{1,0:T(8,128)(2,1)S(1)}, u32[]{:S(2)}, u32[]{:S(2)}) %collective-permute-start.7) | collective-permute-done | bytes 131104 | tf_op jit(solution)/shard_map/ppermute | solution.py:352
  72.3 3.5 %pack.3 = bf16[128,64,128]{2,1,0:T(8,128)(2,1)} custom-call(s32[128]{0:T(128)} %home_in.3, s32[128,128]{1,0:T(8,128)} %table_in.3, bf16[32,32,256]{2,1,0:T(8,128)(2,1)} %cache.3, bf16[1024,256]{1,0:T(8,128)(2,1)} %collective-permute-done.3.g1.refs_0_, bf16[1024,256]{1,0:T(8,128)(2,1)} %collective-permute-done.4.g2.refs_1_, ...), custom_call_target="tpu_custom_call" | custom-call | bytes 4194304 | tf_op jit(solution)/shard_map/pack/pallas_call | solution.py:99
  75.9 3.7 %all-to-all-done.keys = bf16[128,72,128]{2,1,0:T(8,128)(2,1)S(1)} async-done(((bf16[128,72,128]{2,1,0:T(8,128)(2,1)}), bf16[128,72,128]{2,1,0:T(8,128)(2,1)S(1)}, u32[]{:S(2)}, u32[]{:S(2)}) %all-to-all-start) | async-done | bytes 2359328 | tf_op jit(solution)/shard_map/all_to_all | solution.py:357
  79.5 11.5 %all-to-all-start.1 = ((bf16[128,64,128]{2,1,0:T(8,128)(2,1)}), bf16[128,64,128]{2,1,0:T(8,128)(2,1)}, u32[]{:S(2)}, u32[]{:S(2)}) async-start(bf16[128,64,128]{2,1,0:T(8,128)(2,1)} %pack.3), calls=%async_computation.1 | async-start | bytes 4194304 | tf_op jit(solution)/shard_map/all_to_all | solution.py:378
  95.3 2.4 %collective-permute-start.1 = (bf16[512,256]{1,0:T(8,128)(2,1)S(1)}, bf16[512,256]{1,0:T(8,128)(2,1)S(1)}, u32[]{:S(2)}, u32[]{:S(2)}) collective-permute-start(bf16[512,256]{1,0:T(8,128)(2,1)S(1)} %gather_fusion), channel_id=1, source_target_pairs={{0,2},{1,3},{2,0},{3,1},{4,6},{5,7},{6,4},{7,5},{8,10},{9,11},{10,... | collective-permute-start | bytes 786440 | tf_op jit(solution)/shard_map/ppermute | solution.py:352
  97.7 3.0 %collective-permute-start = (bf16[512,256]{1,0:T(8,128)(2,1)S(1)}, bf16[512,256]{1,0:T(8,128)(2,1)S(1)}, u32[]{:S(2)}, u32[]{:S(2)}) collective-permute-start(bf16[512,256]{1,0:T(8,128)(2,1)S(1)} %gather_fusion), channel_id=1, source_target_pairs={{0,1},{1,2},{2,3},{3,0},{4,5},{5,6},{6,7},{7,4},{8,9},{9,10},{10,1... | collective-permute-start | bytes 786440 | tf_op jit(solution)/shard_map/ppermute | solution.py:352
  102.2 3.3 %collective-permute-done.1.r2 = bf16[512,256]{1,0:T(8,128)(2,1)S(1)} collective-permute-done((bf16[512,256]{1,0:T(8,128)(2,1)S(1)}, bf16[512,256]{1,0:T(8,128)(2,1)S(1)}, u32[]{:S(2)}, u32[]{:S(2)}) %collective-permute-start.1) | collective-permute-done | bytes 262176 | tf_op jit(solution)/shard_map/ppermute | solution.py:352
  105.5 7.0 %collective-permute-done.r1 = bf16[512,256]{1,0:T(8,128)(2,1)S(1)} collective-permute-done((bf16[512,256]{1,0:T(8,128)(2,1)S(1)}, bf16[512,256]{1,0:T(8,128)(2,1)S(1)}, u32[]{:S(2)}, u32[]{:S(2)}) %collective-permute-start) | collective-permute-done | bytes 262176 | tf_op jit(solution)/shard_map/ppermute | solution.py:352
  113.2 7.1 %project.1 = (bf16[4,512,256]{2,1,0:T(8,128)(2,1)S(1)}, bf16[512,256]{1,0:T(8,128)(2,1)S(1)}, f32[512,256]{1,0:T(8,128)}) custom-call(bf16[512,256]{1,0:T(8,128)(2,1)} %copy-done.3, bf16[512,256]{1,0:T(8,128)(2,1)} %copy-done.13, bf16[512,256]{1,0:T(8,128)(2,1)} %copy-done.12, bf16[512,256]{1,0:T(8,128)(2,1)} %copy-done.11, bf16[1024,1024]{1,0:T(8,128)(2,1)} %bitcast.32, ...), custom_call_target="tpu_custom_call" | custom-call | flops 1879048192 | bytes 8388608 | tf_op jit(solution)/shard_map/project/pallas_call | solution.py:166
  121.3 6.7 %weights.1 = bf16[8,2,512,512]{3,2,1,0:T(8,128)(2,1)} custom-call(bf16[512,256]{1,0:T(8,128)(2,1)S(1)} %get-tuple-element.8.query, bf16[128,72,128]{2,1,0:T(8,128)(2,1)S(1)} %all-to-all-done.keys, f32[4,4096]{1,0:T(4,128)S(1)} %broadcast_multiply_fusion.mask.refs_4_), custom_call_target="tpu_custom_call" | custom-call | flops 1073741824 | bytes 12582912 | tf_op jit(solution)/shard_map/weights/pallas_call | solution.py:208
  128.0 14.9 %all-to-all-done.1.values = bf16[128,64,128]{2,1,0:T(8,128)(2,1)} async-done(((bf16[128,64,128]{2,1,0:T(8,128)(2,1)}), bf16[128,64,128]{2,1,0:T(8,128)(2,1)}, u32[]{:S(2)}, u32[]{:S(2)}) %all-to-all-start.1) | async-done | bytes 2097184 | tf_op jit(solution)/shard_map/all_to_all | solution.py:378
  142.8 5.9 %values.1 = bf16[4,512,256]{2,1,0:T(8,128)(2,1)S(1)} custom-call(bf16[8,2,512,512]{3,2,1,0:T(8,128)(2,1)} %weights.1, bf16[128,64,128]{2,1,0:T(8,128)(2,1)} %all-to-all-done.1.values, f32[512,256]{1,0:T(8,128)} %get-tuple-element.9.own), custom_call_target="tpu_custom_call" | custom-call | flops 1073741824 | bytes 12582912 | tf_op jit(solution)/shard_map/values/pallas_call | solution.py:270
  148.8 16.8 %all_to_all.15.attn = bf16[4,512,256]{2,1,0:T(8,128)(2,1)S(1)} all-to-all(bf16[4,512,256]{2,1,0:T(8,128)(2,1)S(1)} %values.1), channel_id=1, replica_groups=mesh['req'=128,'mp'=4] {'mp'}, dimensions={0} | all-to-all | bytes 2097152 | tf_op jit(solution)/shard_map/all_to_all | solution.py:392
  (62 shorter events, 16.8 us)
Async XLA Ops:
  3.6 76.0 %all-to-all-start = ((bf16[128,72,128]{2,1,0:T(8,128)(2,1)}), bf16[128,72,128]{2,1,0:T(8,128)(2,1)S(1)}, u32[]{:S(2)}, u32[]{:S(2)}) async-start(bf16[128,72,128]{2,1,0:T(8,128)(2,1)} %pack.2), calls=%async_computation | async-start | bytes 4718592 | tf_op jit(solution)/shard_map/all_to_all | solution.py:357
  22.0 12.7 %copy-start.5 = (bf16[256,1024]{1,0:T(8,128)(2,1)S(1)}, bf16[256,1024]{1,0:T(8,128)(2,1)}, u32[]{:S(2)}) copy-start(bf16[256,1024]{1,0:T(8,128)(2,1)} %param.13) | copy-start | bytes 1572868
  22.0 20.6 %copy-start.10 = (s32[128]{0:T(128)S(1)}, s32[128]{0:T(128)}, u32[]{:S(2)}) copy-start(s32[128]{0:T(128)} %home_in.3) | copy-start | bytes 1540
  22.0 21.9 %copy-start.8 = (s32[1,4,128]{2,1,0:T(4,128)S(1)}, s32[1,4,128]{2,1,0:T(4,128)}, u32[]{:S(2)}) copy-start(s32[1,4,128]{2,1,0:T(4,128)} %param.19) | copy-start | bytes 6148
  25.3 45.4 %collective-permute-start.5 = (bf16[1024,256]{1,0:T(8,128)(2,1)}, bf16[1024,256]{1,0:T(8,128)(2,1)}, u32[]{:S(2)}, u32[]{:S(2)}) collective-permute-start(bf16[1024,256]{1,0:T(8,128)(2,1)} %bitcast.29), channel_id=1, source_target_pairs={{0,3},{1,0},{2,1},{3,2},{4,7},{5,4},{6,5},{7,6},{8,11},{9,8},{10,9... | collective-permute-start | bytes 1572872 | tf_op jit(solution)/shard_map/ppermute | solution.py:352
  29.7 41.0 %collective-permute-start.4 = (bf16[1024,256]{1,0:T(8,128)(2,1)}, bf16[1024,256]{1,0:T(8,128)(2,1)}, u32[]{:S(2)}, u32[]{:S(2)}) collective-permute-start(bf16[1024,256]{1,0:T(8,128)(2,1)} %bitcast.29), channel_id=1, source_target_pairs={{0,2},{1,3},{2,0},{3,1},{4,6},{5,7},{6,4},{7,5},{8,10},{9,11},{10,... | collective-permute-start | bytes 1572872 | tf_op jit(solution)/shard_map/ppermute | solution.py:352
  32.1 38.6 %collective-permute-start.3 = (bf16[1024,256]{1,0:T(8,128)(2,1)}, bf16[1024,256]{1,0:T(8,128)(2,1)}, u32[]{:S(2)}, u32[]{:S(2)}) collective-permute-start(bf16[1024,256]{1,0:T(8,128)(2,1)} %bitcast.29), channel_id=1, source_target_pairs={{0,1},{1,2},{2,3},{3,0},{4,5},{5,6},{6,7},{7,4},{8,9},{9,10},{10,1... | collective-permute-start | bytes 1572872 | tf_op jit(solution)/shard_map/ppermute | solution.py:352
  35.4 25.7 %collective-permute-start.6 = (bf16[256,256]{1,0:T(8,128)(2,1)S(1)}, bf16[256,256]{1,0:T(8,128)(2,1)S(1)}, u32[]{:S(2)}, u32[]{:S(2)}) collective-permute-start(bf16[256,256]{1,0:T(8,128)(2,1)S(1)} %get-tuple-element.12), channel_id=1, source_target_pairs={{0,1},{1,2},{2,3},{3,0},{4,5},{5,6},{6,7},{7,4},{8,9},{9,10},{10,1... | collective-permute-start | bytes 393224 | tf_op jit(solution)/shard_map/ppermute | solution.py:352
  38.9 28.2 %collective-permute-start.8 = (bf16[256,256]{1,0:T(8,128)(2,1)S(1)}, bf16[256,256]{1,0:T(8,128)(2,1)S(1)}, u32[]{:S(2)}, u32[]{:S(2)}) collective-permute-start(bf16[256,256]{1,0:T(8,128)(2,1)S(1)} %get-tuple-element.13), channel_id=1, source_target_pairs={{0,3},{1,0},{2,1},{3,2},{4,7},{5,4},{6,5},{7,6},{8,11},{9,8},{10,9... | collective-permute-start | bytes 393224 | tf_op jit(solution)/shard_map/ppermute | solution.py:352
  61.2 8.0 %collective-permute-start.7 = (bf16[256,256]{1,0:T(8,128)(2,1)S(1)}, bf16[256,256]{1,0:T(8,128)(2,1)S(1)}, u32[]{:S(2)}, u32[]{:S(2)}) collective-permute-start(bf16[256,256]{1,0:T(8,128)(2,1)S(1)} %get-tuple-element.14), channel_id=1, source_target_pairs={{0,2},{1,3},{2,0},{3,1},{4,6},{5,7},{6,4},{7,5},{8,10},{9,11},{10,... | collective-permute-start | bytes 393224 | tf_op jit(solution)/shard_map/ppermute | solution.py:352
  63.6 5.5 %copy-start.6 = (bf16[1,256,256]{2,1,0:T(8,128)(2,1)S(1)}, bf16[1,256,256]{2,1,0:T(8,128)(2,1)}, u32[]{:S(2)}) copy-start(bf16[1,256,256]{2,1,0:T(8,128)(2,1)} %get-tuple-element.11) | copy-start | bytes 393220
  67.1 2.1 %copy-start.7 = (bf16[256,256]{1,0:T(8,128)(2,1)}, bf16[256,256]{1,0:T(8,128)(2,1)S(1)}, u32[]{:S(2)}) copy-start(bf16[256,256]{1,0:T(8,128)(2,1)S(1)} %collective-permute-done.8) | copy-start | bytes 393220
  70.7 1.6 copy-start
  75.8 15.2 %copy-start.9 = (s32[1,512]{1,0:T(1,128)S(1)}, s32[1,512]{1,0:T(1,128)}, u32[]{:S(2)}) copy-start(s32[1,512]{1,0:T(1,128)} %param.11) | copy-start | bytes 6148
  79.5 63.3 %all-to-all-start.1 = ((bf16[128,64,128]{2,1,0:T(8,128)(2,1)}), bf16[128,64,128]{2,1,0:T(8,128)(2,1)}, u32[]{:S(2)}, u32[]{:S(2)}) async-start(bf16[128,64,128]{2,1,0:T(8,128)(2,1)} %pack.3), calls=%async_computation.1 | async-start | bytes 4194304 | tf_op jit(solution)/shard_map/all_to_all | solution.py:378
  93.3 19.1 %copy-start.3 = (bf16[512,256]{1,0:T(8,128)(2,1)}, bf16[512,256]{1,0:T(8,128)(2,1)S(1)}, u32[]{:S(2)}) copy-start(bf16[512,256]{1,0:T(8,128)(2,1)S(1)} %gather_fusion) | copy-start | bytes 786436
  93.3 8.8 %collective-permute-start.2 = (bf16[512,256]{1,0:T(8,128)(2,1)S(1)}, bf16[512,256]{1,0:T(8,128)(2,1)S(1)}, u32[]{:S(2)}, u32[]{:S(2)}) collective-permute-start(bf16[512,256]{1,0:T(8,128)(2,1)S(1)} %gather_fusion), channel_id=1, source_target_pairs={{0,3},{1,0},{2,1},{3,2},{4,7},{5,4},{6,5},{7,6},{8,11},{9,8},{10,9... | collective-permute-start | bytes 786440 | tf_op jit(solution)/shard_map/ppermute | solution.py:352
  95.3 10.2 %collective-permute-start.1 = (bf16[512,256]{1,0:T(8,128)(2,1)S(1)}, bf16[512,256]{1,0:T(8,128)(2,1)S(1)}, u32[]{:S(2)}, u32[]{:S(2)}) collective-permute-start(bf16[512,256]{1,0:T(8,128)(2,1)S(1)} %gather_fusion), channel_id=1, source_target_pairs={{0,2},{1,3},{2,0},{3,1},{4,6},{5,7},{6,4},{7,5},{8,10},{9,11},{10,... | collective-permute-start | bytes 786440 | tf_op jit(solution)/shard_map/ppermute | solution.py:352
  97.7 14.7 %collective-permute-start = (bf16[512,256]{1,0:T(8,128)(2,1)S(1)}, bf16[512,256]{1,0:T(8,128)(2,1)S(1)}, u32[]{:S(2)}, u32[]{:S(2)}) collective-permute-start(bf16[512,256]{1,0:T(8,128)(2,1)S(1)} %gather_fusion), channel_id=1, source_target_pairs={{0,1},{1,2},{2,3},{3,0},{4,5},{5,6},{6,7},{7,4},{8,9},{9,10},{10,1... | collective-permute-start | bytes 786440 | tf_op jit(solution)/shard_map/ppermute | solution.py:352
  102.2 10.3 %copy-start.11 = (bf16[512,256]{1,0:T(8,128)(2,1)}, bf16[512,256]{1,0:T(8,128)(2,1)S(1)}, u32[]{:S(2)}) copy-start(bf16[512,256]{1,0:T(8,128)(2,1)S(1)} %collective-permute-done.2.r3) | copy-start | bytes 786436
  105.5 7.0 %copy-start.12 = (bf16[512,256]{1,0:T(8,128)(2,1)}, bf16[512,256]{1,0:T(8,128)(2,1)S(1)}, u32[]{:S(2)}) copy-start(bf16[512,256]{1,0:T(8,128)(2,1)S(1)} %collective-permute-done.1.r2) | copy-start | bytes 786436
  120.3 1.0 copy-start.1
  148.8 16.8 %copy-start.2 = (bf16[4,512,256]{2,1,0:T(8,128)(2,1)S(1)}, bf16[4,512,256]{2,1,0:T(8,128)(2,1)}, u32[]{:S(2)}) copy-start(bf16[4,512,256]{2,1,0:T(8,128)(2,1)} %copy-done.1) | copy-start | bytes 3145732
  148.8 16.8 %copy-start.4 = (bf16[512,256]{1,0:T(8,128)(2,1)S(1)}, bf16[512,256]{1,0:T(8,128)(2,1)}, u32[]{:S(2)}) copy-start(bf16[512,256]{1,0:T(8,128)(2,1)} %copy-done.3) | copy-start | bytes 786436
  (1 other events, 0.7 us)

commit v4 on v3

--- a/solution.py
+++ b/solution.py
@@ -13,6 +13,7 @@
 MAXBLK = 128
 GROUP = 128
 CSLOT = 4
+PER = 32
 EPS = 1e-05
 VMEM = 28 * 1024 * 1024
 WHOLE = pl.BlockSpec(memory_space=pltpu.VMEM)
@@ -40,35 +41,15 @@
     return jnp.dot(pick, x, preferred_element_type=jnp.float32).astype(rows_in.dtype)
 
 
-def pack_kernel(home_in, table_in, cache, *refs):
-    out, home, table, held, made, cand, index_sem, load_sem, store_sem = refs[-9:]
-    indices = [
-        pltpu.make_async_copy(home_in, home, index_sem.at[0]),
-        pltpu.make_async_copy(table_in, table, index_sem.at[1]),
-    ]
-    parts = load_sem.shape[0]
-    size = cache.shape[0] // parts
-    blocks = []
-    for i in range(parts):
-        at = pl.ds(i * size, size)
-        blocks.append(pltpu.make_async_copy(cache.at[at], held.at[at], load_sem.at[i]))
-    for load in indices:
-        load.start()
-    shards, rows, _ = made.shape
-    if rows > 2 * BLK:
-        extra = pltpu.make_async_copy(refs[0], cand, index_sem.at[2])
-        extra.start()
-    for load in blocks:
-        load.start()
-    if rows > 2 * BLK:
-        extra.wait()
-        step = 32
-        for b in range(0, cand.shape[0], step):
-            x = spread_rows(cand[b : b + step, :])
-            n = step // CSLOT
-            made[b // CSLOT : b // CSLOT + n, 2 * BLK :, :] = x.reshape(n, rows - 2 * BLK, DH)
-    for load in indices + blocks:
-        load.wait()
+def copy_kernel_inputs(pairs, sems):
+    copies = [pltpu.make_async_copy(a, b, sems.at[i]) for i, (a, b) in enumerate(pairs)]
+    for copy in copies:
+        copy.start()
+    return copies
+
+
+def send_rows(home, table, made, out, store_sem, fill):
+    shards = made.shape[0]
     me = lax.axis_index("req")
     per = shards // store_sem.shape[0]
     stores = []
@@ -76,45 +57,109 @@
         chunk = pl.ds(c * per, per)
         for r in range(c * per, (c + 1) * per):
             behind = me - home[r]
-            block = held[table[r, jnp.where(behind < 0, behind + shards, behind)]]
-            made[r, :BLK, :] = block[:, :DH]
-            made[r, BLK : 2 * BLK, :] = block[:, DH:]
+            fill(r, table[r, jnp.where(behind < 0, behind + shards, behind)])
         stores.append(pltpu.make_async_copy(made.at[chunk], out.at[chunk], store_sem.at[c]))
         stores[-1].start()
     for store in stores:
         store.wait()
 
 
-def pack(home, table, cache, cand=None, after=()):
+def first_pack_kernel(
+    home_in, table_in, keys_in, values_in, cand_in, out, home, table, keys, values, cand, made, sem, store_sem
+):
+    head = BLK // 2
+    size = keys.shape[0] // 4
+    loads = copy_kernel_inputs(
+        [
+            (cand_in, cand),
+            (home_in, home),
+            (table_in, table),
+            (values_in.at[:, pl.ds(0, head), pl.ds(0, DH)], values),
+        ]
+        + [(keys_in.at[pl.ds(i * size, size)], keys.at[pl.ds(i * size, size)]) for i in range(4)],
+        sem,
+    )
+    loads[0].wait()
+    rows = made.shape[1]
+    first = 2 * BLK + head
+    step = 32
+    for b in range(0, cand.shape[0], step):
+        x = spread_rows(cand[b : b + step, :])
+        n = step // CSLOT
+        made[b // CSLOT : b // CSLOT + n, first:, :] = x.reshape(n, rows - first, DH)
+    for load in loads[1:]:
+        load.wait()
+
+    def fill(r, slot):
+        block = keys[slot]
+        made[r, :BLK, :] = block[:, :DH]
+        made[r, BLK : 2 * BLK, :] = block[:, DH:]
+        made[r, 2 * BLK : first, :] = values[slot]
+
+    send_rows(home, table, made, out, store_sem, fill)
+
+
+def first_pack(home, table, keys, values, cand):
     shards = home.shape[0]
-    rows = 2 * BLK
-    args = [hbm(home), hbm(table), hbm(cache)]
-    held_cand = (16, DH)
-    if cand is not None:
-        rows += cand.shape[0] * cand.shape[1] // (DH * shards)
-        args.append(hbm(cand))
-        held_cand = cand.shape
-    in_specs = [IN_HBM] * len(args) + [pl.BlockSpec(memory_space=pl.ANY)] * len(after)
+    rows = 2 * BLK + BLK // 2 + cand.shape[0] * cand.shape[1] // (DH * shards)
     out_shape = (shards, rows, DH)
     return pl.pallas_call(
-        pack_kernel,
-        out_shape=pltpu.HBM(out_shape, cache.dtype),
-        in_specs=in_specs,
+        first_pack_kernel,
+        out_shape=pltpu.HBM(out_shape, keys.dtype),
+        in_specs=[IN_HBM] * 5,
         out_specs=IN_HBM,
         scratch_shapes=[
             pltpu.SMEM(home.shape, jnp.int32),
             pltpu.SMEM(table.shape, jnp.int32),
-            pltpu.VMEM(cache.shape, cache.dtype),
-            pltpu.VMEM(out_shape, cache.dtype),
-            pltpu.VMEM(held_cand, cache.dtype),
+            pltpu.VMEM(keys.shape, keys.dtype),
+            pltpu.VMEM((values.shape[0], BLK // 2, DH), keys.dtype),
+            pltpu.VMEM(cand.shape, cand.dtype),
+            pltpu.VMEM(out_shape, keys.dtype),
+            pltpu.SemaphoreType.DMA((8,)),
+            pltpu.SemaphoreType.DMA((4,)),
+        ],
+        compiler_params=pltpu.CompilerParams(vmem_limit_bytes=VMEM),
+        cost_estimate=cost(0, 2 * shards * rows * DH * 2),
+        name="first_pack",
+    )(hbm(home), hbm(table), hbm(keys), hbm(values), hbm(cand))
+
+
+def second_pack_kernel(home_in, table_in, values_in, *refs):
+    out, home, table, values, made, sem, store_sem = refs[-7:]
+    for load in copy_kernel_inputs(
+        [(home_in, home), (table_in, table), (values_in, values)], sem
+    ):
+        load.wait()
+    head = BLK // 2
+
+    def fill(r, slot):
+        block = values[slot]
+        made[r, :head, :] = block[head:, :DH]
+        made[r, head:, :] = block[:, DH:]
+
+    send_rows(home, table, made, out, store_sem, fill)
+
+
+def second_pack(home, table, values, after):
+    shards = home.shape[0]
+    out_shape = (shards, BLK + BLK // 2, DH)
+    return pl.pallas_call(
+        second_pack_kernel,
+        out_shape=pltpu.HBM(out_shape, values.dtype),
+        in_specs=[IN_HBM] * 3 + [pl.BlockSpec(memory_space=pl.ANY)] * len(after),
+        out_specs=IN_HBM,
+        scratch_shapes=[
+            pltpu.SMEM(home.shape, jnp.int32),
+            pltpu.SMEM(table.shape, jnp.int32),
+            pltpu.VMEM(values.shape, values.dtype),
+            pltpu.VMEM(out_shape, values.dtype),
             pltpu.SemaphoreType.DMA((3,)),
             pltpu.SemaphoreType.DMA((4,)),
-            pltpu.SemaphoreType.DMA((4,)),
         ],
         compiler_params=pltpu.CompilerParams(vmem_limit_bytes=VMEM),
-        cost_estimate=cost(0, 2 * shards * rows * DH * 2),
-        name="pack",
-    )(*args, *after)
+        cost_estimate=cost(0, 2 * shards * out_shape[1] * DH * 2),
+        name="second_pack",
+    )(hbm(home), hbm(table), hbm(values), *after)
 
 
 def silu(half):
@@ -184,74 +229,99 @@
     )(*[hbm(r) for r in rows], hbm(w), *[hbm(g) for g in gate_w])
 
 
-def weights_kernel(query, keys, mask, out):
-    sources = keys.shape[0]
-    n = sources * BLK
+def head_weights(query, keys, mask):
+    s = lax.dot_general(query, keys, (((1,), (1,)), ((), ())), preferred_element_type=jnp.float32)
+    return silu(s * mask).astype(jnp.bfloat16)
+
+
+def half_rows(blocks, i):
+    half = BLK // 2
+    part = blocks[:, i * half : (i + 1) * half, :]
+    return part.reshape(part.shape[0] * half, DH)
+
+
+def weights_kernel(query, got, mask, own, out, base, early):
+    n = PER * BLK // 2
+
+    @pl.when(pl.program_id(0) == 0)
+    def _():
+        base[...] = own[...]
+
     for h in range(query.shape[1] // DH):
-        k = keys[:, h * BLK : (h + 1) * BLK, :].reshape(n, DH)
+        a, b = half_rows(got, 2 * h), half_rows(got, 2 * h + 1)
         for g in range(query.shape[0] // GROUP):
             rows = slice(g * GROUP, (g + 1) * GROUP)
-            s = lax.dot_general(
-                query[rows, h * DH : (h + 1) * DH],
-                k,
-                (((1,), (1,)), ((), ())),
-                preferred_element_type=jnp.float32,
-            )
-            out[0, h, rows, :] = silu(s * mask[g : g + 1, :]).astype(jnp.bfloat16)
-
-
-def attention_weights(query, got, mask):
-    shards = got.shape[0]
+            q = query[rows, h * DH : (h + 1) * DH]
+            at = mask[g : g + 1, :]
+            w_a, w_b = head_weights(q, a, at[:, :n]), head_weights(q, b, at[:, n:])
+            if h == 0:
+                early[rows, :] = w_a
+                out[0, rows, :n] = w_b
+            else:
+                out[0, rows, n : 2 * n] = w_a
+                out[0, rows, 2 * n :] = w_b
+    base[:, :DH] += jnp.dot(early[...], half_rows(got, 4), preferred_element_type=jnp.float32)
+
+
+def attention_weights(query, got, mask, own):
+    steps = got.shape[0] // PER
     cands, width = query.shape
-    heads = width // DH
-    per = 16
+    n = PER * BLK
+    whole = lambda a: pl.BlockSpec(a.shape, lambda i: (0, 0))
     return pl.pallas_call(
         weights_kernel,
-        out_shape=pltpu.HBM((shards // per, heads, cands, per * BLK), jnp.bfloat16),
-        grid=(shards // per,),
+        out_shape=(
+            pltpu.HBM((steps, cands, 3 * n // 2), jnp.bfloat16),
+            pltpu.HBM((cands, width), jnp.float32),
+        ),
+        grid=(steps,),
         in_specs=[
-            pl.BlockSpec((cands, width), lambda i: (0, 0)),
-            pl.BlockSpec((per, 2 * BLK, DH), lambda i: (i, 0, 0)),
-            pl.BlockSpec((mask.shape[0], per * BLK), lambda i: (0, i)),
+            whole(query),
+            pl.BlockSpec((PER, 2 * BLK + BLK // 2, DH), lambda i: (i, 0, 0)),
+            pl.BlockSpec((mask.shape[0], n), lambda i: (0, i)),
+            whole(own),
         ],
-        out_specs=pl.BlockSpec((1, heads, cands, per * BLK), lambda i: (i, 0, 0, 0)),
+        out_specs=(pl.BlockSpec((1, cands, 3 * n // 2), lambda i: (i, 0, 0)), whole(own)),
+        scratch_shapes=[pltpu.VMEM((cands, n // 2), jnp.bfloat16)],
         compiler_params=pltpu.CompilerParams(vmem_limit_bytes=VMEM),
         cost_estimate=cost(
-            2 * cands * shards * BLK * width, 12 << 20, heads * cands * shards * BLK
+            2 * cands * steps * n * width, 12 << 20, steps * cands * n * width // DH
         ),
         name="weights",
-    )(query, got, mask)
-
-
-def values_kernel(weights, values, own, out, w, v, held, total, w_sem, v_sem, own_sem):
-    steps, heads, cands, n = weights.shape
-    per = n // BLK
-    copies = out.shape[0]
+    )(query, got, mask, own)
+
+
+def values_kernel(weights, values, base, out, w, v, held, total, w_sem, v_sem, base_sem):
+    steps, cands, count = weights.shape
+    n = count // 3
     loads = []
     for c in range(steps):
-        chunk = pl.ds(c * per, per)
+        chunk = pl.ds(c * PER, PER)
         loads.append(
-            [pltpu.make_async_copy(values.at[chunk], v.at[chunk], v_sem.at[c])]
-            + [
-                pltpu.make_async_copy(weights.at[c, h], w.at[c, h], w_sem.at[c, h])
-                for h in range(heads)
-            ]
+            (
+                pltpu.make_async_copy(values.at[chunk], v.at[chunk], v_sem.at[c]),
+                pltpu.make_async_copy(weights.at[pl.ds(c, 1)], w.at[pl.ds(c, 1)], w_sem.at[c]),
+            )
         )
         for load in loads[-1]:
             load.start()
-    last = pltpu.make_async_copy(own, held, own_sem)
+    last = pltpu.make_async_copy(base, held, base_sem)
     last.start()
     for c in range(steps):
         for load in loads[c]:
             load.wait()
         if c == steps - 1:
             last.wait()
-        for h in range(heads):
+        blocks = v[c * PER : (c + 1) * PER]
+        for h, pieces in enumerate(((0,), (1, 2))):
             cols = slice(h * DH, (h + 1) * DH)
-            part = jnp.dot(
-                w[c, h],
-                v[c * per : (c + 1) * per, h * BLK : (h + 1) * BLK, :].reshape(n, DH),
-                preferred_element_type=jnp.float32,
+            part = sum(
+                jnp.dot(
+                    w[c, :, i * n : (i + 1) * n],
+                    half_rows(blocks, i),
+                    preferred_element_type=jnp.float32,
+                )
+                for i in pieces
             )
             if c == 0:
                 total[:, cols] = part
@@ -259,32 +329,31 @@
                 total[:, cols] += part
             else:
                 done = (total[:, cols] + part + held[:, cols]).astype(jnp.bfloat16)
-                for i in range(copies):
+                for i in range(out.shape[0]):
                     out[i, :, cols] = done
 
 
-def weighted_values(weights, got, own, copies):
-    shards = got.shape[0]
-    steps, heads, cands, _ = weights.shape
-    width = own.shape[1]
+def weighted_values(weights, got, base, copies):
+    steps = weights.shape[0]
+    cands, width = base.shape
     return pl.pallas_call(
         values_kernel,
         out_shape=jax.ShapeDtypeStruct((copies, cands, width), jnp.bfloat16),
-        in_specs=[IN_HBM, IN_HBM, IN_HBM],
+        in_specs=[IN_HBM] * 3,
         out_specs=WHOLE,
         scratch_shapes=[
             pltpu.VMEM(weights.shape, weights.dtype),
             pltpu.VMEM(got.shape, got.dtype),
-            pltpu.VMEM(own.shape, own.dtype),
+            pltpu.VMEM(base.shape, base.dtype),
             pltpu.VMEM((cands, width), jnp.float32),
-            pltpu.SemaphoreType.DMA((steps, heads)),
+            pltpu.SemaphoreType.DMA((steps,)),
             pltpu.SemaphoreType.DMA((steps,)),
             pltpu.SemaphoreType.DMA,
         ],
         compiler_params=pltpu.CompilerParams(vmem_limit_bytes=VMEM),
-        cost_estimate=cost(2 * cands * shards * BLK * width, 12 << 20),
+        cost_estimate=cost(2 * weights.size * DH, 12 << 20),
         name="values",
-    )(hbm(weights), hbm(got), hbm(own))
+    )(hbm(weights), hbm(got), hbm(base))
 
 
 def finish_kernel(attn, gates, w, rows, out, made, sems):
@@ -354,7 +423,7 @@
     exchange = functools.partial(
         lax.all_to_all, axis_name="req", split_axis=0, concat_axis=0, tiled=True
     )
-    got_keys = exchange(pack(hist_home, hist_slot, cache_k, cand=cand_feats))
+    got_first = exchange(first_pack(hist_home, hist_slot, cache_k, cache_v, cand_feats))
 
     w_gate = w_in[:, 0, :]
     gate_w = [back(w_gate, d) for d in range(1, split)]
@@ -366,19 +435,21 @@
     own_out = jnp.take(jnp.stack(own_out), backs, axis=0, mode="clip")
     own_out = own_out.reshape(split * columns, columns)
 
+    chunks, half = shards // PER, BLK // 2
     home = hist_home[me]
     order = (jnp.arange(shards, dtype=jnp.int32) - home) % shards
     seen = jnp.take(hist_mask[0], order, axis=1, mode="clip").astype(jnp.float32)
-    inside = order[:, None] * BLK + jnp.arange(BLK, dtype=jnp.int32)[None, :] < hist_len[0]
-    mask = seen[:, :, None] * jnp.where(inside, 0.5 * DH**-0.5, 0.0)[None]
+    place = jnp.arange(BLK, dtype=jnp.int32).reshape(2, 1, half)
+    inside = order.reshape(chunks, 1, PER, 1) * BLK + place < hist_len[0]
+    mask = seen.reshape(-1, chunks, 1, PER, 1) * jnp.where(inside, 0.5 * DH**-0.5, 0.0)[None]
     mask = mask.reshape(hist_mask.shape[1], shards * BLK)
 
     w_flat = w_in.reshape(w_in.shape[0], 4 * width)
     ready = [*gate_w, own_out, mask, w_flat]
-    got_values = exchange(pack(hist_home, hist_slot, cache_v, after=ready))
+    got_second = exchange(second_pack(hist_home, hist_slot, cache_v, ready))
 
     arrived = (
-        got_keys[:, 2 * BLK :, :]
+        got_first[:, 2 * BLK + half :, :]
         .reshape(shards, halves, cand_slot, DH)
         .transpose(0, 2, 1, 3)
         .reshape(cands, columns)
@@ -387,8 +458,8 @@
     rows = [own_rows] + [back(own_rows, d) for d in range(1, split)]
     gates, query, own = project(rows, w_flat, gate_w)
 
-    weights = attention_weights(query, got_keys, mask)
-    attn = weighted_values(weights, got_values, own, split)
+    weights, base = attention_weights(query, got_first, mask, own)
+    attn = weighted_values(weights, got_second, base, split)
     attn = lax.all_to_all(attn, "mp", split_axis=0, concat_axis=0, tiled=True)
     return finish(attn, gates, own_out, own_rows)
 

time: 168 us -> 165 us (0.982)
  local copies, waits for them, and re-layouts: 15.5 us -> 13.1 us
  Pallas kernels: 28.4 us -> 26.4 us
  waiting for transfers between devices: 47.8 us -> 45.9 us
    all_to_all x2, waiting for transfers between devices: 18.6 us -> 15.1 us  [the longest x1 15 us: local(): exchange(first_pack(hist_home, hist_slot, cache_k, cache_v, cand_feats))]
    unnamed x32 -> x34, local copies, waits for them, and re-layouts: 7.86 us -> 4.96 us
    ppermute x9, starting transfers between devices: 25.6 us -> 27.7 us  [back(): return lax.ppermute(x, 'mp', [(i, (i + d) % split) for i in range(split)])]
    pallas_call x1, Pallas kernels: 5.95 us -> 4.02 us  [weighted_values(): pl.pallas_call(values_kernel, out_shape=jax.ShapeDtypeStruct((copies, can...]
where the time goes in v4:
time: 165 us; the launch traced here: 164 us
  starting transfers between devices  56.3 us (34%)
  waiting for transfers between devices  45.9 us (28%)
  Pallas kernels  26.4 us (16%)
  blocking collectives  17.4 us (11%)
  local copies, waits for them, and re-layouts  13.1 us (8%)
  other arithmetic  3.31 us (2%)
    ppermute x9, waiting for transfers between devices, back(): return lax.ppermute(x, 'mp', [(i, (i + d) % split) for i in range(split)])  30.8 us
    ppermute x9, starting transfers between devices, back(): return lax.ppermute(x, 'mp', [(i, (i + d) % split) for i in range(split)])  27.7 us
    all_to_all x1, starting transfers between devices, local(): exchange(first_pack(hist_home, hist_slot, cache_k, cache_v, cand_feats))  19 us
    all_to_all x1, blocking collectives, local(): attn = lax.all_to_all(attn, 'mp', split_axis=0, concat_axis=0, tiled=True)  17.4 us
    all_to_all x1, waiting for transfers between devices, local(): exchange(first_pack(hist_home, hist_slot, cache_k, cache_v, cand_feats))  15 us
    all_to_all x1, starting transfers between devices, local(): got_second = exchange(second_pack(hist_home, hist_slot, cache_v, ready))  9.63 us
    pallas_call x1, Pallas kernels, project(): pl.pallas_call(project_kernel, out_shape=(jax.ShapeDtypeStruct((split, ca...  7.09 us
    pallas_call x1, Pallas kernels, attention_weights(): pl.pallas_call(weights_kernel, out_shape=(pltpu.HBM((steps, cands, 3 * n...  6.9 us
  transfers between devices with their start and end apart: 11, of which 7 were waited for; matrix products, arithmetic and copies ran while one was open for 9% of the time, Pallas kernels for 10%

profile of v4, /device:TPU:1, one launch (start us, length us, event | category | flops | bytes accessed | tf_op | source)
XLA Modules:
  0.0 163.7 jit_solution(14710443703700081167)
XLA Ops:
  0.0 3.7 %first_pack.1 = bf16[128,88,128]{2,1,0:T(8,128)(2,1)} custom-call(s32[128]{0:T(128)} %home_in.3, s32[128,128]{1,0:T(8,128)} %table_in.3, bf16[32,32,256]{2,1,0:T(8,128)(2,1)} %keys_in.1, bf16[32,32,256]{2,1,0:T(8,128)(2,1)} %values_in.3, bf16[512,256]{1,0:T(8,128)(2,1)} %cand_in.1), custom_call_target="tpu_custom_call" | custom-call | bytes 5767168 | tf_op jit(solution)/shard_map/first_pack/pallas_call | solution.py:106
  3.7 19.0 %all-to-all-start = ((bf16[128,88,128]{2,1,0:T(8,128)(2,1)}), bf16[128,88,128]{2,1,0:T(8,128)(2,1)}, u32[]{:S(2)}, u32[]{:S(2)}) async-start(bf16[128,88,128]{2,1,0:T(8,128)(2,1)} %first_pack.1), calls=%async_computation | async-start | bytes 5767168 | tf_op jit(solution)/shard_map/all_to_all | solution.py:426
  24.4 4.4 %collective-permute-start.5 = (bf16[1024,256]{1,0:T(8,128)(2,1)}, bf16[1024,256]{1,0:T(8,128)(2,1)S(1)}, u32[]{:S(2)}, u32[]{:S(2)}) collective-permute-start(bf16[1024,256]{1,0:T(8,128)(2,1)} %bitcast.32), channel_id=1, source_target_pairs={{0,3},{1,0},{2,1},{3,2},{4,7},{5,4},{6,5},{7,6},{8,11},{9,8},{10,9... | collective-permute-start | bytes 1572872 | tf_op jit(solution)/shard_map/ppermute | solution.py:421
  28.7 2.4 %collective-permute-start.4 = (bf16[1024,256]{1,0:T(8,128)(2,1)}, bf16[1024,256]{1,0:T(8,128)(2,1)}, u32[]{:S(2)}, u32[]{:S(2)}) collective-permute-start(bf16[1024,256]{1,0:T(8,128)(2,1)} %bitcast.32), channel_id=1, source_target_pairs={{0,2},{1,3},{2,0},{3,1},{4,6},{5,7},{6,4},{7,5},{8,10},{9,11},{10,... | collective-permute-start | bytes 1572872 | tf_op jit(solution)/shard_map/ppermute | solution.py:421
  31.2 2.5 %collective-permute-start.3 = (bf16[1024,256]{1,0:T(8,128)(2,1)}, bf16[1024,256]{1,0:T(8,128)(2,1)}, u32[]{:S(2)}, u32[]{:S(2)}) collective-permute-start(bf16[1024,256]{1,0:T(8,128)(2,1)} %bitcast.32), channel_id=1, source_target_pairs={{0,1},{1,2},{2,3},{3,0},{4,5},{5,6},{6,7},{7,4},{8,9},{9,10},{10,1... | collective-permute-start | bytes 1572872 | tf_op jit(solution)/shard_map/ppermute | solution.py:421
  34.5 3.4 %collective-permute-start.6 = (bf16[256,256]{1,0:T(8,128)(2,1)S(1)}, bf16[256,256]{1,0:T(8,128)(2,1)S(1)}, u32[]{:S(2)}, u32[]{:S(2)}) collective-permute-start(bf16[256,256]{1,0:T(8,128)(2,1)S(1)} %get-tuple-element.16), channel_id=1, source_target_pairs={{0,1},{1,2},{2,3},{3,0},{4,5},{5,6},{6,7},{7,4},{8,9},{9,10},{10,1... | collective-permute-start | bytes 393224 | tf_op jit(solution)/shard_map/ppermute | solution.py:421
  37.9 3.1 %collective-permute-start.8 = (bf16[256,256]{1,0:T(8,128)(2,1)}, bf16[256,256]{1,0:T(8,128)(2,1)}, u32[]{:S(2)}, u32[]{:S(2)}) collective-permute-start(bf16[256,256]{1,0:T(8,128)(2,1)} %get-tuple-element.17), channel_id=1, source_target_pairs={{0,3},{1,0},{2,1},{3,2},{4,7},{5,4},{6,5},{7,6},{8,11},{9,8},{10,9... | collective-permute-start | bytes 393224 | tf_op jit(solution)/shard_map/ppermute | solution.py:421
  45.3 15.1 %collective-permute-done.6 = bf16[256,256]{1,0:T(8,128)(2,1)S(1)} collective-permute-done((bf16[256,256]{1,0:T(8,128)(2,1)S(1)}, bf16[256,256]{1,0:T(8,128)(2,1)S(1)}, u32[]{:S(2)}, u32[]{:S(2)}) %collective-permute-start.6) | collective-permute-done | bytes 131104 | tf_op jit(solution)/shard_map/ppermute | solution.py:421
  60.3 2.4 %collective-permute-start.7 = (bf16[256,256]{1,0:T(8,128)(2,1)S(1)}, bf16[256,256]{1,0:T(8,128)(2,1)S(1)}, u32[]{:S(2)}, u32[]{:S(2)}) collective-permute-start(bf16[256,256]{1,0:T(8,128)(2,1)S(1)} %get-tuple-element.18), channel_id=1, source_target_pairs={{0,2},{1,3},{2,0},{3,1},{4,6},{5,7},{6,4},{7,5},{8,10},{9,11},{10,... | collective-permute-start | bytes 393224 | tf_op jit(solution)/shard_map/ppermute | solution.py:421
  62.8 2.1 %copy.21 = bf16[128,8,4,256]{3,1,2,0:T(8,128)(2,1)S(1)} copy(bf16[128,8,4,256]{3,2,1,0:T(4,128)(2,1)} %bitcast.40) | data formatting | bytes 4194304
  65.0 3.6 %collective-permute-done.7 = bf16[256,256]{1,0:T(8,128)(2,1)S(1)} collective-permute-done((bf16[256,256]{1,0:T(8,128)(2,1)S(1)}, bf16[256,256]{1,0:T(8,128)(2,1)S(1)}, u32[]{:S(2)}, u32[]{:S(2)}) %collective-permute-start.7) | collective-permute-done | bytes 131104 | tf_op jit(solution)/shard_map/ppermute | solution.py:421
  72.0 3.1 %second_pack.1 = bf16[128,48,128]{2,1,0:T(8,128)(2,1)} custom-call(s32[128]{0:T(128)} %home_in.3, s32[128,128]{1,0:T(8,128)} %table_in.3, bf16[32,32,256]{2,1,0:T(8,128)(2,1)} %values_in.3, bf16[1024,256]{1,0:T(8,128)(2,1)} %collective-permute-done.3.g1.refs_0_, bf16[1024,256]{1,0:T(8,128)(2,1)} %collective-permute-done.4.g2.refs_1_, ...), custom_call_target="tpu_custom_call" | custom-call | bytes 3145728 | tf_op jit(solution)/shard_map/second_pack/pallas_call | solution.py:146
  75.1 15.0 %all-to-all-done.got = bf16[128,88,128]{2,1,0:T(8,128)(2,1)} async-done(((bf16[128,88,128]{2,1,0:T(8,128)(2,1)}), bf16[128,88,128]{2,1,0:T(8,128)(2,1)}, u32[]{:S(2)}, u32[]{:S(2)}) %all-to-all-start) | async-done | bytes 2883616 | tf_op jit(solution)/shard_map/all_to_all | solution.py:426
  90.1 9.6 %all-to-all-start.1 = ((bf16[128,48,128]{2,1,0:T(8,128)(2,1)}), bf16[128,48,128]{2,1,0:T(8,128)(2,1)}, u32[]{:S(2)}, u32[]{:S(2)}) async-start(bf16[128,48,128]{2,1,0:T(8,128)(2,1)} %second_pack.1), calls=%async_computation.1 | async-start | bytes 3145728 | tf_op jit(solution)/shard_map/all_to_all | solution.py:449
  101.0 2.0 %gather_fusion = bf16[512,256]{1,0:T(8,128)(2,1)S(1)} fusion(bf16[512,256]{1,0:T(8,128)(2,1)S(1)} %bitcast.39, s32[1024]{0:T(1024)S(1)} %pad_clamp_fusion.2), kind=kCustom, calls=%fused_computation | custom fusion | bytes 526336 | tf_op jit(solution)/shard_map/jit(_take)/gather | solution.py:457
  102.9 4.4 %collective-permute-start.2 = (bf16[512,256]{1,0:T(8,128)(2,1)S(1)}, bf16[512,256]{1,0:T(8,128)(2,1)S(1)}, u32[]{:S(2)}, u32[]{:S(2)}) collective-permute-start(bf16[512,256]{1,0:T(8,128)(2,1)S(1)} %gather_fusion), channel_id=1, source_target_pairs={{0,3},{1,0},{2,1},{3,2},{4,7},{5,4},{6,5},{7,6},{8,11},{9,8},{10,9... | collective-permute-start | bytes 786440 | tf_op jit(solution)/shard_map/ppermute | solution.py:421
  107.3 2.4 %collective-permute-start.1 = (bf16[512,256]{1,0:T(8,128)(2,1)S(1)}, bf16[512,256]{1,0:T(8,128)(2,1)S(1)}, u32[]{:S(2)}, u32[]{:S(2)}) collective-permute-start(bf16[512,256]{1,0:T(8,128)(2,1)S(1)} %gather_fusion), channel_id=1, source_target_pairs={{0,2},{1,3},{2,0},{3,1},{4,6},{5,7},{6,4},{7,5},{8,10},{9,11},{10,... | collective-permute-start | bytes 786440 | tf_op jit(solution)/shard_map/ppermute | solution.py:421
  109.8 2.7 %collective-permute-start = (bf16[512,256]{1,0:T(8,128)(2,1)S(1)}, bf16[512,256]{1,0:T(8,128)(2,1)S(1)}, u32[]{:S(2)}, u32[]{:S(2)}) collective-permute-start(bf16[512,256]{1,0:T(8,128)(2,1)S(1)} %gather_fusion), channel_id=1, source_target_pairs={{0,1},{1,2},{2,3},{3,0},{4,5},{5,6},{6,7},{7,4},{8,9},{9,10},{10,1... | collective-permute-start | bytes 786440 | tf_op jit(solution)/shard_map/ppermute | solution.py:421
  112.8 4.7 %collective-permute-done.1.r2 = bf16[512,256]{1,0:T(8,128)(2,1)S(1)} collective-permute-done((bf16[512,256]{1,0:T(8,128)(2,1)S(1)}, bf16[512,256]{1,0:T(8,128)(2,1)S(1)}, u32[]{:S(2)}, u32[]{:S(2)}) %collective-permute-start.1) | collective-permute-done | bytes 262176 | tf_op jit(solution)/shard_map/ppermute | solution.py:421
  117.4 7.2 %collective-permute-done.r1 = bf16[512,256]{1,0:T(8,128)(2,1)S(1)} collective-permute-done((bf16[512,256]{1,0:T(8,128)(2,1)S(1)}, bf16[512,256]{1,0:T(8,128)(2,1)S(1)}, u32[]{:S(2)}, u32[]{:S(2)}) %collective-permute-start) | collective-permute-done | bytes 262176 | tf_op jit(solution)/shard_map/ppermute | solution.py:421
  125.3 7.1 %project.1 = (bf16[4,512,256]{2,1,0:T(8,128)(2,1)S(1)}, bf16[512,256]{1,0:T(8,128)(2,1)S(1)}, f32[512,256]{1,0:T(8,128)}) custom-call(bf16[512,256]{1,0:T(8,128)(2,1)} %copy-done.1, bf16[512,256]{1,0:T(8,128)(2,1)} %copy-done.14, bf16[512,256]{1,0:T(8,128)(2,1)} %copy-done.13, bf16[512,256]{1,0:T(8,128)(2,1)} %copy-done.12, bf16[1024,1024]{1,0:T(8,128)(2,1)} %bitcast.36, ...), custom_call_target="tpu_custom_call" | custom-call | flops 1879048192 | bytes 8388608 | tf_op jit(solution)/shard_map/project/pallas_call | solution.py:211
  133.5 6.9 %weights.1 = (bf16[4,512,1536]{2,1,0:T(8,128)(2,1)}, f32[512,256]{1,0:T(8,128)}) custom-call(bf16[512,256]{1,0:T(8,128)(2,1)S(1)} %get-tuple-element.10.query, bf16[128,88,128]{2,1,0:T(8,128)(2,1)} %all-to-all-done.got, f32[4,4096]{1,0:T(4,128)S(1)} %broadcast_multiply_fusion.mask.refs_4_, f32[512,256]{1,0:T(8,128)S(1)} %copy-done.4), custom_call_target="tpu_custom_call" | custom-call | flops 1073741824 | bytes 12582912 | tf_op jit(solution)/shard_map/weights/pallas_call | solution.py:271
  140.5 4.0 %values.1 = bf16[4,512,256]{2,1,0:T(8,128)(2,1)S(1)} custom-call(bf16[4,512,1536]{2,1,0:T(8,128)(2,1)} %get-tuple-element.12.weights, bf16[128,48,128]{2,1,0:T(8,128)(2,1)} %all-to-all-done.1.values, f32[512,256]{1,0:T(8,128)} %get-tuple-element.13.base), custom_call_target="tpu_custom_call" | custom-call | flops 805306368 | bytes 12582912 | tf_op jit(solution)/shard_map/values/pallas_call | solution.py:339
  144.6 17.4 %all_to_all.15.attn = bf16[4,512,256]{2,1,0:T(8,128)(2,1)S(1)} all-to-all(bf16[4,512,256]{2,1,0:T(8,128)(2,1)S(1)} %values.1), channel_id=1, replica_groups=mesh['req'=128,'mp'=4] {'mp'}, dimensions={0} | all-to-all | bytes 2097152 | tf_op jit(solution)/shard_map/all_to_all | solution.py:463
  (62 shorter events, 14.4 us)
Async XLA Ops:
  3.7 19.0 %copy-start.5 = (bf16[1024,4,256]{2,1,0:T(4,128)(2,1)S(1)}, bf16[1024,4,256]{2,1,0:T(4,128)(2,1)}, u32[]{:S(2)}) copy-start(bf16[1024,4,256]{2,1,0:T(4,128)(2,1)} %param.12) | copy-start | bytes 6291460
  3.7 86.4 %all-to-all-start = ((bf16[128,88,128]{2,1,0:T(8,128)(2,1)}), bf16[128,88,128]{2,1,0:T(8,128)(2,1)}, u32[]{:S(2)}, u32[]{:S(2)}) async-start(bf16[128,88,128]{2,1,0:T(8,128)(2,1)} %first_pack.1), calls=%async_computation | async-start | bytes 5767168 | tf_op jit(solution)/shard_map/all_to_all | solution.py:426
  22.7 11.1 %copy-start.6 = (bf16[256,1024]{1,0:T(8,128)(2,1)S(1)}, bf16[256,1024]{1,0:T(8,128)(2,1)}, u32[]{:S(2)}) copy-start(bf16[256,1024]{1,0:T(8,128)(2,1)} %param.13) | copy-start | bytes 1572868
  22.7 18.9 %copy-start.9 = (s32[128]{0:T(128)S(1)}, s32[128]{0:T(128)}, u32[]{:S(2)}) copy-start(s32[128]{0:T(128)} %home_in.3) | copy-start | bytes 1540
  22.7 19.6 %copy-start.10 = (s32[1,4,128]{2,1,0:T(4,128)S(1)}, s32[1,4,128]{2,1,0:T(4,128)}, u32[]{:S(2)}) copy-start(s32[1,4,128]{2,1,0:T(4,128)} %param.19) | copy-start | bytes 6148
  24.4 47.6 %collective-permute-start.5 = (bf16[1024,256]{1,0:T(8,128)(2,1)}, bf16[1024,256]{1,0:T(8,128)(2,1)S(1)}, u32[]{:S(2)}, u32[]{:S(2)}) collective-permute-start(bf16[1024,256]{1,0:T(8,128)(2,1)} %bitcast.32), channel_id=1, source_target_pairs={{0,3},{1,0},{2,1},{3,2},{4,7},{5,4},{6,5},{7,6},{8,11},{9,8},{10,9... | collective-permute-start | bytes 1572872 | tf_op jit(solution)/shard_map/ppermute | solution.py:421
  28.7 43.2 %collective-permute-start.4 = (bf16[1024,256]{1,0:T(8,128)(2,1)}, bf16[1024,256]{1,0:T(8,128)(2,1)}, u32[]{:S(2)}, u32[]{:S(2)}) collective-permute-start(bf16[1024,256]{1,0:T(8,128)(2,1)} %bitcast.32), channel_id=1, source_target_pairs={{0,2},{1,3},{2,0},{3,1},{4,6},{5,7},{6,4},{7,5},{8,10},{9,11},{10,... | collective-permute-start | bytes 1572872 | tf_op jit(solution)/shard_map/ppermute | solution.py:421
  31.2 40.8 %collective-permute-start.3 = (bf16[1024,256]{1,0:T(8,128)(2,1)}, bf16[1024,256]{1,0:T(8,128)(2,1)}, u32[]{:S(2)}, u32[]{:S(2)}) collective-permute-start(bf16[1024,256]{1,0:T(8,128)(2,1)} %bitcast.32), channel_id=1, source_target_pairs={{0,1},{1,2},{2,3},{3,0},{4,5},{5,6},{6,7},{7,4},{8,9},{9,10},{10,1... | collective-permute-start | bytes 1572872 | tf_op jit(solution)/shard_map/ppermute | solution.py:421
  34.5 25.8 %collective-permute-start.6 = (bf16[256,256]{1,0:T(8,128)(2,1)S(1)}, bf16[256,256]{1,0:T(8,128)(2,1)S(1)}, u32[]{:S(2)}, u32[]{:S(2)}) collective-permute-start(bf16[256,256]{1,0:T(8,128)(2,1)S(1)} %get-tuple-element.16), channel_id=1, source_target_pairs={{0,1},{1,2},{2,3},{3,0},{4,5},{5,6},{6,7},{7,4},{8,9},{9,10},{10,1... | collective-permute-start | bytes 393224 | tf_op jit(solution)/shard_map/ppermute | solution.py:421
  37.9 27.0 %collective-permute-start.8 = (bf16[256,256]{1,0:T(8,128)(2,1)}, bf16[256,256]{1,0:T(8,128)(2,1)}, u32[]{:S(2)}, u32[]{:S(2)}) collective-permute-start(bf16[256,256]{1,0:T(8,128)(2,1)} %get-tuple-element.17), channel_id=1, source_target_pairs={{0,3},{1,0},{2,1},{3,2},{4,7},{5,4},{6,5},{7,6},{8,11},{9,8},{10,9... | collective-permute-start | bytes 393224 | tf_op jit(solution)/shard_map/ppermute | solution.py:421
  60.3 2.4 %copy-start.7 = (bf16[256,256]{1,0:T(8,128)(2,1)}, bf16[256,256]{1,0:T(8,128)(2,1)S(1)}, u32[]{:S(2)}) copy-start(bf16[256,256]{1,0:T(8,128)(2,1)S(1)} %collective-permute-done.6) | copy-start | bytes 393220
  60.3 8.2 %collective-permute-start.7 = (bf16[256,256]{1,0:T(8,128)(2,1)S(1)}, bf16[256,256]{1,0:T(8,128)(2,1)S(1)}, u32[]{:S(2)}, u32[]{:S(2)}) collective-permute-start(bf16[256,256]{1,0:T(8,128)(2,1)S(1)} %get-tuple-element.18), channel_id=1, source_target_pairs={{0,2},{1,3},{2,0},{3,1},{4,6},{5,7},{6,4},{7,5},{8,10},{9,11},{10,... | collective-permute-start | bytes 393224 | tf_op jit(solution)/shard_map/ppermute | solution.py:421
  62.8 5.7 %copy-start.8 = (bf16[256,256]{1,0:T(8,128)(2,1)S(1)}, bf16[256,256]{1,0:T(8,128)(2,1)}, u32[]{:S(2)}) copy-start(bf16[256,256]{1,0:T(8,128)(2,1)} %copy-done.7) | copy-start | bytes 393220
  64.9 10.1 %copy-start = (bf16[128,8,4,256]{3,1,2,0:T(8,128)(2,1)}, bf16[128,8,4,256]{3,1,2,0:T(8,128)(2,1)S(1)}, u32[]{:S(2)}) copy-start(bf16[128,8,4,256]{3,1,2,0:T(8,128)(2,1)S(1)} %copy.21) | copy-start | bytes 6291460
  71.9 3.1 %copy-start.3 = (bf16[1024,256]{1,0:T(8,128)(2,1)}, bf16[1024,256]{1,0:T(8,128)(2,1)S(1)}, u32[]{:S(2)}) copy-start(bf16[1024,256]{1,0:T(8,128)(2,1)S(1)} %collective-permute-done.5.g3.refs_2_) | copy-start | bytes 1572868
  75.1 24.6 %copy-start.11 = (s32[1,512]{1,0:T(1,128)S(1)}, s32[1,512]{1,0:T(1,128)}, u32[]{:S(2)}) copy-start(s32[1,512]{1,0:T(1,128)} %param.11) | copy-start | bytes 6148
  90.1 50.4 %all-to-all-start.1 = ((bf16[128,48,128]{2,1,0:T(8,128)(2,1)}), bf16[128,48,128]{2,1,0:T(8,128)(2,1)}, u32[]{:S(2)}, u32[]{:S(2)}) async-start(bf16[128,48,128]{2,1,0:T(8,128)(2,1)} %second_pack.1), calls=%async_computation.1 | async-start | bytes 3145728 | tf_op jit(solution)/shard_map/all_to_all | solution.py:449
  102.9 21.7 %copy-start.1 = (bf16[512,256]{1,0:T(8,128)(2,1)}, bf16[512,256]{1,0:T(8,128)(2,1)S(1)}, u32[]{:S(2)}) copy-start(bf16[512,256]{1,0:T(8,128)(2,1)S(1)} %gather_fusion) | copy-start | bytes 786436
  102.9 9.8 %collective-permute-start.2 = (bf16[512,256]{1,0:T(8,128)(2,1)S(1)}, bf16[512,256]{1,0:T(8,128)(2,1)S(1)}, u32[]{:S(2)}, u32[]{:S(2)}) collective-permute-start(bf16[512,256]{1,0:T(8,128)(2,1)S(1)} %gather_fusion), channel_id=1, source_target_pairs={{0,3},{1,0},{2,1},{3,2},{4,7},{5,4},{6,5},{7,6},{8,11},{9,8},{10,9... | collective-permute-start | bytes 786440 | tf_op jit(solution)/shard_map/ppermute | solution.py:421
  107.3 10.1 %collective-permute-start.1 = (bf16[512,256]{1,0:T(8,128)(2,1)S(1)}, bf16[512,256]{1,0:T(8,128)(2,1)S(1)}, u32[]{:S(2)}, u32[]{:S(2)}) collective-permute-start(bf16[512,256]{1,0:T(8,128)(2,1)S(1)} %gather_fusion), channel_id=1, source_target_pairs={{0,2},{1,3},{2,0},{3,1},{4,6},{5,7},{6,4},{7,5},{8,10},{9,11},{10,... | collective-permute-start | bytes 786440 | tf_op jit(solution)/shard_map/ppermute | solution.py:421
  109.8 14.9 %collective-permute-start = (bf16[512,256]{1,0:T(8,128)(2,1)S(1)}, bf16[512,256]{1,0:T(8,128)(2,1)S(1)}, u32[]{:S(2)}, u32[]{:S(2)}) collective-permute-start(bf16[512,256]{1,0:T(8,128)(2,1)S(1)} %gather_fusion), channel_id=1, source_target_pairs={{0,1},{1,2},{2,3},{3,0},{4,5},{5,6},{6,7},{7,4},{8,9},{9,10},{10,1... | collective-permute-start | bytes 786440 | tf_op jit(solution)/shard_map/ppermute | solution.py:421
  112.8 11.9 %copy-start.12 = (bf16[512,256]{1,0:T(8,128)(2,1)}, bf16[512,256]{1,0:T(8,128)(2,1)S(1)}, u32[]{:S(2)}) copy-start(bf16[512,256]{1,0:T(8,128)(2,1)S(1)} %collective-permute-done.2.r3) | copy-start | bytes 786436
  117.4 7.2 %copy-start.13 = (bf16[512,256]{1,0:T(8,128)(2,1)}, bf16[512,256]{1,0:T(8,128)(2,1)S(1)}, u32[]{:S(2)}) copy-start(bf16[512,256]{1,0:T(8,128)(2,1)S(1)} %collective-permute-done.1.r2) | copy-start | bytes 786436
  144.5 17.4 %copy-start.2 = (bf16[512,256]{1,0:T(8,128)(2,1)S(1)}, bf16[512,256]{1,0:T(8,128)(2,1)}, u32[]{:S(2)}) copy-start(bf16[512,256]{1,0:T(8,128)(2,1)} %copy-done.1) | copy-start | bytes 786436
  (2 other events, 1.7 us)

commit v5 on v3

v5 whole, which is shorter than its diff:
```python
import functools

import jax
import jax.numpy as jnp
from jax import lax
from jax.experimental import pallas as pl
from jax.experimental.pallas import tpu as pltpu
from jax.sharding import PartitionSpec as P

HEADS = 8
DH = 128
BLK = 32
MAXBLK = 128
GROUP = 128
CSLOT = 4
PER = 32
EPS = 1e-05
VMEM = 28 * 1024 * 1024
WHOLE = pl.BlockSpec(memory_space=pltpu.VMEM)
IN_HBM = pl.BlockSpec(memory_space=pltpu.HBM)


def hbm(x):
    return pltpu.with_memory_space_constraint(x, pltpu.HBM)


def cost(flops, nbytes, trans=0):
    return pl.CostEstimate(flops=flops, bytes_accessed=nbytes, transcendentals=trans)


def spread_rows(rows_in):
    count, columns = rows_in.shape
    halves = columns // DH
    x = jnp.concatenate([rows_in[:, h * DH : (h + 1) * DH] for h in range(halves)], axis=0)
    shape = (halves * count, halves * count)
    at = lax.broadcasted_iota(jnp.int32, shape, 0)
    source = lax.broadcasted_iota(jnp.int32, shape, 1)
    group, inner = at // (CSLOT * halves), at % (CSLOT * halves)
    wanted = (inner // CSLOT) * count + group * CSLOT + inner % CSLOT
    pick = jnp.where(source == wanted, 1.0, 0.0).astype(jnp.bfloat16)
    return jnp.dot(pick, x, preferred_element_type=jnp.float32).astype(rows_in.dtype)


def pack_kernel(head, with_rows, home_in, table_in, keys_in, values_in, *refs):
    out, home, table, keys, values, cand, made, index_sem, load_sem, store_sem = refs[-10:]
    cols = pl.ds(head * DH, DH)
    pairs = [(home_in, home), (table_in, table)]
    if with_rows:
        pairs.append((refs[0], cand))
    indices = [pltpu.make_async_copy(a, b, index_sem.at[i]) for i, (a, b) in enumerate(pairs)]
    blocks = [
        pltpu.make_async_copy(a.at[:, :, cols], b, load_sem.at[i])
        for i, (a, b) in enumerate(((keys_in, keys), (values_in, values)))
    ]
    for load in indices[2:] + indices[:2] + blocks:
        load.start()
    shards, rows, _ = made.shape
    if with_rows:
        indices[2].wait()
        step = 32
        for b in range(0, cand.shape[0], step):
            x = spread_rows(cand[b : b + step, :])
            n = step // CSLOT
            made[b // CSLOT : b // CSLOT + n, 2 * BLK :, :] = x.reshape(n, rows - 2 * BLK, DH)
    for load in indices[:2] + blocks:
        load.wait()
    me = lax.axis_index("req")
    per = shards // store_sem.shape[0]
    stores = []
    for c in range(store_sem.shape[0]):
        chunk = pl.ds(c * per, per)
        for r in range(c * per, (c + 1) * per):
            behind = me - home[r]
            slot = table[r, jnp.where(behind < 0, behind + shards, behind)]
            made[r, :BLK, :] = keys[slot]
            made[r, BLK : 2 * BLK, :] = values[slot]
        stores.append(pltpu.make_async_copy(made.at[chunk], out.at[chunk], store_sem.at[c]))
        stores[-1].start()
    for store in stores:
        store.wait()


def pack(head, home, table, keys, values, cand=None, after=()):
    shards = home.shape[0]
    rows = 2 * BLK
    args = [hbm(home), hbm(table), hbm(keys), hbm(values)]
    held_cand = (16, DH)
    if cand is not None:
        rows += cand.shape[0] * cand.shape[1] // (DH * shards)
        args.append(hbm(cand))
        held_cand = cand.shape
    out_shape = (shards, rows, DH)
    held = (keys.shape[0], BLK, DH)
    return pl.pallas_call(
        functools.partial(pack_kernel, head, cand is not None),
        out_shape=pltpu.HBM(out_shape, keys.dtype),
        in_specs=[IN_HBM] * len(args) + [pl.BlockSpec(memory_space=pl.ANY)] * len(after),
        out_specs=IN_HBM,
        scratch_shapes=[
            pltpu.SMEM(home.shape, jnp.int32),
            pltpu.SMEM(table.shape, jnp.int32),
            pltpu.VMEM(held, keys.dtype),
            pltpu.VMEM(held, keys.dtype),
            pltpu.VMEM(held_cand, keys.dtype),
            pltpu.VMEM(out_shape, keys.dtype),
            pltpu.SemaphoreType.DMA((3,)),
            pltpu.SemaphoreType.DMA((2,)),
            pltpu.SemaphoreType.DMA((4,)),
        ],
        compiler_params=pltpu.CompilerParams(vmem_limit_bytes=VMEM),
        cost_estimate=cost(0, 2 * shards * rows * DH * 2),
        name="pack",
    )(*args, *after)


def silu(half):
    return half + half * jnp.tanh(half)


def project_kernel(r0, r1, r2, r3, w, g1, g2, g3, gates, query, own, normed):
    pieces = [r[...].astype(jnp.float32) for r in (r0, r1, r2, r3)]
    split = len(pieces)
    width = r0.shape[1]
    total = split * width
    part = lax.axis_index("mp")
    place = [lax.rem(part + (split - d), split) for d in range(split)]
    mean = sum(jnp.sum(p, axis=1, keepdims=True) for p in pieces) / total
    centred = [p - mean for p in pieces]
    spread = sum(jnp.sum(c * c, axis=1, keepdims=True) for c in centred) / total
    scale = lax.rsqrt(spread + EPS)
    for d in range(split):
        at = pl.multiple_of(place[d] * width, width)
        normed[:, pl.ds(at, width)] = (centred[d] * scale).astype(jnp.bfloat16)
    x = normed[...]

    def times(matrix):
        return silu(0.5 * jnp.dot(x, matrix, preferred_element_type=jnp.float32)).astype(
            jnp.bfloat16
        )

    gates[place[0]] = times(w[:, :width])
    for d, g in ((1, g1), (2, g2), (3, g3)):
        gates[place[d]] = times(g[...])
    value = times(w[:, width : 2 * width]).astype(jnp.float32)
    q = times(w[:, 2 * width : 3 * width])
    key = times(w[:, 3 * width :]).astype(jnp.float32)
    product = q.astype(jnp.float32) * key
    for h in range(width // DH):
        cols = slice(h * DH, (h + 1) * DH)
        half = jnp.sum(product[:, cols], axis=1, keepdims=True) * (0.5 * DH**-0.5)
        own[h] = silu(half) * value[:, cols]
        query[h] = q[:, cols]


def project(rows, w, gate_w):
    cands, width = rows[0].shape
    split = len(rows)
    depth = split * width
    step = 256
    heads = width // DH
    block = pl.BlockSpec((step, width), lambda i: (i, 0))
    by_head = pl.BlockSpec((heads, step, DH), lambda i: (0, i, 0))
    whole = lambda a: pl.BlockSpec(a.shape, lambda i: (0, 0))
    return pl.pallas_call(
        project_kernel,
        out_shape=(
            jax.ShapeDtypeStruct((split, cands, width), jnp.bfloat16),
            pltpu.HBM((heads, cands, DH), jnp.bfloat16),
            pltpu.HBM((heads, cands, DH), jnp.float32),
        ),
        grid=(cands // step,),
        in_specs=[block] * split + [whole(w)] + [whole(g) for g in gate_w],
        out_specs=(
            pl.BlockSpec((split, step, width), lambda i: (0, i, 0)),
            by_head,
            by_head,
        ),
        scratch_shapes=[pltpu.VMEM((step, depth), jnp.bfloat16)],
        compiler_params=pltpu.CompilerParams(vmem_limit_bytes=VMEM),
        cost_estimate=cost(2 * cands * depth * 7 * width, 8 << 20, cands * 7 * width),
        name="project",
    )(*[hbm(r) for r in rows], hbm(w), *[hbm(g) for g in gate_w])


def attend_kernel(query, got, mask, own, *refs):
    out, weights, total = refs[-3:]
    step = pl.program_id(0)
    n = got.shape[0] * BLK
    keys = got[:, :BLK, :].reshape(n, DH)
    for g in range(weights.shape[0] // GROUP):
        rows = slice(g * GROUP, (g + 1) * GROUP)
        s = lax.dot_general(
            query[0, rows, :], keys, (((1,), (1,)), ((), ())), preferred_element_type=jnp.float32
        )
        weights[rows, :] = silu(s * mask[g : g + 1, :]).astype(jnp.bfloat16)
    part = jnp.dot(
        weights[...], got[:, BLK : 2 * BLK, :].reshape(n, DH), preferred_element_type=jnp.float32
    )

    @pl.when(step == 0)
    def _():
        total[...] = own[0] + part

    @pl.when(step > 0)
    def _():
        total[...] += part

    @pl.when(step == pl.num_programs(0) - 1)
    def _():
        done = total[...].astype(jnp.bfloat16)
        for i in range(out.shape[0]):
            out[i] = done


def attend(head, query, got, mask, own, copies, after=()):
    shards = got.shape[0]
    _, cands, _ = query.shape
    n = PER * BLK
    of_head = pl.BlockSpec((1, cands, DH), lambda i: (head, 0, 0))
    return pl.pallas_call(
        attend_kernel,
        out_shape=jax.ShapeDtypeStruct((copies, cands, DH), jnp.bfloat16),
        grid=(shards // PER,),
        in_specs=[
            of_head,
            pl.BlockSpec((PER, 2 * BLK, DH), lambda i: (i, 0, 0)),
            pl.BlockSpec((mask.shape[0], n), lambda i: (0, i)),
            of_head,
        ]
        + [pl.BlockSpec(memory_space=pl.ANY)] * len(after),
        out_specs=pl.BlockSpec((copies, cands, DH), lambda i: (0, 0, 0)),
        scratch_shapes=[
            pltpu.VMEM((cands, n), jnp.bfloat16),
            pltpu.VMEM((cands, DH), jnp.float32),
        ],
        compiler_params=pltpu.CompilerParams(vmem_limit_bytes=VMEM),
        cost_estimate=cost(4 * cands * shards * BLK * DH, 4 << 20, cands * shards * BLK),
        name="attend",
    )(hbm(query), hbm(got), hbm(mask), hbm(own), *after)


def finish_kernel(a0, a1, a2, a3, last, gates, w, rows, out, made, sems):
    split, cands, width = gates.shape
    total = split * width
    count = sems.shape[0]
    step = cands // count
    part = lax.axis_index("mp")
    place = [lax.rem(part + (split - d), split) for d in range(split)]
    stores = []
    for b in range(count):
        here = slice(b * step, (b + 1) * step)
        pieces = [
            jnp.concatenate([a[0, here, :], last[place[d], here, :]], axis=1).astype(jnp.float32)
            for d, a in enumerate((a0, a1, a2, a3))
        ]
        mean = jnp.sum(sum(pieces), axis=1, keepdims=True) / total
        centred = [p - mean for p in pieces]
        spread = jnp.sum(sum(c * c for c in centred), axis=1, keepdims=True) / total
        scale = lax.rsqrt(spread + EPS)
        result = rows[here, :].astype(jnp.float32)
        for d in range(split):
            gate = gates[place[d], here, :].astype(jnp.float32)
            result += jnp.dot(
                (centred[d] * scale * gate).astype(jnp.bfloat16),
                w[place[d]],
                preferred_element_type=jnp.float32,
            )
        made[here, :] = result.astype(made.dtype)
        at = pl.ds(b * step, step)
        stores.append(pltpu.make_async_copy(made.at[at], out.at[at], sems.at[b]))
        stores[-1].start()
    for store in stores:
        store.wait()


def finish(firsts, last, gates, w, rows):
    split, cands, width = gates.shape
    return pl.pallas_call(
        finish_kernel,
        out_shape=pltpu.HBM(rows.shape, jnp.bfloat16),
        in_specs=[WHOLE] * (len(firsts) + 4),
        out_specs=IN_HBM,
        scratch_shapes=[
            pltpu.VMEM(rows.shape, jnp.bfloat16),
            pltpu.SemaphoreType.DMA((4,)),
        ],
        compiler_params=pltpu.CompilerParams(vmem_limit_bytes=VMEM),
        cost_estimate=cost(2 * cands * split * width * rows.shape[1], 3 << 20),
        name="finish",
    )(*firsts, last, gates, w, rows)


def local(
    cand_feats, cand_perm, w_in, w_out, cache_k, cache_v, hist_len, hist_home, hist_slot, hist_mask
):
    shards = lax.axis_size("req")
    split = lax.axis_size("mp")
    me = lax.axis_index("req")
    part = lax.axis_index("mp")
    columns = cand_feats.shape[1]
    halves = columns // DH
    cand_slot = cand_feats.shape[0] // shards
    cands = cand_perm.shape[1]
    width = w_in.shape[2]

    def back(x, d):
        return lax.ppermute(x, "mp", [(i, (i + d) % split) for i in range(split)])

    exchange = functools.partial(
        lax.all_to_all, axis_name="req", split_axis=0, concat_axis=0, tiled=True
    )
    history = (hist_home, hist_slot, cache_k, cache_v)
    got_first = exchange(pack(0, *history, cand=cand_feats))

    w_gate = w_in[:, 0, :]
    gate_w = [back(w_gate, d) for d in range(1, split)]
    own_out = []
    for d in range(split):
        piece = lax.dynamic_slice_in_dim(w_out, (part + d) % split * columns, columns, axis=1)
        own_out.append(back(piece, d) if d else piece)
    backs = (part - jnp.arange(split, dtype=jnp.int32)) % split
    own_out = jnp.take(jnp.stack(own_out), backs, axis=0, mode="clip")

    home = hist_home[me]
    order = (jnp.arange(shards, dtype=jnp.int32) - home) % shards
    seen = jnp.take(hist_mask[0], order, axis=1, mode="clip").astype(jnp.float32)
    inside = order[:, None] * BLK + jnp.arange(BLK, dtype=jnp.int32)[None, :] < hist_len[0]
    mask = seen[:, :, None] * jnp.where(inside, 0.5 * DH**-0.5, 0.0)[None]
    mask = mask.reshape(hist_mask.shape[1], shards * BLK)

    w_flat = w_in.reshape(w_in.shape[0], 4 * width)
    ready = [*gate_w, own_out, mask, w_flat]
    got_second = exchange(pack(1, *history, after=ready))

    arrived = (
        got_first[:, 2 * BLK :, :]
        .reshape(shards, halves, cand_slot, DH)
        .transpose(0, 2, 1, 3)
        .reshape(cands, columns)
    )
    own_rows = jnp.take(arrived, cand_perm[0], axis=0, mode="clip")
    rows = [own_rows] + [back(own_rows, d) for d in range(1, split)]
    gates, query, own = project(rows, w_flat, gate_w)

    first = attend(0, query, got_first, mask, own, 1)
    firsts = [first] + [back(first, d) for d in range(1, split)]
    last = attend(1, query, got_second, mask, own, split, after=firsts[1:])
    last = lax.all_to_all(last, "mp", split_axis=0, concat_axis=0, tiled=True)
    return finish(firsts, last, gates, own_out, own_rows)


def solution(mesh):
    in_specs = (
        P("req", "mp"),
        P("req", None),
        P(None, None, "mp"),
        P("mp", None),
        P("req", None, "mp"),
        P("req", None, "mp"),
        P("req"),
        P(),
        P(),
        P("req", None, None),
    )
    out_specs = P("req", "mp")
    return jax.shard_map(local, mesh=mesh, in_specs=in_specs, out_specs=out_specs, check_vma=False)
```

time: 168 us -> 160 us (0.952)
  starting transfers between devices: 55.5 us -> 71.9 us
  waiting for transfers between devices: 47.8 us -> 34.7 us
  blocking collectives: 16.8 us -> 12.2 us
  local copies, waits for them, and re-layouts: 15.5 us -> 11.3 us
  Pallas kernels: 28.4 us -> 24.4 us
    ppermute x9 -> x12, starting transfers between devices: 25.6 us -> 44.1 us  [back(): return lax.ppermute(x, 'mp', [(i, (i + d) % split) for i in range(split)])]
    ppermute x9 -> x12, waiting for transfers between devices: 29.2 us -> 21.6 us  [back(): return lax.ppermute(x, 'mp', [(i, (i + d) % split) for i in range(split)])]
    all_to_all x2, waiting for transfers between devices: 18.6 us -> 13 us  [the longest x1 6.91 us: local(): got_second = exchange(pack(1, *history, after=ready))]
    all_to_all x1, blocking collectives: 16.8 us -> 12.2 us  [local(): last = lax.all_to_all(last, 'mp', split_axis=0, concat_axis=0, tiled=True)]
    unnamed x32 -> x34, local copies, waits for them, and re-layouts: 7.86 us -> 3.91 us
    pallas_call x4, Pallas kernels: 19.7 us -> 16.2 us  [the longest x2 9.24 us: attend(): pl.pallas_call(attend_kernel, out_shape=jax.ShapeDtypeStruct((copies, can...]
    all_to_all x2, starting transfers between devices: 29.9 us -> 27.7 us  [the longest x1 19 us: local(): got_first = exchange(pack(0, *history, cand=cand_feats))]
  transfers between devices with their start and end apart: 11 -> 14, of which waited for: 7 -> 6; matrix products, arithmetic and copies ran while one was open for 9% -> 9% of each run, Pallas kernels for 10% -> 9%
where the time goes in v5:
time: 160 us; the launch traced here: 159 us
  starting transfers between devices  71.9 us (45%)
  waiting for transfers between devices  34.7 us (22%)
  Pallas kernels  24.4 us (15%)
  blocking collectives  12.2 us (8%)
  local copies, waits for them, and re-layouts  11.3 us (7%)
  other arithmetic  3.17 us (2%)
    ppermute x12, starting transfers between devices, back(): return lax.ppermute(x, 'mp', [(i, (i + d) % split) for i in range(split)])  44.1 us
    ppermute x12, waiting for transfers between devices, back(): return lax.ppermute(x, 'mp', [(i, (i + d) % split) for i in range(split)])  21.6 us
    all_to_all x1, starting transfers between devices, local(): got_first = exchange(pack(0, *history, cand=cand_feats))  19 us
    all_to_all x1, blocking collectives, local(): last = lax.all_to_all(last, 'mp', split_axis=0, concat_axis=0, tiled=True)  12.2 us
    pallas_call x2, Pallas kernels, attend(): pl.pallas_call(attend_kernel, out_shape=jax.ShapeDtypeStruct((copies, can...  9.24 us
    all_to_all x1, starting transfers between devices, local(): got_second = exchange(pack(1, *history, after=ready))  8.76 us
    pallas_call x2, Pallas kernels, pack(): pl.pallas_call(functools.partial(pack_kernel, head, cand is not None), ou...  6.99 us
    all_to_all x1, waiting for transfers between devices, local(): got_second = exchange(pack(1, *history, after=ready))  6.91 us
  transfers between devices with their start and end apart: 14, of which 6 were waited for; matrix products, arithmetic and copies ran while one was open for 9% of the time, Pallas kernels for 9%

profile of v5, /device:TPU:1, one launch (start us, length us, event | category | flops | bytes accessed | tf_op | source)
XLA Modules:
  0.0 158.8 jit_solution(2872497014711784377)
XLA Ops:
  0.0 3.5 %pack.2 = bf16[128,72,128]{2,1,0:T(8,128)(2,1)} custom-call(s32[128]{0:T(128)} %home_in.3, s32[128,128]{1,0:T(8,128)} %table_in.3, bf16[32,32,256]{2,1,0:T(8,128)(2,1)} %keys_in.3, bf16[32,32,256]{2,1,0:T(8,128)(2,1)} %values_in.3, bf16[512,256]{1,0:T(8,128)(2,1)} %refs_0_.1), custom_call_target="tpu_custom_call" | custom-call | bytes 4718592 | tf_op jit(solution)/shard_map/pack/pallas_call | solution.py:94
  3.5 19.0 %all-to-all-start = ((bf16[128,72,128]{2,1,0:T(8,128)(2,1)}), bf16[128,72,128]{2,1,0:T(8,128)(2,1)}, u32[]{:S(2)}, u32[]{:S(2)}) async-start(bf16[128,72,128]{2,1,0:T(8,128)(2,1)} %pack.2), calls=%async_computation | async-start | bytes 4718592 | tf_op jit(solution)/shard_map/all_to_all | solution.py:313
  24.2 3.1 %collective-permute-start.3 = (bf16[1024,256]{1,0:T(8,128)(2,1)}, bf16[1024,256]{1,0:T(8,128)(2,1)S(1)}, u32[]{:S(2)}, u32[]{:S(2)}) collective-permute-start(bf16[1024,256]{1,0:T(8,128)(2,1)} %bitcast.28), channel_id=1, source_target_pairs={{0,1},{1,2},{2,3},{3,0},{4,5},{5,6},{6,7},{7,4},{8,9},{9,10},{10,1... | collective-permute-start | bytes 1572872 | tf_op jit(solution)/shard_map/ppermute | solution.py:307
  27.3 4.4 %collective-permute-start.4 = (bf16[1024,256]{1,0:T(8,128)(2,1)}, bf16[1024,256]{1,0:T(8,128)(2,1)}, u32[]{:S(2)}, u32[]{:S(2)}) collective-permute-start(bf16[1024,256]{1,0:T(8,128)(2,1)} %bitcast.28), channel_id=1, source_target_pairs={{0,2},{1,3},{2,0},{3,1},{4,6},{5,7},{6,4},{7,5},{8,10},{9,11},{10,... | collective-permute-start | bytes 1572872 | tf_op jit(solution)/shard_map/ppermute | solution.py:307
  31.7 3.1 %collective-permute-start.5 = (bf16[1024,256]{1,0:T(8,128)(2,1)}, bf16[1024,256]{1,0:T(8,128)(2,1)}, u32[]{:S(2)}, u32[]{:S(2)}) collective-permute-start(bf16[1024,256]{1,0:T(8,128)(2,1)} %bitcast.28), channel_id=1, source_target_pairs={{0,3},{1,0},{2,1},{3,2},{4,7},{5,4},{6,5},{7,6},{8,11},{9,8},{10,9... | collective-permute-start | bytes 1572872 | tf_op jit(solution)/shard_map/ppermute | solution.py:307
  36.8 4.0 %collective-permute-start.10 = (bf16[256,256]{1,0:T(8,128)(2,1)S(1)}, bf16[256,256]{1,0:T(8,128)(2,1)}, u32[]{:S(2)}, u32[]{:S(2)}) collective-permute-start(bf16[256,256]{1,0:T(8,128)(2,1)S(1)} %get-tuple-element.14), channel_id=1, source_target_pairs={{0,2},{1,3},{2,0},{3,1},{4,6},{5,7},{6,4},{7,5},{8,10},{9,11},{10,... | collective-permute-start | bytes 393224 | tf_op jit(solution)/shard_map/ppermute | solution.py:307
  44.9 13.1 %collective-permute-done.11 = bf16[256,256]{1,0:T(8,128)(2,1)S(1)} collective-permute-done((bf16[256,256]{1,0:T(8,128)(2,1)S(1)}, bf16[256,256]{1,0:T(8,128)(2,1)S(1)}, u32[]{:S(2)}, u32[]{:S(2)}) %collective-permute-start.11) | collective-permute-done | bytes 131104 | tf_op jit(solution)/shard_map/ppermute | solution.py:307
  58.0 5.4 %collective-permute-start.9 = (bf16[256,256]{1,0:T(8,128)(2,1)S(1)}, bf16[256,256]{1,0:T(8,128)(2,1)S(1)}, u32[]{:S(2)}, u32[]{:S(2)}) collective-permute-start(bf16[256,256]{1,0:T(8,128)(2,1)S(1)} %get-tuple-element.12), channel_id=1, source_target_pairs={{0,1},{1,2},{2,3},{3,0},{4,5},{5,6},{6,7},{7,4},{8,9},{9,10},{10,1... | collective-permute-start | bytes 393224 | tf_op jit(solution)/shard_map/ppermute | solution.py:307
  63.5 2.1 %copy.21 = bf16[128,8,4,256]{3,1,2,0:T(8,128)(2,1)S(1)} copy(bf16[128,8,4,256]{3,2,1,0:T(4,128)(2,1)} %bitcast.34) | data formatting | bytes 4194304
  70.1 3.5 %pack.3 = bf16[128,64,128]{2,1,0:T(8,128)(2,1)} custom-call(s32[128]{0:T(128)} %home_in.3, s32[128,128]{1,0:T(8,128)} %table_in.3, bf16[32,32,256]{2,1,0:T(8,128)(2,1)} %keys_in.3, bf16[32,32,256]{2,1,0:T(8,128)(2,1)} %values_in.3, bf16[1024,256]{1,0:T(8,128)(2,1)S(1)} %collective-permute-done.3.g1.refs_0_, ...), custom_call_target="tpu_custom_call" | custom-call | bytes 4194304 | tf_op jit(solution)/shard_map/pack/pallas_call | solution.py:94
  73.6 6.1 %all-to-all-done.got = bf16[128,72,128]{2,1,0:T(8,128)(2,1)} async-done(((bf16[128,72,128]{2,1,0:T(8,128)(2,1)}), bf16[128,72,128]{2,1,0:T(8,128)(2,1)}, u32[]{:S(2)}, u32[]{:S(2)}) %all-to-all-start) | async-done | bytes 2359328 | tf_op jit(solution)/shard_map/all_to_all | solution.py:313
  79.7 8.8 %all-to-all-start.1 = ((bf16[128,64,128]{2,1,0:T(8,128)(2,1)}), bf16[128,64,128]{2,1,0:T(8,128)(2,1)}, u32[]{:S(2)}, u32[]{:S(2)}) async-start(bf16[128,64,128]{2,1,0:T(8,128)(2,1)} %pack.3), calls=%async_computation.1 | async-start | bytes 4194304 | tf_op jit(solution)/shard_map/all_to_all | solution.py:333
  91.7 3.1 %collective-permute-start = (bf16[512,256]{1,0:T(8,128)(2,1)S(1)}, bf16[512,256]{1,0:T(8,128)(2,1)S(1)}, u32[]{:S(2)}, u32[]{:S(2)}) collective-permute-start(bf16[512,256]{1,0:T(8,128)(2,1)S(1)} %gather_fusion), channel_id=1, source_target_pairs={{0,1},{1,2},{2,3},{3,0},{4,5},{5,6},{6,7},{7,4},{8,9},{9,10},{10,1... | collective-permute-start | bytes 786440 | tf_op jit(solution)/shard_map/ppermute | solution.py:307
  94.8 4.2 %collective-permute-start.1 = (bf16[512,256]{1,0:T(8,128)(2,1)S(1)}, bf16[512,256]{1,0:T(8,128)(2,1)S(1)}, u32[]{:S(2)}, u32[]{:S(2)}) collective-permute-start(bf16[512,256]{1,0:T(8,128)(2,1)S(1)} %gather_fusion), channel_id=1, source_target_pairs={{0,2},{1,3},{2,0},{3,1},{4,6},{5,7},{6,4},{7,5},{8,10},{9,11},{10,... | collective-permute-start | bytes 786440 | tf_op jit(solution)/shard_map/ppermute | solution.py:307
  99.0 3.1 %collective-permute-start.2 = (bf16[512,256]{1,0:T(8,128)(2,1)S(1)}, bf16[512,256]{1,0:T(8,128)(2,1)S(1)}, u32[]{:S(2)}, u32[]{:S(2)}) collective-permute-start(bf16[512,256]{1,0:T(8,128)(2,1)S(1)} %gather_fusion), channel_id=1, source_target_pairs={{0,3},{1,0},{2,1},{3,2},{4,7},{5,4},{6,5},{7,6},{8,11},{9,8},{10,9... | collective-permute-start | bytes 786440 | tf_op jit(solution)/shard_map/ppermute | solution.py:307
  102.1 6.1 %collective-permute-done.1.r2 = bf16[512,256]{1,0:T(8,128)(2,1)S(1)} collective-permute-done((bf16[512,256]{1,0:T(8,128)(2,1)S(1)}, bf16[512,256]{1,0:T(8,128)(2,1)S(1)}, u32[]{:S(2)}, u32[]{:S(2)}) %collective-permute-start.1) | collective-permute-done | bytes 262176 | tf_op jit(solution)/shard_map/ppermute | solution.py:307
  110.3 6.5 %project.1 = (bf16[4,512,256]{2,1,0:T(8,128)(2,1)S(1)}, bf16[2,512,128]{2,1,0:T(8,128)(2,1)}, f32[2,512,128]{2,1,0:T(8,128)}) custom-call(bf16[512,256]{1,0:T(8,128)(2,1)} %copy-done.1, bf16[512,256]{1,0:T(8,128)(2,1)} %copy-done.12, bf16[512,256]{1,0:T(8,128)(2,1)} %copy-done.13, bf16[512,256]{1,0:T(8,128)(2,1)} %copy-done.14, bf16[1024,1024]{1,0:T(8,128)(2,1)} %bitcast.32, ...), custom_call_target="tpu_custom_call" | custom-call | flops 1879048192 | bytes 8388608 | tf_op jit(solution)/shard_map/project/pallas_call | solution.py:164
  116.8 4.6 %attend.2.a0 = bf16[1,512,128]{2,1,0:T(8,128)(2,1)S(1)} custom-call(bf16[2,512,128]{2,1,0:T(8,128)(2,1)} %get-tuple-element.8.query, bf16[128,72,128]{2,1,0:T(8,128)(2,1)} %all-to-all-done.got, f32[4,4096]{1,0:T(4,128)} %copy-done.4, f32[2,512,128]{2,1,0:T(8,128)} %get-tuple-element.9.own), custom_call_target="tpu_custom_call" | custom-call | flops 1073741824 | bytes 4194304 | tf_op jit(solution)/shard_map/attend/pallas_call | solution.py:220
  121.5 5.7 %collective-permute-start.6 = (bf16[1,512,128]{2,1,0:T(8,128)(2,1)S(1)}, bf16[1,512,128]{2,1,0:T(8,128)(2,1)S(1)}, u32[]{:S(2)}, u32[]{:S(2)}) collective-permute-start(bf16[1,512,128]{2,1,0:T(8,128)(2,1)S(1)} %attend.2.a0), channel_id=1, source_target_pairs={{0,1},{1,2},{2,3},{3,0},{4,5},{5,6},{6,7},{7,4},{8,9},{9,10},{10,1... | collective-permute-start | bytes 393224 | tf_op jit(solution)/shard_map/ppermute | solution.py:307
  127.1 2.7 %collective-permute-start.7 = (bf16[1,512,128]{2,1,0:T(8,128)(2,1)S(1)}, bf16[1,512,128]{2,1,0:T(8,128)(2,1)S(1)}, u32[]{:S(2)}, u32[]{:S(2)}) collective-permute-start(bf16[1,512,128]{2,1,0:T(8,128)(2,1)S(1)} %attend.2.a0), channel_id=1, source_target_pairs={{0,2},{1,3},{2,0},{3,1},{4,6},{5,7},{6,4},{7,5},{8,10},{9,11},{10,... | collective-permute-start | bytes 393224 | tf_op jit(solution)/shard_map/ppermute | solution.py:307
  129.9 3.5 %collective-permute-start.8 = (bf16[1,512,128]{2,1,0:T(8,128)(2,1)S(1)}, bf16[1,512,128]{2,1,0:T(8,128)(2,1)S(1)}, u32[]{:S(2)}, u32[]{:S(2)}) collective-permute-start(bf16[1,512,128]{2,1,0:T(8,128)(2,1)S(1)} %attend.2.a0), channel_id=1, source_target_pairs={{0,3},{1,0},{2,1},{3,2},{4,7},{5,4},{6,5},{7,6},{8,11},{9,8},{10,9... | collective-permute-start | bytes 393224 | tf_op jit(solution)/shard_map/ppermute | solution.py:307
  133.4 6.9 %all-to-all-done.1.got = bf16[128,64,128]{2,1,0:T(8,128)(2,1)} async-done(((bf16[128,64,128]{2,1,0:T(8,128)(2,1)}), bf16[128,64,128]{2,1,0:T(8,128)(2,1)}, u32[]{:S(2)}, u32[]{:S(2)}) %all-to-all-start.1) | async-done | bytes 2097184 | tf_op jit(solution)/shard_map/all_to_all | solution.py:333
  140.3 4.6 %attend.3 = bf16[4,512,128]{2,1,0:T(8,128)(2,1)S(1)} custom-call(bf16[2,512,128]{2,1,0:T(8,128)(2,1)} %get-tuple-element.8.query, bf16[128,64,128]{2,1,0:T(8,128)(2,1)} %all-to-all-done.1.got, f32[4,4096]{1,0:T(4,128)} %copy-done.4, f32[2,512,128]{2,1,0:T(8,128)} %get-tuple-element.9.own, bf16[1,512,128]{2,1,0:T(8,128)(2,1)S(1)} %collective-permute-done.6.refs_0_.a1, ...), custom_call_target="tpu_custom_call" | custom-call | flops 1073741824 | bytes 4194304 | tf_op jit(solution)/shard_map/attend/pallas_call | solution.py:220
  144.9 12.2 %all_to_all.15.last = bf16[4,512,128]{2,1,0:T(8,128)(2,1)S(1)} all-to-all(bf16[4,512,128]{2,1,0:T(8,128)(2,1)S(1)} %attend.3), channel_id=1, replica_groups=mesh['req'=128,'mp'=4] {'mp'}, dimensions={0} | all-to-all | bytes 1048576 | tf_op jit(solution)/shard_map/all_to_all | solution.py:348
  (70 shorter events, 18.4 us)
Async XLA Ops:
  3.5 19.0 %copy-start.5 = (bf16[1024,4,256]{2,1,0:T(4,128)(2,1)S(1)}, bf16[1024,4,256]{2,1,0:T(4,128)(2,1)}, u32[]{:S(2)}) copy-start(bf16[1024,4,256]{2,1,0:T(4,128)(2,1)} %param.12) | copy-start | bytes 6291460
  3.5 76.2 %all-to-all-start = ((bf16[128,72,128]{2,1,0:T(8,128)(2,1)}), bf16[128,72,128]{2,1,0:T(8,128)(2,1)}, u32[]{:S(2)}, u32[]{:S(2)}) async-start(bf16[128,72,128]{2,1,0:T(8,128)(2,1)} %pack.2), calls=%async_computation | async-start | bytes 4718592 | tf_op jit(solution)/shard_map/all_to_all | solution.py:313
  22.5 12.3 %copy-start.6 = (bf16[256,1024]{1,0:T(8,128)(2,1)S(1)}, bf16[256,1024]{1,0:T(8,128)(2,1)}, u32[]{:S(2)}) copy-start(bf16[256,1024]{1,0:T(8,128)(2,1)} %param.13) | copy-start | bytes 1572868
  22.5 18.3 %copy-start.9 = (s32[1,4,128]{2,1,0:T(4,128)S(1)}, s32[1,4,128]{2,1,0:T(4,128)}, u32[]{:S(2)}) copy-start(s32[1,4,128]{2,1,0:T(4,128)} %param.19) | copy-start | bytes 6148
  22.6 18.4 %copy-start.11 = (s32[128]{0:T(128)S(1)}, s32[128]{0:T(128)}, u32[]{:S(2)}) copy-start(s32[128]{0:T(128)} %home_in.3) | copy-start | bytes 1540
  24.2 45.9 %collective-permute-start.3 = (bf16[1024,256]{1,0:T(8,128)(2,1)}, bf16[1024,256]{1,0:T(8,128)(2,1)S(1)}, u32[]{:S(2)}, u32[]{:S(2)}) collective-permute-start(bf16[1024,256]{1,0:T(8,128)(2,1)} %bitcast.28), channel_id=1, source_target_pairs={{0,1},{1,2},{2,3},{3,0},{4,5},{5,6},{6,7},{7,4},{8,9},{9,10},{10,1... | collective-permute-start | bytes 1572872 | tf_op jit(solution)/shard_map/ppermute | solution.py:307
  27.3 42.8 %collective-permute-start.4 = (bf16[1024,256]{1,0:T(8,128)(2,1)}, bf16[1024,256]{1,0:T(8,128)(2,1)}, u32[]{:S(2)}, u32[]{:S(2)}) collective-permute-start(bf16[1024,256]{1,0:T(8,128)(2,1)} %bitcast.28), channel_id=1, source_target_pairs={{0,2},{1,3},{2,0},{3,1},{4,6},{5,7},{6,4},{7,5},{8,10},{9,11},{10,... | collective-permute-start | bytes 1572872 | tf_op jit(solution)/shard_map/ppermute | solution.py:307
  31.7 38.4 %collective-permute-start.5 = (bf16[1024,256]{1,0:T(8,128)(2,1)}, bf16[1024,256]{1,0:T(8,128)(2,1)}, u32[]{:S(2)}, u32[]{:S(2)}) collective-permute-start(bf16[1024,256]{1,0:T(8,128)(2,1)} %bitcast.28), channel_id=1, source_target_pairs={{0,3},{1,0},{2,1},{3,2},{4,7},{5,4},{6,5},{7,6},{8,11},{9,8},{10,9... | collective-permute-start | bytes 1572872 | tf_op jit(solution)/shard_map/ppermute | solution.py:307
  34.9 23.1 %collective-permute-start.11 = (bf16[256,256]{1,0:T(8,128)(2,1)S(1)}, bf16[256,256]{1,0:T(8,128)(2,1)S(1)}, u32[]{:S(2)}, u32[]{:S(2)}) collective-permute-start(bf16[256,256]{1,0:T(8,128)(2,1)S(1)} %get-tuple-element.13), channel_id=1, source_target_pairs={{0,3},{1,0},{2,1},{3,2},{4,7},{5,4},{6,5},{7,6},{8,11},{9,8},{10,9... | collective-permute-start | bytes 393224 | tf_op jit(solution)/shard_map/ppermute | solution.py:307
  36.8 28.8 %collective-permute-start.10 = (bf16[256,256]{1,0:T(8,128)(2,1)S(1)}, bf16[256,256]{1,0:T(8,128)(2,1)}, u32[]{:S(2)}, u32[]{:S(2)}) collective-permute-start(bf16[256,256]{1,0:T(8,128)(2,1)S(1)} %get-tuple-element.14), channel_id=1, source_target_pairs={{0,2},{1,3},{2,0},{3,1},{4,6},{5,7},{6,4},{7,5},{8,10},{9,11},{10,... | collective-permute-start | bytes 393224 | tf_op jit(solution)/shard_map/ppermute | solution.py:307
  44.9 25.2 %copy-start.4 = (f32[4,4096]{1,0:T(4,128)}, f32[4,4096]{1,0:T(4,128)S(1)}, u32[]{:S(2)}) copy-start(f32[4,4096]{1,0:T(4,128)S(1)} %broadcast_multiply_fusion.mask.refs_4_) | copy-start | bytes 196612
  58.0 8.7 %collective-permute-start.9 = (bf16[256,256]{1,0:T(8,128)(2,1)S(1)}, bf16[256,256]{1,0:T(8,128)(2,1)S(1)}, u32[]{:S(2)}, u32[]{:S(2)}) collective-permute-start(bf16[256,256]{1,0:T(8,128)(2,1)S(1)} %get-tuple-element.12), channel_id=1, source_target_pairs={{0,1},{1,2},{2,3},{3,0},{4,5},{5,6},{6,7},{7,4},{8,9},{9,10},{10,1... | collective-permute-start | bytes 393224 | tf_op jit(solution)/shard_map/ppermute | solution.py:307
  65.6 8.0 %copy-start = (bf16[128,8,4,256]{3,1,2,0:T(8,128)(2,1)}, bf16[128,8,4,256]{3,1,2,0:T(8,128)(2,1)S(1)}, u32[]{:S(2)}) copy-start(bf16[128,8,4,256]{3,1,2,0:T(8,128)(2,1)S(1)} %copy.21) | copy-start | bytes 6291460
  73.6 14.9 %copy-start.10 = (s32[1,512]{1,0:T(1,128)S(1)}, s32[1,512]{1,0:T(1,128)}, u32[]{:S(2)}) copy-start(s32[1,512]{1,0:T(1,128)} %param.11) | copy-start | bytes 6148
  79.7 60.6 %all-to-all-start.1 = ((bf16[128,64,128]{2,1,0:T(8,128)(2,1)}), bf16[128,64,128]{2,1,0:T(8,128)(2,1)}, u32[]{:S(2)}, u32[]{:S(2)}) async-start(bf16[128,64,128]{2,1,0:T(8,128)(2,1)} %pack.3), calls=%async_computation.1 | async-start | bytes 4194304 | tf_op jit(solution)/shard_map/all_to_all | solution.py:333
  91.7 17.9 %copy-start.1 = (bf16[512,256]{1,0:T(8,128)(2,1)}, bf16[512,256]{1,0:T(8,128)(2,1)S(1)}, u32[]{:S(2)}) copy-start(bf16[512,256]{1,0:T(8,128)(2,1)S(1)} %gather_fusion) | copy-start | bytes 786436
  91.7 10.4 %collective-permute-start = (bf16[512,256]{1,0:T(8,128)(2,1)S(1)}, bf16[512,256]{1,0:T(8,128)(2,1)S(1)}, u32[]{:S(2)}, u32[]{:S(2)}) collective-permute-start(bf16[512,256]{1,0:T(8,128)(2,1)S(1)} %gather_fusion), channel_id=1, source_target_pairs={{0,1},{1,2},{2,3},{3,0},{4,5},{5,6},{6,7},{7,4},{8,9},{9,10},{10,1... | collective-permute-start | bytes 786440 | tf_op jit(solution)/shard_map/ppermute | solution.py:307
  94.8 13.3 %collective-permute-start.1 = (bf16[512,256]{1,0:T(8,128)(2,1)S(1)}, bf16[512,256]{1,0:T(8,128)(2,1)S(1)}, u32[]{:S(2)}, u32[]{:S(2)}) collective-permute-start(bf16[512,256]{1,0:T(8,128)(2,1)S(1)} %gather_fusion), channel_id=1, source_target_pairs={{0,2},{1,3},{2,0},{3,1},{4,6},{5,7},{6,4},{7,5},{8,10},{9,11},{10,... | collective-permute-start | bytes 786440 | tf_op jit(solution)/shard_map/ppermute | solution.py:307
  99.0 10.6 %collective-permute-start.2 = (bf16[512,256]{1,0:T(8,128)(2,1)S(1)}, bf16[512,256]{1,0:T(8,128)(2,1)S(1)}, u32[]{:S(2)}, u32[]{:S(2)}) collective-permute-start(bf16[512,256]{1,0:T(8,128)(2,1)S(1)} %gather_fusion), channel_id=1, source_target_pairs={{0,3},{1,0},{2,1},{3,2},{4,7},{5,4},{6,5},{7,6},{8,11},{9,8},{10,9... | collective-permute-start | bytes 786440 | tf_op jit(solution)/shard_map/ppermute | solution.py:307
  102.1 7.5 %copy-start.12 = (bf16[512,256]{1,0:T(8,128)(2,1)}, bf16[512,256]{1,0:T(8,128)(2,1)S(1)}, u32[]{:S(2)}) copy-start(bf16[512,256]{1,0:T(8,128)(2,1)S(1)} %collective-permute-done.r1) | copy-start | bytes 786436
  121.4 35.7 %copy-start.2 = (bf16[512,256]{1,0:T(8,128)(2,1)S(1)}, bf16[512,256]{1,0:T(8,128)(2,1)}, u32[]{:S(2)}) copy-start(bf16[512,256]{1,0:T(8,128)(2,1)} %copy-done.1) | copy-start | bytes 786436
  121.5 18.8 %collective-permute-start.6 = (bf16[1,512,128]{2,1,0:T(8,128)(2,1)S(1)}, bf16[1,512,128]{2,1,0:T(8,128)(2,1)S(1)}, u32[]{:S(2)}, u32[]{:S(2)}) collective-permute-start(bf16[1,512,128]{2,1,0:T(8,128)(2,1)S(1)} %attend.2.a0), channel_id=1, source_target_pairs={{0,1},{1,2},{2,3},{3,0},{4,5},{5,6},{6,7},{7,4},{8,9},{9,10},{10,1... | collective-permute-start | bytes 393224 | tf_op jit(solution)/shard_map/ppermute | solution.py:307
  127.1 13.2 %collective-permute-start.7 = (bf16[1,512,128]{2,1,0:T(8,128)(2,1)S(1)}, bf16[1,512,128]{2,1,0:T(8,128)(2,1)S(1)}, u32[]{:S(2)}, u32[]{:S(2)}) collective-permute-start(bf16[1,512,128]{2,1,0:T(8,128)(2,1)S(1)} %attend.2.a0), channel_id=1, source_target_pairs={{0,2},{1,3},{2,0},{3,1},{4,6},{5,7},{6,4},{7,5},{8,10},{9,11},{10,... | collective-permute-start | bytes 393224 | tf_op jit(solution)/shard_map/ppermute | solution.py:307
  129.9 10.4 %collective-permute-start.8 = (bf16[1,512,128]{2,1,0:T(8,128)(2,1)S(1)}, bf16[1,512,128]{2,1,0:T(8,128)(2,1)S(1)}, u32[]{:S(2)}, u32[]{:S(2)}) collective-permute-start(bf16[1,512,128]{2,1,0:T(8,128)(2,1)S(1)} %attend.2.a0), channel_id=1, source_target_pairs={{0,3},{1,0},{2,1},{3,2},{4,7},{5,4},{6,5},{7,6},{8,11},{9,8},{10,9... | collective-permute-start | bytes 393224 | tf_op jit(solution)/shard_map/ppermute | solution.py:307
  (5 other events, 14.3 us)

commit v6 on v5

--- a/solution.py
+++ b/solution.py
@@ -13,7 +13,7 @@
 MAXBLK = 128
 GROUP = 128
 CSLOT = 4
-PER = 32
+PER = 64
 EPS = 1e-05
 VMEM = 28 * 1024 * 1024
 WHOLE = pl.BlockSpec(memory_space=pltpu.VMEM)

time: 160 us -> 159 us (level)
  no operation moved by 1% of the time
where the time goes in v6:
time: 159 us; the launch traced here: 158 us
  starting transfers between devices  72 us (45%)
  waiting for transfers between devices  35.1 us (22%)
  Pallas kernels  23.2 us (15%)
  blocking collectives  12.2 us (8%)
  local copies, waits for them, and re-layouts  11.3 us (7%)
  other arithmetic  3.17 us (2%)
    ppermute x12, starting transfers between devices, back(): return lax.ppermute(x, 'mp', [(i, (i + d) % split) for i in range(split)])  44.3 us
    ppermute x12, waiting for transfers between devices, back(): return lax.ppermute(x, 'mp', [(i, (i + d) % split) for i in range(split)])  21.4 us
    all_to_all x1, starting transfers between devices, local(): got_first = exchange(pack(0, *history, cand=cand_feats))  19 us
    all_to_all x1, blocking collectives, local(): last = lax.all_to_all(last, 'mp', split_axis=0, concat_axis=0, tiled=True)  12.2 us
    all_to_all x1, starting transfers between devices, local(): got_second = exchange(pack(1, *history, after=ready))  8.76 us
    pallas_call x2, Pallas kernels, attend(): pl.pallas_call(attend_kernel, out_shape=jax.ShapeDtypeStruct((copies, can...  8.01 us
    all_to_all x1, waiting for transfers between devices, local(): got_second = exchange(pack(1, *history, after=ready))  7.53 us
    pallas_call x2, Pallas kernels, pack(): pl.pallas_call(functools.partial(pack_kernel, head, cand is not None), ou...  6.99 us
  transfers between devices with their start and end apart: 14, of which 6 were waited for; matrix products, arithmetic and copies ran while one was open for 9% of the time, Pallas kernels for 9%

profile of v6, /device:TPU:1, one launch (start us, length us, event | category | flops | bytes accessed | tf_op | source)
XLA Modules:
  0.0 158.3 jit_solution(3477259411515354187)
XLA Ops:
  0.0 3.5 %pack.2 = bf16[128,72,128]{2,1,0:T(8,128)(2,1)} custom-call(s32[128]{0:T(128)} %home_in.3, s32[128,128]{1,0:T(8,128)} %table_in.3, bf16[32,32,256]{2,1,0:T(8,128)(2,1)} %keys_in.3, bf16[32,32,256]{2,1,0:T(8,128)(2,1)} %values_in.3, bf16[512,256]{1,0:T(8,128)(2,1)} %refs_0_.1), custom_call_target="tpu_custom_call" | custom-call | bytes 4718592 | tf_op jit(solution)/shard_map/pack/pallas_call | solution.py:94
  3.5 19.0 %all-to-all-start = ((bf16[128,72,128]{2,1,0:T(8,128)(2,1)}), bf16[128,72,128]{2,1,0:T(8,128)(2,1)}, u32[]{:S(2)}, u32[]{:S(2)}) async-start(bf16[128,72,128]{2,1,0:T(8,128)(2,1)} %pack.2), calls=%async_computation | async-start | bytes 4718592 | tf_op jit(solution)/shard_map/all_to_all | solution.py:313
  24.2 3.1 %collective-permute-start.3 = (bf16[1024,256]{1,0:T(8,128)(2,1)}, bf16[1024,256]{1,0:T(8,128)(2,1)S(1)}, u32[]{:S(2)}, u32[]{:S(2)}) collective-permute-start(bf16[1024,256]{1,0:T(8,128)(2,1)} %bitcast.28), channel_id=1, source_target_pairs={{0,1},{1,2},{2,3},{3,0},{4,5},{5,6},{6,7},{7,4},{8,9},{9,10},{10,1... | collective-permute-start | bytes 1572872 | tf_op jit(solution)/shard_map/ppermute | solution.py:307
  27.3 4.4 %collective-permute-start.4 = (bf16[1024,256]{1,0:T(8,128)(2,1)}, bf16[1024,256]{1,0:T(8,128)(2,1)}, u32[]{:S(2)}, u32[]{:S(2)}) collective-permute-start(bf16[1024,256]{1,0:T(8,128)(2,1)} %bitcast.28), channel_id=1, source_target_pairs={{0,2},{1,3},{2,0},{3,1},{4,6},{5,7},{6,4},{7,5},{8,10},{9,11},{10,... | collective-permute-start | bytes 1572872 | tf_op jit(solution)/shard_map/ppermute | solution.py:307
  31.7 3.1 %collective-permute-start.5 = (bf16[1024,256]{1,0:T(8,128)(2,1)}, bf16[1024,256]{1,0:T(8,128)(2,1)}, u32[]{:S(2)}, u32[]{:S(2)}) collective-permute-start(bf16[1024,256]{1,0:T(8,128)(2,1)} %bitcast.28), channel_id=1, source_target_pairs={{0,3},{1,0},{2,1},{3,2},{4,7},{5,4},{6,5},{7,6},{8,11},{9,8},{10,9... | collective-permute-start | bytes 1572872 | tf_op jit(solution)/shard_map/ppermute | solution.py:307
  36.8 4.0 %collective-permute-start.10 = (bf16[256,256]{1,0:T(8,128)(2,1)S(1)}, bf16[256,256]{1,0:T(8,128)(2,1)}, u32[]{:S(2)}, u32[]{:S(2)}) collective-permute-start(bf16[256,256]{1,0:T(8,128)(2,1)S(1)} %get-tuple-element.14), channel_id=1, source_target_pairs={{0,2},{1,3},{2,0},{3,1},{4,6},{5,7},{6,4},{7,5},{8,10},{9,11},{10,... | collective-permute-start | bytes 393224 | tf_op jit(solution)/shard_map/ppermute | solution.py:307
  44.9 13.1 %collective-permute-done.11 = bf16[256,256]{1,0:T(8,128)(2,1)S(1)} collective-permute-done((bf16[256,256]{1,0:T(8,128)(2,1)S(1)}, bf16[256,256]{1,0:T(8,128)(2,1)S(1)}, u32[]{:S(2)}, u32[]{:S(2)}) %collective-permute-start.11) | collective-permute-done | bytes 131104 | tf_op jit(solution)/shard_map/ppermute | solution.py:307
  58.0 5.4 %collective-permute-start.9 = (bf16[256,256]{1,0:T(8,128)(2,1)S(1)}, bf16[256,256]{1,0:T(8,128)(2,1)S(1)}, u32[]{:S(2)}, u32[]{:S(2)}) collective-permute-start(bf16[256,256]{1,0:T(8,128)(2,1)S(1)} %get-tuple-element.12), channel_id=1, source_target_pairs={{0,1},{1,2},{2,3},{3,0},{4,5},{5,6},{6,7},{7,4},{8,9},{9,10},{10,1... | collective-permute-start | bytes 393224 | tf_op jit(solution)/shard_map/ppermute | solution.py:307
  63.5 2.1 %copy.21 = bf16[128,8,4,256]{3,1,2,0:T(8,128)(2,1)S(1)} copy(bf16[128,8,4,256]{3,2,1,0:T(4,128)(2,1)} %bitcast.34) | data formatting | bytes 4194304
  70.1 3.5 %pack.3 = bf16[128,64,128]{2,1,0:T(8,128)(2,1)} custom-call(s32[128]{0:T(128)} %home_in.3, s32[128,128]{1,0:T(8,128)} %table_in.3, bf16[32,32,256]{2,1,0:T(8,128)(2,1)} %keys_in.3, bf16[32,32,256]{2,1,0:T(8,128)(2,1)} %values_in.3, bf16[1024,256]{1,0:T(8,128)(2,1)S(1)} %collective-permute-done.3.g1.refs_0_, ...), custom_call_target="tpu_custom_call" | custom-call | bytes 4194304 | tf_op jit(solution)/shard_map/pack/pallas_call | solution.py:94
  73.6 6.1 %all-to-all-done.got = bf16[128,72,128]{2,1,0:T(8,128)(2,1)} async-done(((bf16[128,72,128]{2,1,0:T(8,128)(2,1)}), bf16[128,72,128]{2,1,0:T(8,128)(2,1)}, u32[]{:S(2)}, u32[]{:S(2)}) %all-to-all-start) | async-done | bytes 2359328 | tf_op jit(solution)/shard_map/all_to_all | solution.py:313
  79.7 8.8 %all-to-all-start.1 = ((bf16[128,64,128]{2,1,0:T(8,128)(2,1)}), bf16[128,64,128]{2,1,0:T(8,128)(2,1)}, u32[]{:S(2)}, u32[]{:S(2)}) async-start(bf16[128,64,128]{2,1,0:T(8,128)(2,1)} %pack.3), calls=%async_computation.1 | async-start | bytes 4194304 | tf_op jit(solution)/shard_map/all_to_all | solution.py:333
  91.7 3.1 %collective-permute-start = (bf16[512,256]{1,0:T(8,128)(2,1)S(1)}, bf16[512,256]{1,0:T(8,128)(2,1)S(1)}, u32[]{:S(2)}, u32[]{:S(2)}) collective-permute-start(bf16[512,256]{1,0:T(8,128)(2,1)S(1)} %gather_fusion), channel_id=1, source_target_pairs={{0,1},{1,2},{2,3},{3,0},{4,5},{5,6},{6,7},{7,4},{8,9},{9,10},{10,1... | collective-permute-start | bytes 786440 | tf_op jit(solution)/shard_map/ppermute | solution.py:307
  94.8 4.2 %collective-permute-start.1 = (bf16[512,256]{1,0:T(8,128)(2,1)S(1)}, bf16[512,256]{1,0:T(8,128)(2,1)S(1)}, u32[]{:S(2)}, u32[]{:S(2)}) collective-permute-start(bf16[512,256]{1,0:T(8,128)(2,1)S(1)} %gather_fusion), channel_id=1, source_target_pairs={{0,2},{1,3},{2,0},{3,1},{4,6},{5,7},{6,4},{7,5},{8,10},{9,11},{10,... | collective-permute-start | bytes 786440 | tf_op jit(solution)/shard_map/ppermute | solution.py:307
  99.0 3.2 %collective-permute-start.2 = (bf16[512,256]{1,0:T(8,128)(2,1)S(1)}, bf16[512,256]{1,0:T(8,128)(2,1)S(1)}, u32[]{:S(2)}, u32[]{:S(2)}) collective-permute-start(bf16[512,256]{1,0:T(8,128)(2,1)S(1)} %gather_fusion), channel_id=1, source_target_pairs={{0,3},{1,0},{2,1},{3,2},{4,7},{5,4},{6,5},{7,6},{8,11},{9,8},{10,9... | collective-permute-start | bytes 786440 | tf_op jit(solution)/shard_map/ppermute | solution.py:307
  102.3 5.9 %collective-permute-done.1.r2 = bf16[512,256]{1,0:T(8,128)(2,1)S(1)} collective-permute-done((bf16[512,256]{1,0:T(8,128)(2,1)S(1)}, bf16[512,256]{1,0:T(8,128)(2,1)S(1)}, u32[]{:S(2)}, u32[]{:S(2)}) %collective-permute-start.1) | collective-permute-done | bytes 262176 | tf_op jit(solution)/shard_map/ppermute | solution.py:307
  110.3 6.5 %project.1 = (bf16[4,512,256]{2,1,0:T(8,128)(2,1)S(1)}, bf16[2,512,128]{2,1,0:T(8,128)(2,1)}, f32[2,512,128]{2,1,0:T(8,128)}) custom-call(bf16[512,256]{1,0:T(8,128)(2,1)} %copy-done.1, bf16[512,256]{1,0:T(8,128)(2,1)} %copy-done.12, bf16[512,256]{1,0:T(8,128)(2,1)} %copy-done.13, bf16[512,256]{1,0:T(8,128)(2,1)} %copy-done.14, bf16[1024,1024]{1,0:T(8,128)(2,1)} %bitcast.32, ...), custom_call_target="tpu_custom_call" | custom-call | flops 1879048192 | bytes 8388608 | tf_op jit(solution)/shard_map/project/pallas_call | solution.py:164
  116.8 4.0 %attend.2.a0 = bf16[1,512,128]{2,1,0:T(8,128)(2,1)S(1)} custom-call(bf16[2,512,128]{2,1,0:T(8,128)(2,1)} %get-tuple-element.8.query, bf16[128,72,128]{2,1,0:T(8,128)(2,1)} %all-to-all-done.got, f32[4,4096]{1,0:T(4,128)} %copy-done.4, f32[2,512,128]{2,1,0:T(8,128)} %get-tuple-element.9.own), custom_call_target="tpu_custom_call" | custom-call | flops 1073741824 | bytes 4194304 | tf_op jit(solution)/shard_map/attend/pallas_call | solution.py:220
  120.8 5.7 %collective-permute-start.6 = (bf16[1,512,128]{2,1,0:T(8,128)(2,1)S(1)}, bf16[1,512,128]{2,1,0:T(8,128)(2,1)S(1)}, u32[]{:S(2)}, u32[]{:S(2)}) collective-permute-start(bf16[1,512,128]{2,1,0:T(8,128)(2,1)S(1)} %attend.2.a0), channel_id=1, source_target_pairs={{0,1},{1,2},{2,3},{3,0},{4,5},{5,6},{6,7},{7,4},{8,9},{9,10},{10,1... | collective-permute-start | bytes 393224 | tf_op jit(solution)/shard_map/ppermute | solution.py:307
  126.5 2.7 %collective-permute-start.7 = (bf16[1,512,128]{2,1,0:T(8,128)(2,1)S(1)}, bf16[1,512,128]{2,1,0:T(8,128)(2,1)S(1)}, u32[]{:S(2)}, u32[]{:S(2)}) collective-permute-start(bf16[1,512,128]{2,1,0:T(8,128)(2,1)S(1)} %attend.2.a0), channel_id=1, source_target_pairs={{0,2},{1,3},{2,0},{3,1},{4,6},{5,7},{6,4},{7,5},{8,10},{9,11},{10,... | collective-permute-start | bytes 393224 | tf_op jit(solution)/shard_map/ppermute | solution.py:307
  129.3 3.5 %collective-permute-start.8 = (bf16[1,512,128]{2,1,0:T(8,128)(2,1)S(1)}, bf16[1,512,128]{2,1,0:T(8,128)(2,1)S(1)}, u32[]{:S(2)}, u32[]{:S(2)}) collective-permute-start(bf16[1,512,128]{2,1,0:T(8,128)(2,1)S(1)} %attend.2.a0), channel_id=1, source_target_pairs={{0,3},{1,0},{2,1},{3,2},{4,7},{5,4},{6,5},{7,6},{8,11},{9,8},{10,9... | collective-permute-start | bytes 393224 | tf_op jit(solution)/shard_map/ppermute | solution.py:307
  132.8 7.5 %all-to-all-done.1.got = bf16[128,64,128]{2,1,0:T(8,128)(2,1)} async-done(((bf16[128,64,128]{2,1,0:T(8,128)(2,1)}), bf16[128,64,128]{2,1,0:T(8,128)(2,1)}, u32[]{:S(2)}, u32[]{:S(2)}) %all-to-all-start.1) | async-done | bytes 2097184 | tf_op jit(solution)/shard_map/all_to_all | solution.py:333
  140.3 4.0 %attend.3 = bf16[4,512,128]{2,1,0:T(8,128)(2,1)S(1)} custom-call(bf16[2,512,128]{2,1,0:T(8,128)(2,1)} %get-tuple-element.8.query, bf16[128,64,128]{2,1,0:T(8,128)(2,1)} %all-to-all-done.1.got, f32[4,4096]{1,0:T(4,128)} %copy-done.4, f32[2,512,128]{2,1,0:T(8,128)} %get-tuple-element.9.own, bf16[1,512,128]{2,1,0:T(8,128)(2,1)S(1)} %collective-permute-done.6.refs_0_.a1, ...), custom_call_target="tpu_custom_call" | custom-call | flops 1073741824 | bytes 4194304 | tf_op jit(solution)/shard_map/attend/pallas_call | solution.py:220
  144.3 12.2 %all_to_all.15.last = bf16[4,512,128]{2,1,0:T(8,128)(2,1)S(1)} all-to-all(bf16[4,512,128]{2,1,0:T(8,128)(2,1)S(1)} %attend.3), channel_id=1, replica_groups=mesh['req'=128,'mp'=4] {'mp'}, dimensions={0} | all-to-all | bytes 1048576 | tf_op jit(solution)/shard_map/all_to_all | solution.py:348
  (70 shorter events, 18.4 us)
Async XLA Ops:
  3.5 19.0 %copy-start.5 = (bf16[1024,4,256]{2,1,0:T(4,128)(2,1)S(1)}, bf16[1024,4,256]{2,1,0:T(4,128)(2,1)}, u32[]{:S(2)}) copy-start(bf16[1024,4,256]{2,1,0:T(4,128)(2,1)} %param.12) | copy-start | bytes 6291460
  3.5 76.2 %all-to-all-start = ((bf16[128,72,128]{2,1,0:T(8,128)(2,1)}), bf16[128,72,128]{2,1,0:T(8,128)(2,1)}, u32[]{:S(2)}, u32[]{:S(2)}) async-start(bf16[128,72,128]{2,1,0:T(8,128)(2,1)} %pack.2), calls=%async_computation | async-start | bytes 4718592 | tf_op jit(solution)/shard_map/all_to_all | solution.py:313
  22.5 12.3 %copy-start.6 = (bf16[256,1024]{1,0:T(8,128)(2,1)S(1)}, bf16[256,1024]{1,0:T(8,128)(2,1)}, u32[]{:S(2)}) copy-start(bf16[256,1024]{1,0:T(8,128)(2,1)} %param.13) | copy-start | bytes 1572868
  22.5 18.3 %copy-start.9 = (s32[1,4,128]{2,1,0:T(4,128)S(1)}, s32[1,4,128]{2,1,0:T(4,128)}, u32[]{:S(2)}) copy-start(s32[1,4,128]{2,1,0:T(4,128)} %param.19) | copy-start | bytes 6148
  22.6 18.4 %copy-start.11 = (s32[128]{0:T(128)S(1)}, s32[128]{0:T(128)}, u32[]{:S(2)}) copy-start(s32[128]{0:T(128)} %home_in.3) | copy-start | bytes 1540
  24.2 45.9 %collective-permute-start.3 = (bf16[1024,256]{1,0:T(8,128)(2,1)}, bf16[1024,256]{1,0:T(8,128)(2,1)S(1)}, u32[]{:S(2)}, u32[]{:S(2)}) collective-permute-start(bf16[1024,256]{1,0:T(8,128)(2,1)} %bitcast.28), channel_id=1, source_target_pairs={{0,1},{1,2},{2,3},{3,0},{4,5},{5,6},{6,7},{7,4},{8,9},{9,10},{10,1... | collective-permute-start | bytes 1572872 | tf_op jit(solution)/shard_map/ppermute | solution.py:307
  27.3 42.8 %collective-permute-start.4 = (bf16[1024,256]{1,0:T(8,128)(2,1)}, bf16[1024,256]{1,0:T(8,128)(2,1)}, u32[]{:S(2)}, u32[]{:S(2)}) collective-permute-start(bf16[1024,256]{1,0:T(8,128)(2,1)} %bitcast.28), channel_id=1, source_target_pairs={{0,2},{1,3},{2,0},{3,1},{4,6},{5,7},{6,4},{7,5},{8,10},{9,11},{10,... | collective-permute-start | bytes 1572872 | tf_op jit(solution)/shard_map/ppermute | solution.py:307
  31.7 38.4 %collective-permute-start.5 = (bf16[1024,256]{1,0:T(8,128)(2,1)}, bf16[1024,256]{1,0:T(8,128)(2,1)}, u32[]{:S(2)}, u32[]{:S(2)}) collective-permute-start(bf16[1024,256]{1,0:T(8,128)(2,1)} %bitcast.28), channel_id=1, source_target_pairs={{0,3},{1,0},{2,1},{3,2},{4,7},{5,4},{6,5},{7,6},{8,11},{9,8},{10,9... | collective-permute-start | bytes 1572872 | tf_op jit(solution)/shard_map/ppermute | solution.py:307
  34.9 23.1 %collective-permute-start.11 = (bf16[256,256]{1,0:T(8,128)(2,1)S(1)}, bf16[256,256]{1,0:T(8,128)(2,1)S(1)}, u32[]{:S(2)}, u32[]{:S(2)}) collective-permute-start(bf16[256,256]{1,0:T(8,128)(2,1)S(1)} %get-tuple-element.13), channel_id=1, source_target_pairs={{0,3},{1,0},{2,1},{3,2},{4,7},{5,4},{6,5},{7,6},{8,11},{9,8},{10,9... | collective-permute-start | bytes 393224 | tf_op jit(solution)/shard_map/ppermute | solution.py:307
  36.8 28.8 %collective-permute-start.10 = (bf16[256,256]{1,0:T(8,128)(2,1)S(1)}, bf16[256,256]{1,0:T(8,128)(2,1)}, u32[]{:S(2)}, u32[]{:S(2)}) collective-permute-start(bf16[256,256]{1,0:T(8,128)(2,1)S(1)} %get-tuple-element.14), channel_id=1, source_target_pairs={{0,2},{1,3},{2,0},{3,1},{4,6},{5,7},{6,4},{7,5},{8,10},{9,11},{10,... | collective-permute-start | bytes 393224 | tf_op jit(solution)/shard_map/ppermute | solution.py:307
  44.9 25.2 %copy-start.4 = (f32[4,4096]{1,0:T(4,128)}, f32[4,4096]{1,0:T(4,128)S(1)}, u32[]{:S(2)}) copy-start(f32[4,4096]{1,0:T(4,128)S(1)} %broadcast_multiply_fusion.mask.refs_4_) | copy-start | bytes 196612
  58.0 8.7 %collective-permute-start.9 = (bf16[256,256]{1,0:T(8,128)(2,1)S(1)}, bf16[256,256]{1,0:T(8,128)(2,1)S(1)}, u32[]{:S(2)}, u32[]{:S(2)}) collective-permute-start(bf16[256,256]{1,0:T(8,128)(2,1)S(1)} %get-tuple-element.12), channel_id=1, source_target_pairs={{0,1},{1,2},{2,3},{3,0},{4,5},{5,6},{6,7},{7,4},{8,9},{9,10},{10,1... | collective-permute-start | bytes 393224 | tf_op jit(solution)/shard_map/ppermute | solution.py:307
  65.6 8.0 %copy-start = (bf16[128,8,4,256]{3,1,2,0:T(8,128)(2,1)}, bf16[128,8,4,256]{3,1,2,0:T(8,128)(2,1)S(1)}, u32[]{:S(2)}) copy-start(bf16[128,8,4,256]{3,1,2,0:T(8,128)(2,1)S(1)} %copy.21) | copy-start | bytes 6291460
  73.6 14.9 %copy-start.10 = (s32[1,512]{1,0:T(1,128)S(1)}, s32[1,512]{1,0:T(1,128)}, u32[]{:S(2)}) copy-start(s32[1,512]{1,0:T(1,128)} %param.11) | copy-start | bytes 6148
  79.7 60.6 %all-to-all-start.1 = ((bf16[128,64,128]{2,1,0:T(8,128)(2,1)}), bf16[128,64,128]{2,1,0:T(8,128)(2,1)}, u32[]{:S(2)}, u32[]{:S(2)}) async-start(bf16[128,64,128]{2,1,0:T(8,128)(2,1)} %pack.3), calls=%async_computation.1 | async-start | bytes 4194304 | tf_op jit(solution)/shard_map/all_to_all | solution.py:333
  91.7 17.9 %copy-start.1 = (bf16[512,256]{1,0:T(8,128)(2,1)}, bf16[512,256]{1,0:T(8,128)(2,1)S(1)}, u32[]{:S(2)}) copy-start(bf16[512,256]{1,0:T(8,128)(2,1)S(1)} %gather_fusion) | copy-start | bytes 786436
  91.7 10.5 %collective-permute-start = (bf16[512,256]{1,0:T(8,128)(2,1)S(1)}, bf16[512,256]{1,0:T(8,128)(2,1)S(1)}, u32[]{:S(2)}, u32[]{:S(2)}) collective-permute-start(bf16[512,256]{1,0:T(8,128)(2,1)S(1)} %gather_fusion), channel_id=1, source_target_pairs={{0,1},{1,2},{2,3},{3,0},{4,5},{5,6},{6,7},{7,4},{8,9},{9,10},{10,1... | collective-permute-start | bytes 786440 | tf_op jit(solution)/shard_map/ppermute | solution.py:307
  94.8 13.3 %collective-permute-start.1 = (bf16[512,256]{1,0:T(8,128)(2,1)S(1)}, bf16[512,256]{1,0:T(8,128)(2,1)S(1)}, u32[]{:S(2)}, u32[]{:S(2)}) collective-permute-start(bf16[512,256]{1,0:T(8,128)(2,1)S(1)} %gather_fusion), channel_id=1, source_target_pairs={{0,2},{1,3},{2,0},{3,1},{4,6},{5,7},{6,4},{7,5},{8,10},{9,11},{10,... | collective-permute-start | bytes 786440 | tf_op jit(solution)/shard_map/ppermute | solution.py:307
  99.0 10.6 %collective-permute-start.2 = (bf16[512,256]{1,0:T(8,128)(2,1)S(1)}, bf16[512,256]{1,0:T(8,128)(2,1)S(1)}, u32[]{:S(2)}, u32[]{:S(2)}) collective-permute-start(bf16[512,256]{1,0:T(8,128)(2,1)S(1)} %gather_fusion), channel_id=1, source_target_pairs={{0,3},{1,0},{2,1},{3,2},{4,7},{5,4},{6,5},{7,6},{8,11},{9,8},{10,9... | collective-permute-start | bytes 786440 | tf_op jit(solution)/shard_map/ppermute | solution.py:307
  102.3 7.3 %copy-start.12 = (bf16[512,256]{1,0:T(8,128)(2,1)}, bf16[512,256]{1,0:T(8,128)(2,1)S(1)}, u32[]{:S(2)}) copy-start(bf16[512,256]{1,0:T(8,128)(2,1)S(1)} %collective-permute-done.r1) | copy-start | bytes 786436
  120.8 35.7 %copy-start.2 = (bf16[512,256]{1,0:T(8,128)(2,1)S(1)}, bf16[512,256]{1,0:T(8,128)(2,1)}, u32[]{:S(2)}) copy-start(bf16[512,256]{1,0:T(8,128)(2,1)} %copy-done.1) | copy-start | bytes 786436
  120.8 19.5 %collective-permute-start.6 = (bf16[1,512,128]{2,1,0:T(8,128)(2,1)S(1)}, bf16[1,512,128]{2,1,0:T(8,128)(2,1)S(1)}, u32[]{:S(2)}, u32[]{:S(2)}) collective-permute-start(bf16[1,512,128]{2,1,0:T(8,128)(2,1)S(1)} %attend.2.a0), channel_id=1, source_target_pairs={{0,1},{1,2},{2,3},{3,0},{4,5},{5,6},{6,7},{7,4},{8,9},{9,10},{10,1... | collective-permute-start | bytes 393224 | tf_op jit(solution)/shard_map/ppermute | solution.py:307
  126.5 13.8 %collective-permute-start.7 = (bf16[1,512,128]{2,1,0:T(8,128)(2,1)S(1)}, bf16[1,512,128]{2,1,0:T(8,128)(2,1)S(1)}, u32[]{:S(2)}, u32[]{:S(2)}) collective-permute-start(bf16[1,512,128]{2,1,0:T(8,128)(2,1)S(1)} %attend.2.a0), channel_id=1, source_target_pairs={{0,2},{1,3},{2,0},{3,1},{4,6},{5,7},{6,4},{7,5},{8,10},{9,11},{10,... | collective-permute-start | bytes 393224 | tf_op jit(solution)/shard_map/ppermute | solution.py:307
  129.3 11.0 %collective-permute-start.8 = (bf16[1,512,128]{2,1,0:T(8,128)(2,1)S(1)}, bf16[1,512,128]{2,1,0:T(8,128)(2,1)S(1)}, u32[]{:S(2)}, u32[]{:S(2)}) collective-permute-start(bf16[1,512,128]{2,1,0:T(8,128)(2,1)S(1)} %attend.2.a0), channel_id=1, source_target_pairs={{0,3},{1,0},{2,1},{3,2},{4,7},{5,4},{6,5},{7,6},{8,11},{9,8},{10,9... | collective-permute-start | bytes 393224 | tf_op jit(solution)/shard_map/ppermute | solution.py:307
  (5 other events, 14.3 us)

commit v7 on v6

--- a/solution.py
+++ b/solution.py
@@ -105,7 +105,7 @@
             pltpu.VMEM(out_shape, keys.dtype),
             pltpu.SemaphoreType.DMA((3,)),
             pltpu.SemaphoreType.DMA((2,)),
-            pltpu.SemaphoreType.DMA((4,)),
+            pltpu.SemaphoreType.DMA((8,)),
         ],
         compiler_params=pltpu.CompilerParams(vmem_limit_bytes=VMEM),
         cost_estimate=cost(0, 2 * shards * rows * DH * 2),
@@ -228,7 +228,7 @@
             of_head,
         ]
         + [pl.BlockSpec(memory_space=pl.ANY)] * len(after),
-        out_specs=pl.BlockSpec((copies, cands, DH), lambda i: (0, 0, 0)),
+        out_specs=WHOLE,
         scratch_shapes=[
             pltpu.VMEM((cands, n), jnp.bfloat16),
             pltpu.VMEM((cands, DH), jnp.float32),

time: 159 us -> 159 us (level)
  no operation moved by 1% of the time
where the time goes in v7:
time: 159 us; the launch traced here: 158 us
  starting transfers between devices  72 us (45%)
  waiting for transfers between devices  35.1 us (22%)
  Pallas kernels  23.1 us (15%)
  blocking collectives  12.2 us (8%)
  local copies, waits for them, and re-layouts  11.3 us (7%)
  other arithmetic  3.17 us (2%)
    ppermute x12, starting transfers between devices, back(): return lax.ppermute(x, 'mp', [(i, (i + d) % split) for i in range(split)])  44.3 us
    ppermute x12, waiting for transfers between devices, back(): return lax.ppermute(x, 'mp', [(i, (i + d) % split) for i in range(split)])  21.4 us
    all_to_all x1, starting transfers between devices, local(): got_first = exchange(pack(0, *history, cand=cand_feats))  19 us
    all_to_all x1, blocking collectives, local(): last = lax.all_to_all(last, 'mp', split_axis=0, concat_axis=0, tiled=True)  12.2 us
    all_to_all x1, starting transfers between devices, local(): got_second = exchange(pack(1, *history, after=ready))  8.74 us
    pallas_call x2, Pallas kernels, attend(): pl.pallas_call(attend_kernel, out_shape=jax.ShapeDtypeStruct((copies, can...  8.01 us
    all_to_all x1, waiting for transfers between devices, local(): got_second = exchange(pack(1, *history, after=ready))  7.51 us
    pallas_call x2, Pallas kernels, pack(): pl.pallas_call(functools.partial(pack_kernel, head, cand is not None), ou...  6.95 us
  transfers between devices with their start and end apart: 14, of which 6 were waited for; matrix products, arithmetic and copies ran while one was open for 9% of the time, Pallas kernels for 9%

profile of v7, /device:TPU:1, one launch (start us, length us, event | category | flops | bytes accessed | tf_op | source)
XLA Modules:
  0.0 158.3 jit_solution(8137933238765024538)
XLA Ops:
  0.0 3.5 %pack.2 = bf16[128,72,128]{2,1,0:T(8,128)(2,1)} custom-call(s32[128]{0:T(128)} %home_in.3, s32[128,128]{1,0:T(8,128)} %table_in.3, bf16[32,32,256]{2,1,0:T(8,128)(2,1)} %keys_in.3, bf16[32,32,256]{2,1,0:T(8,128)(2,1)} %values_in.3, bf16[512,256]{1,0:T(8,128)(2,1)} %refs_0_.1), custom_call_target="tpu_custom_call" | custom-call | bytes 4718592 | tf_op jit(solution)/shard_map/pack/pallas_call | solution.py:94
  3.5 19.0 %all-to-all-start = ((bf16[128,72,128]{2,1,0:T(8,128)(2,1)}), bf16[128,72,128]{2,1,0:T(8,128)(2,1)}, u32[]{:S(2)}, u32[]{:S(2)}) async-start(bf16[128,72,128]{2,1,0:T(8,128)(2,1)} %pack.2), calls=%async_computation | async-start | bytes 4718592 | tf_op jit(solution)/shard_map/all_to_all | solution.py:313
  24.2 3.1 %collective-permute-start.3 = (bf16[1024,256]{1,0:T(8,128)(2,1)}, bf16[1024,256]{1,0:T(8,128)(2,1)S(1)}, u32[]{:S(2)}, u32[]{:S(2)}) collective-permute-start(bf16[1024,256]{1,0:T(8,128)(2,1)} %bitcast.28), channel_id=1, source_target_pairs={{0,1},{1,2},{2,3},{3,0},{4,5},{5,6},{6,7},{7,4},{8,9},{9,10},{10,1... | collective-permute-start | bytes 1572872 | tf_op jit(solution)/shard_map/ppermute | solution.py:307
  27.3 4.4 %collective-permute-start.4 = (bf16[1024,256]{1,0:T(8,128)(2,1)}, bf16[1024,256]{1,0:T(8,128)(2,1)}, u32[]{:S(2)}, u32[]{:S(2)}) collective-permute-start(bf16[1024,256]{1,0:T(8,128)(2,1)} %bitcast.28), channel_id=1, source_target_pairs={{0,2},{1,3},{2,0},{3,1},{4,6},{5,7},{6,4},{7,5},{8,10},{9,11},{10,... | collective-permute-start | bytes 1572872 | tf_op jit(solution)/shard_map/ppermute | solution.py:307
  31.6 3.1 %collective-permute-start.5 = (bf16[1024,256]{1,0:T(8,128)(2,1)}, bf16[1024,256]{1,0:T(8,128)(2,1)}, u32[]{:S(2)}, u32[]{:S(2)}) collective-permute-start(bf16[1024,256]{1,0:T(8,128)(2,1)} %bitcast.28), channel_id=1, source_target_pairs={{0,3},{1,0},{2,1},{3,2},{4,7},{5,4},{6,5},{7,6},{8,11},{9,8},{10,9... | collective-permute-start | bytes 1572872 | tf_op jit(solution)/shard_map/ppermute | solution.py:307
  36.8 4.0 %collective-permute-start.10 = (bf16[256,256]{1,0:T(8,128)(2,1)S(1)}, bf16[256,256]{1,0:T(8,128)(2,1)}, u32[]{:S(2)}, u32[]{:S(2)}) collective-permute-start(bf16[256,256]{1,0:T(8,128)(2,1)S(1)} %get-tuple-element.14), channel_id=1, source_target_pairs={{0,2},{1,3},{2,0},{3,1},{4,6},{5,7},{6,4},{7,5},{8,10},{9,11},{10,... | collective-permute-start | bytes 393224 | tf_op jit(solution)/shard_map/ppermute | solution.py:307
  44.8 13.1 %collective-permute-done.11 = bf16[256,256]{1,0:T(8,128)(2,1)S(1)} collective-permute-done((bf16[256,256]{1,0:T(8,128)(2,1)S(1)}, bf16[256,256]{1,0:T(8,128)(2,1)S(1)}, u32[]{:S(2)}, u32[]{:S(2)}) %collective-permute-start.11) | collective-permute-done | bytes 131104 | tf_op jit(solution)/shard_map/ppermute | solution.py:307
  57.9 5.4 %collective-permute-start.9 = (bf16[256,256]{1,0:T(8,128)(2,1)S(1)}, bf16[256,256]{1,0:T(8,128)(2,1)S(1)}, u32[]{:S(2)}, u32[]{:S(2)}) collective-permute-start(bf16[256,256]{1,0:T(8,128)(2,1)S(1)} %get-tuple-element.12), channel_id=1, source_target_pairs={{0,1},{1,2},{2,3},{3,0},{4,5},{5,6},{6,7},{7,4},{8,9},{9,10},{10,1... | collective-permute-start | bytes 393224 | tf_op jit(solution)/shard_map/ppermute | solution.py:307
  63.4 2.1 %copy.21 = bf16[128,8,4,256]{3,1,2,0:T(8,128)(2,1)S(1)} copy(bf16[128,8,4,256]{3,2,1,0:T(4,128)(2,1)} %bitcast.34) | data formatting | bytes 4194304
  70.1 3.4 %pack.3 = bf16[128,64,128]{2,1,0:T(8,128)(2,1)} custom-call(s32[128]{0:T(128)} %home_in.3, s32[128,128]{1,0:T(8,128)} %table_in.3, bf16[32,32,256]{2,1,0:T(8,128)(2,1)} %keys_in.3, bf16[32,32,256]{2,1,0:T(8,128)(2,1)} %values_in.3, bf16[1024,256]{1,0:T(8,128)(2,1)S(1)} %collective-permute-done.3.g1.refs_0_, ...), custom_call_target="tpu_custom_call" | custom-call | bytes 4194304 | tf_op jit(solution)/shard_map/pack/pallas_call | solution.py:94
  73.6 6.1 %all-to-all-done.got = bf16[128,72,128]{2,1,0:T(8,128)(2,1)} async-done(((bf16[128,72,128]{2,1,0:T(8,128)(2,1)}), bf16[128,72,128]{2,1,0:T(8,128)(2,1)}, u32[]{:S(2)}, u32[]{:S(2)}) %all-to-all-start) | async-done | bytes 2359328 | tf_op jit(solution)/shard_map/all_to_all | solution.py:313
  79.7 8.7 %all-to-all-start.1 = ((bf16[128,64,128]{2,1,0:T(8,128)(2,1)}), bf16[128,64,128]{2,1,0:T(8,128)(2,1)}, u32[]{:S(2)}, u32[]{:S(2)}) async-start(bf16[128,64,128]{2,1,0:T(8,128)(2,1)} %pack.3), calls=%async_computation.1 | async-start | bytes 4194304 | tf_op jit(solution)/shard_map/all_to_all | solution.py:333
  91.7 3.1 %collective-permute-start = (bf16[512,256]{1,0:T(8,128)(2,1)S(1)}, bf16[512,256]{1,0:T(8,128)(2,1)S(1)}, u32[]{:S(2)}, u32[]{:S(2)}) collective-permute-start(bf16[512,256]{1,0:T(8,128)(2,1)S(1)} %gather_fusion), channel_id=1, source_target_pairs={{0,1},{1,2},{2,3},{3,0},{4,5},{5,6},{6,7},{7,4},{8,9},{9,10},{10,1... | collective-permute-start | bytes 786440 | tf_op jit(solution)/shard_map/ppermute | solution.py:307
  94.8 4.2 %collective-permute-start.1 = (bf16[512,256]{1,0:T(8,128)(2,1)S(1)}, bf16[512,256]{1,0:T(8,128)(2,1)S(1)}, u32[]{:S(2)}, u32[]{:S(2)}) collective-permute-start(bf16[512,256]{1,0:T(8,128)(2,1)S(1)} %gather_fusion), channel_id=1, source_target_pairs={{0,2},{1,3},{2,0},{3,1},{4,6},{5,7},{6,4},{7,5},{8,10},{9,11},{10,... | collective-permute-start | bytes 786440 | tf_op jit(solution)/shard_map/ppermute | solution.py:307
  99.0 3.2 %collective-permute-start.2 = (bf16[512,256]{1,0:T(8,128)(2,1)S(1)}, bf16[512,256]{1,0:T(8,128)(2,1)S(1)}, u32[]{:S(2)}, u32[]{:S(2)}) collective-permute-start(bf16[512,256]{1,0:T(8,128)(2,1)S(1)} %gather_fusion), channel_id=1, source_target_pairs={{0,3},{1,0},{2,1},{3,2},{4,7},{5,4},{6,5},{7,6},{8,11},{9,8},{10,9... | collective-permute-start | bytes 786440 | tf_op jit(solution)/shard_map/ppermute | solution.py:307
  102.3 5.9 %collective-permute-done.1.r2 = bf16[512,256]{1,0:T(8,128)(2,1)S(1)} collective-permute-done((bf16[512,256]{1,0:T(8,128)(2,1)S(1)}, bf16[512,256]{1,0:T(8,128)(2,1)S(1)}, u32[]{:S(2)}, u32[]{:S(2)}) %collective-permute-start.1) | collective-permute-done | bytes 262176 | tf_op jit(solution)/shard_map/ppermute | solution.py:307
  110.3 6.5 %project.1 = (bf16[4,512,256]{2,1,0:T(8,128)(2,1)S(1)}, bf16[2,512,128]{2,1,0:T(8,128)(2,1)}, f32[2,512,128]{2,1,0:T(8,128)}) custom-call(bf16[512,256]{1,0:T(8,128)(2,1)} %copy-done.1, bf16[512,256]{1,0:T(8,128)(2,1)} %copy-done.12, bf16[512,256]{1,0:T(8,128)(2,1)} %copy-done.13, bf16[512,256]{1,0:T(8,128)(2,1)} %copy-done.14, bf16[1024,1024]{1,0:T(8,128)(2,1)} %bitcast.32, ...), custom_call_target="tpu_custom_call" | custom-call | flops 1879048192 | bytes 8388608 | tf_op jit(solution)/shard_map/project/pallas_call | solution.py:164
  116.8 4.0 %attend.2.a0 = bf16[1,512,128]{2,1,0:T(8,128)(2,1)S(1)} custom-call(bf16[2,512,128]{2,1,0:T(8,128)(2,1)} %get-tuple-element.8.query, bf16[128,72,128]{2,1,0:T(8,128)(2,1)} %all-to-all-done.got, f32[4,4096]{1,0:T(4,128)} %copy-done.4, f32[2,512,128]{2,1,0:T(8,128)} %get-tuple-element.9.own), custom_call_target="tpu_custom_call" | custom-call | flops 1073741824 | bytes 4194304 | tf_op jit(solution)/shard_map/attend/pallas_call | solution.py:220
  120.8 5.7 %collective-permute-start.6 = (bf16[1,512,128]{2,1,0:T(8,128)(2,1)S(1)}, bf16[1,512,128]{2,1,0:T(8,128)(2,1)S(1)}, u32[]{:S(2)}, u32[]{:S(2)}) collective-permute-start(bf16[1,512,128]{2,1,0:T(8,128)(2,1)S(1)} %attend.2.a0), channel_id=1, source_target_pairs={{0,1},{1,2},{2,3},{3,0},{4,5},{5,6},{6,7},{7,4},{8,9},{9,10},{10,1... | collective-permute-start | bytes 393224 | tf_op jit(solution)/shard_map/ppermute | solution.py:307
  126.5 2.7 %collective-permute-start.7 = (bf16[1,512,128]{2,1,0:T(8,128)(2,1)S(1)}, bf16[1,512,128]{2,1,0:T(8,128)(2,1)S(1)}, u32[]{:S(2)}, u32[]{:S(2)}) collective-permute-start(bf16[1,512,128]{2,1,0:T(8,128)(2,1)S(1)} %attend.2.a0), channel_id=1, source_target_pairs={{0,2},{1,3},{2,0},{3,1},{4,6},{5,7},{6,4},{7,5},{8,10},{9,11},{10,... | collective-permute-start | bytes 393224 | tf_op jit(solution)/shard_map/ppermute | solution.py:307
  129.2 3.5 %collective-permute-start.8 = (bf16[1,512,128]{2,1,0:T(8,128)(2,1)S(1)}, bf16[1,512,128]{2,1,0:T(8,128)(2,1)S(1)}, u32[]{:S(2)}, u32[]{:S(2)}) collective-permute-start(bf16[1,512,128]{2,1,0:T(8,128)(2,1)S(1)} %attend.2.a0), channel_id=1, source_target_pairs={{0,3},{1,0},{2,1},{3,2},{4,7},{5,4},{6,5},{7,6},{8,11},{9,8},{10,9... | collective-permute-start | bytes 393224 | tf_op jit(solution)/shard_map/ppermute | solution.py:307
  132.7 7.5 %all-to-all-done.1.got = bf16[128,64,128]{2,1,0:T(8,128)(2,1)} async-done(((bf16[128,64,128]{2,1,0:T(8,128)(2,1)}), bf16[128,64,128]{2,1,0:T(8,128)(2,1)}, u32[]{:S(2)}, u32[]{:S(2)}) %all-to-all-start.1) | async-done | bytes 2097184 | tf_op jit(solution)/shard_map/all_to_all | solution.py:333
  140.3 4.0 %attend.3 = bf16[4,512,128]{2,1,0:T(8,128)(2,1)S(1)} custom-call(bf16[2,512,128]{2,1,0:T(8,128)(2,1)} %get-tuple-element.8.query, bf16[128,64,128]{2,1,0:T(8,128)(2,1)} %all-to-all-done.1.got, f32[4,4096]{1,0:T(4,128)} %copy-done.4, f32[2,512,128]{2,1,0:T(8,128)} %get-tuple-element.9.own, bf16[1,512,128]{2,1,0:T(8,128)(2,1)S(1)} %collective-permute-done.6.refs_0_.a1, ...), custom_call_target="tpu_custom_call" | custom-call | flops 1073741824 | bytes 4194304 | tf_op jit(solution)/shard_map/attend/pallas_call | solution.py:220
  144.3 12.2 %all_to_all.15.last = bf16[4,512,128]{2,1,0:T(8,128)(2,1)S(1)} all-to-all(bf16[4,512,128]{2,1,0:T(8,128)(2,1)S(1)} %attend.3), channel_id=1, replica_groups=mesh['req'=128,'mp'=4] {'mp'}, dimensions={0} | all-to-all | bytes 1048576 | tf_op jit(solution)/shard_map/all_to_all | solution.py:348
  (70 shorter events, 18.3 us)
Async XLA Ops:
  3.5 19.0 %copy-start.5 = (bf16[1024,4,256]{2,1,0:T(4,128)(2,1)S(1)}, bf16[1024,4,256]{2,1,0:T(4,128)(2,1)}, u32[]{:S(2)}) copy-start(bf16[1024,4,256]{2,1,0:T(4,128)(2,1)} %param.12) | copy-start | bytes 6291460
  3.5 76.2 %all-to-all-start = ((bf16[128,72,128]{2,1,0:T(8,128)(2,1)}), bf16[128,72,128]{2,1,0:T(8,128)(2,1)}, u32[]{:S(2)}, u32[]{:S(2)}) async-start(bf16[128,72,128]{2,1,0:T(8,128)(2,1)} %pack.2), calls=%async_computation | async-start | bytes 4718592 | tf_op jit(solution)/shard_map/all_to_all | solution.py:313
  22.5 12.3 %copy-start.6 = (bf16[256,1024]{1,0:T(8,128)(2,1)S(1)}, bf16[256,1024]{1,0:T(8,128)(2,1)}, u32[]{:S(2)}) copy-start(bf16[256,1024]{1,0:T(8,128)(2,1)} %param.13) | copy-start | bytes 1572868
  22.5 18.3 %copy-start.9 = (s32[1,4,128]{2,1,0:T(4,128)S(1)}, s32[1,4,128]{2,1,0:T(4,128)}, u32[]{:S(2)}) copy-start(s32[1,4,128]{2,1,0:T(4,128)} %param.19) | copy-start | bytes 6148
  22.5 18.4 %copy-start.11 = (s32[128]{0:T(128)S(1)}, s32[128]{0:T(128)}, u32[]{:S(2)}) copy-start(s32[128]{0:T(128)} %home_in.3) | copy-start | bytes 1540
  24.2 45.9 %collective-permute-start.3 = (bf16[1024,256]{1,0:T(8,128)(2,1)}, bf16[1024,256]{1,0:T(8,128)(2,1)S(1)}, u32[]{:S(2)}, u32[]{:S(2)}) collective-permute-start(bf16[1024,256]{1,0:T(8,128)(2,1)} %bitcast.28), channel_id=1, source_target_pairs={{0,1},{1,2},{2,3},{3,0},{4,5},{5,6},{6,7},{7,4},{8,9},{9,10},{10,1... | collective-permute-start | bytes 1572872 | tf_op jit(solution)/shard_map/ppermute | solution.py:307
  27.3 42.8 %collective-permute-start.4 = (bf16[1024,256]{1,0:T(8,128)(2,1)}, bf16[1024,256]{1,0:T(8,128)(2,1)}, u32[]{:S(2)}, u32[]{:S(2)}) collective-permute-start(bf16[1024,256]{1,0:T(8,128)(2,1)} %bitcast.28), channel_id=1, source_target_pairs={{0,2},{1,3},{2,0},{3,1},{4,6},{5,7},{6,4},{7,5},{8,10},{9,11},{10,... | collective-permute-start | bytes 1572872 | tf_op jit(solution)/shard_map/ppermute | solution.py:307
  31.6 38.4 %collective-permute-start.5 = (bf16[1024,256]{1,0:T(8,128)(2,1)}, bf16[1024,256]{1,0:T(8,128)(2,1)}, u32[]{:S(2)}, u32[]{:S(2)}) collective-permute-start(bf16[1024,256]{1,0:T(8,128)(2,1)} %bitcast.28), channel_id=1, source_target_pairs={{0,3},{1,0},{2,1},{3,2},{4,7},{5,4},{6,5},{7,6},{8,11},{9,8},{10,9... | collective-permute-start | bytes 1572872 | tf_op jit(solution)/shard_map/ppermute | solution.py:307
  34.9 23.1 %collective-permute-start.11 = (bf16[256,256]{1,0:T(8,128)(2,1)S(1)}, bf16[256,256]{1,0:T(8,128)(2,1)S(1)}, u32[]{:S(2)}, u32[]{:S(2)}) collective-permute-start(bf16[256,256]{1,0:T(8,128)(2,1)S(1)} %get-tuple-element.13), channel_id=1, source_target_pairs={{0,3},{1,0},{2,1},{3,2},{4,7},{5,4},{6,5},{7,6},{8,11},{9,8},{10,9... | collective-permute-start | bytes 393224 | tf_op jit(solution)/shard_map/ppermute | solution.py:307
  36.8 28.8 %collective-permute-start.10 = (bf16[256,256]{1,0:T(8,128)(2,1)S(1)}, bf16[256,256]{1,0:T(8,128)(2,1)}, u32[]{:S(2)}, u32[]{:S(2)}) collective-permute-start(bf16[256,256]{1,0:T(8,128)(2,1)S(1)} %get-tuple-element.14), channel_id=1, source_target_pairs={{0,2},{1,3},{2,0},{3,1},{4,6},{5,7},{6,4},{7,5},{8,10},{9,11},{10,... | collective-permute-start | bytes 393224 | tf_op jit(solution)/shard_map/ppermute | solution.py:307
  44.8 25.2 %copy-start.4 = (f32[4,4096]{1,0:T(4,128)}, f32[4,4096]{1,0:T(4,128)S(1)}, u32[]{:S(2)}) copy-start(f32[4,4096]{1,0:T(4,128)S(1)} %broadcast_multiply_fusion.mask.refs_4_) | copy-start | bytes 196612
  57.9 8.7 %collective-permute-start.9 = (bf16[256,256]{1,0:T(8,128)(2,1)S(1)}, bf16[256,256]{1,0:T(8,128)(2,1)S(1)}, u32[]{:S(2)}, u32[]{:S(2)}) collective-permute-start(bf16[256,256]{1,0:T(8,128)(2,1)S(1)} %get-tuple-element.12), channel_id=1, source_target_pairs={{0,1},{1,2},{2,3},{3,0},{4,5},{5,6},{6,7},{7,4},{8,9},{9,10},{10,1... | collective-permute-start | bytes 393224 | tf_op jit(solution)/shard_map/ppermute | solution.py:307
  65.6 8.0 %copy-start = (bf16[128,8,4,256]{3,1,2,0:T(8,128)(2,1)}, bf16[128,8,4,256]{3,1,2,0:T(8,128)(2,1)S(1)}, u32[]{:S(2)}) copy-start(bf16[128,8,4,256]{3,1,2,0:T(8,128)(2,1)S(1)} %copy.21) | copy-start | bytes 6291460
  73.6 14.9 %copy-start.10 = (s32[1,512]{1,0:T(1,128)S(1)}, s32[1,512]{1,0:T(1,128)}, u32[]{:S(2)}) copy-start(s32[1,512]{1,0:T(1,128)} %param.11) | copy-start | bytes 6148
  79.7 60.5 %all-to-all-start.1 = ((bf16[128,64,128]{2,1,0:T(8,128)(2,1)}), bf16[128,64,128]{2,1,0:T(8,128)(2,1)}, u32[]{:S(2)}, u32[]{:S(2)}) async-start(bf16[128,64,128]{2,1,0:T(8,128)(2,1)} %pack.3), calls=%async_computation.1 | async-start | bytes 4194304 | tf_op jit(solution)/shard_map/all_to_all | solution.py:333
  91.7 17.9 %copy-start.1 = (bf16[512,256]{1,0:T(8,128)(2,1)}, bf16[512,256]{1,0:T(8,128)(2,1)S(1)}, u32[]{:S(2)}) copy-start(bf16[512,256]{1,0:T(8,128)(2,1)S(1)} %gather_fusion) | copy-start | bytes 786436
  91.7 10.6 %collective-permute-start = (bf16[512,256]{1,0:T(8,128)(2,1)S(1)}, bf16[512,256]{1,0:T(8,128)(2,1)S(1)}, u32[]{:S(2)}, u32[]{:S(2)}) collective-permute-start(bf16[512,256]{1,0:T(8,128)(2,1)S(1)} %gather_fusion), channel_id=1, source_target_pairs={{0,1},{1,2},{2,3},{3,0},{4,5},{5,6},{6,7},{7,4},{8,9},{9,10},{10,1... | collective-permute-start | bytes 786440 | tf_op jit(solution)/shard_map/ppermute | solution.py:307
  94.8 13.4 %collective-permute-start.1 = (bf16[512,256]{1,0:T(8,128)(2,1)S(1)}, bf16[512,256]{1,0:T(8,128)(2,1)S(1)}, u32[]{:S(2)}, u32[]{:S(2)}) collective-permute-start(bf16[512,256]{1,0:T(8,128)(2,1)S(1)} %gather_fusion), channel_id=1, source_target_pairs={{0,2},{1,3},{2,0},{3,1},{4,6},{5,7},{6,4},{7,5},{8,10},{9,11},{10,... | collective-permute-start | bytes 786440 | tf_op jit(solution)/shard_map/ppermute | solution.py:307
  99.0 10.6 %collective-permute-start.2 = (bf16[512,256]{1,0:T(8,128)(2,1)S(1)}, bf16[512,256]{1,0:T(8,128)(2,1)S(1)}, u32[]{:S(2)}, u32[]{:S(2)}) collective-permute-start(bf16[512,256]{1,0:T(8,128)(2,1)S(1)} %gather_fusion), channel_id=1, source_target_pairs={{0,3},{1,0},{2,1},{3,2},{4,7},{5,4},{6,5},{7,6},{8,11},{9,8},{10,9... | collective-permute-start | bytes 786440 | tf_op jit(solution)/shard_map/ppermute | solution.py:307
  102.3 7.3 %copy-start.12 = (bf16[512,256]{1,0:T(8,128)(2,1)}, bf16[512,256]{1,0:T(8,128)(2,1)S(1)}, u32[]{:S(2)}) copy-start(bf16[512,256]{1,0:T(8,128)(2,1)S(1)} %collective-permute-done.r1) | copy-start | bytes 786436
  120.8 35.7 %copy-start.2 = (bf16[512,256]{1,0:T(8,128)(2,1)S(1)}, bf16[512,256]{1,0:T(8,128)(2,1)}, u32[]{:S(2)}) copy-start(bf16[512,256]{1,0:T(8,128)(2,1)} %copy-done.1) | copy-start | bytes 786436
  120.8 19.5 %collective-permute-start.6 = (bf16[1,512,128]{2,1,0:T(8,128)(2,1)S(1)}, bf16[1,512,128]{2,1,0:T(8,128)(2,1)S(1)}, u32[]{:S(2)}, u32[]{:S(2)}) collective-permute-start(bf16[1,512,128]{2,1,0:T(8,128)(2,1)S(1)} %attend.2.a0), channel_id=1, source_target_pairs={{0,1},{1,2},{2,3},{3,0},{4,5},{5,6},{6,7},{7,4},{8,9},{9,10},{10,1... | collective-permute-start | bytes 393224 | tf_op jit(solution)/shard_map/ppermute | solution.py:307
  126.5 13.8 %collective-permute-start.7 = (bf16[1,512,128]{2,1,0:T(8,128)(2,1)S(1)}, bf16[1,512,128]{2,1,0:T(8,128)(2,1)S(1)}, u32[]{:S(2)}, u32[]{:S(2)}) collective-permute-start(bf16[1,512,128]{2,1,0:T(8,128)(2,1)S(1)} %attend.2.a0), channel_id=1, source_target_pairs={{0,2},{1,3},{2,0},{3,1},{4,6},{5,7},{6,4},{7,5},{8,10},{9,11},{10,... | collective-permute-start | bytes 393224 | tf_op jit(solution)/shard_map/ppermute | solution.py:307
  129.2 11.1 %collective-permute-start.8 = (bf16[1,512,128]{2,1,0:T(8,128)(2,1)S(1)}, bf16[1,512,128]{2,1,0:T(8,128)(2,1)S(1)}, u32[]{:S(2)}, u32[]{:S(2)}) collective-permute-start(bf16[1,512,128]{2,1,0:T(8,128)(2,1)S(1)} %attend.2.a0), channel_id=1, source_target_pairs={{0,3},{1,0},{2,1},{3,2},{4,7},{5,4},{6,5},{7,6},{8,11},{9,8},{10,9... | collective-permute-start | bytes 393224 | tf_op jit(solution)/shard_map/ppermute | solution.py:307
  (5 other events, 14.3 us)

commit v8 on v7

--- a/solution.py
+++ b/solution.py
@@ -52,7 +52,7 @@
         pltpu.make_async_copy(a.at[:, :, cols], b, load_sem.at[i])
         for i, (a, b) in enumerate(((keys_in, keys), (values_in, values)))
     ]
-    for load in indices[2:] + indices[:2] + blocks:
+    for load in [indices[1], indices[0], *indices[2:], *blocks]:
         load.start()
     shards, rows, _ = made.shape
     if with_rows:

time: 159 us -> 159 us (level)
  no operation moved by 1% of the time
where the time goes in v8:
time: 159 us; the launch traced here: 158 us
  starting transfers between devices  72 us (45%)
  waiting for transfers between devices  35.1 us (22%)
  Pallas kernels  23 us (14%)
  blocking collectives  12.2 us (8%)
  local copies, waits for them, and re-layouts  11.3 us (7%)
  other arithmetic  3.17 us (2%)
    ppermute x12, starting transfers between devices, back(): return lax.ppermute(x, 'mp', [(i, (i + d) % split) for i in range(split)])  44.3 us
    ppermute x12, waiting for transfers between devices, back(): return lax.ppermute(x, 'mp', [(i, (i + d) % split) for i in range(split)])  21.4 us
    all_to_all x1, starting transfers between devices, local(): got_first = exchange(pack(0, *history, cand=cand_feats))  19 us
    all_to_all x1, blocking collectives, local(): last = lax.all_to_all(last, 'mp', split_axis=0, concat_axis=0, tiled=True)  12.2 us
    all_to_all x1, starting transfers between devices, local(): got_second = exchange(pack(1, *history, after=ready))  8.74 us
    pallas_call x2, Pallas kernels, attend(): pl.pallas_call(attend_kernel, out_shape=jax.ShapeDtypeStruct((copies, can...  8.01 us
    all_to_all x1, waiting for transfers between devices, local(): got_second = exchange(pack(1, *history, after=ready))  7.52 us
    pallas_call x2, Pallas kernels, pack(): pl.pallas_call(functools.partial(pack_kernel, head, cand is not None), ou...  6.83 us
  transfers between devices with their start and end apart: 14, of which 6 were waited for; matrix products, arithmetic and copies ran while one was open for 9% of the time, Pallas kernels for 9%

profile of v8, /device:TPU:1, one launch (start us, length us, event | category | flops | bytes accessed | tf_op | source)
XLA Modules:
  0.0 158.2 jit_solution(12092372577637159877)
XLA Ops:
  0.0 3.4 %pack.2 = bf16[128,72,128]{2,1,0:T(8,128)(2,1)} custom-call(s32[128]{0:T(128)} %home_in.3, s32[128,128]{1,0:T(8,128)} %table_in.3, bf16[32,32,256]{2,1,0:T(8,128)(2,1)} %keys_in.3, bf16[32,32,256]{2,1,0:T(8,128)(2,1)} %values_in.3, bf16[512,256]{1,0:T(8,128)(2,1)} %refs_0_.1), custom_call_target="tpu_custom_call" | custom-call | bytes 4718592 | tf_op jit(solution)/shard_map/pack/pallas_call | solution.py:94
  3.4 19.0 %all-to-all-start = ((bf16[128,72,128]{2,1,0:T(8,128)(2,1)}), bf16[128,72,128]{2,1,0:T(8,128)(2,1)}, u32[]{:S(2)}, u32[]{:S(2)}) async-start(bf16[128,72,128]{2,1,0:T(8,128)(2,1)} %pack.2), calls=%async_computation | async-start | bytes 4718592 | tf_op jit(solution)/shard_map/all_to_all | solution.py:313
  24.0 3.1 %collective-permute-start.3 = (bf16[1024,256]{1,0:T(8,128)(2,1)}, bf16[1024,256]{1,0:T(8,128)(2,1)S(1)}, u32[]{:S(2)}, u32[]{:S(2)}) collective-permute-start(bf16[1024,256]{1,0:T(8,128)(2,1)} %bitcast.28), channel_id=1, source_target_pairs={{0,1},{1,2},{2,3},{3,0},{4,5},{5,6},{6,7},{7,4},{8,9},{9,10},{10,1... | collective-permute-start | bytes 1572872 | tf_op jit(solution)/shard_map/ppermute | solution.py:307
  27.1 4.4 %collective-permute-start.4 = (bf16[1024,256]{1,0:T(8,128)(2,1)}, bf16[1024,256]{1,0:T(8,128)(2,1)}, u32[]{:S(2)}, u32[]{:S(2)}) collective-permute-start(bf16[1024,256]{1,0:T(8,128)(2,1)} %bitcast.28), channel_id=1, source_target_pairs={{0,2},{1,3},{2,0},{3,1},{4,6},{5,7},{6,4},{7,5},{8,10},{9,11},{10,... | collective-permute-start | bytes 1572872 | tf_op jit(solution)/shard_map/ppermute | solution.py:307
  31.5 3.1 %collective-permute-start.5 = (bf16[1024,256]{1,0:T(8,128)(2,1)}, bf16[1024,256]{1,0:T(8,128)(2,1)}, u32[]{:S(2)}, u32[]{:S(2)}) collective-permute-start(bf16[1024,256]{1,0:T(8,128)(2,1)} %bitcast.28), channel_id=1, source_target_pairs={{0,3},{1,0},{2,1},{3,2},{4,7},{5,4},{6,5},{7,6},{8,11},{9,8},{10,9... | collective-permute-start | bytes 1572872 | tf_op jit(solution)/shard_map/ppermute | solution.py:307
  36.7 4.0 %collective-permute-start.10 = (bf16[256,256]{1,0:T(8,128)(2,1)S(1)}, bf16[256,256]{1,0:T(8,128)(2,1)}, u32[]{:S(2)}, u32[]{:S(2)}) collective-permute-start(bf16[256,256]{1,0:T(8,128)(2,1)S(1)} %get-tuple-element.14), channel_id=1, source_target_pairs={{0,2},{1,3},{2,0},{3,1},{4,6},{5,7},{6,4},{7,5},{8,10},{9,11},{10,... | collective-permute-start | bytes 393224 | tf_op jit(solution)/shard_map/ppermute | solution.py:307
  44.7 13.1 %collective-permute-done.11 = bf16[256,256]{1,0:T(8,128)(2,1)S(1)} collective-permute-done((bf16[256,256]{1,0:T(8,128)(2,1)S(1)}, bf16[256,256]{1,0:T(8,128)(2,1)S(1)}, u32[]{:S(2)}, u32[]{:S(2)}) %collective-permute-start.11) | collective-permute-done | bytes 131104 | tf_op jit(solution)/shard_map/ppermute | solution.py:307
  57.8 5.4 %collective-permute-start.9 = (bf16[256,256]{1,0:T(8,128)(2,1)S(1)}, bf16[256,256]{1,0:T(8,128)(2,1)S(1)}, u32[]{:S(2)}, u32[]{:S(2)}) collective-permute-start(bf16[256,256]{1,0:T(8,128)(2,1)S(1)} %get-tuple-element.12), channel_id=1, source_target_pairs={{0,1},{1,2},{2,3},{3,0},{4,5},{5,6},{6,7},{7,4},{8,9},{9,10},{10,1... | collective-permute-start | bytes 393224 | tf_op jit(solution)/shard_map/ppermute | solution.py:307
  63.3 2.1 %copy.21 = bf16[128,8,4,256]{3,1,2,0:T(8,128)(2,1)S(1)} copy(bf16[128,8,4,256]{3,2,1,0:T(4,128)(2,1)} %bitcast.34) | data formatting | bytes 4194304
  70.0 3.5 %pack.3 = bf16[128,64,128]{2,1,0:T(8,128)(2,1)} custom-call(s32[128]{0:T(128)} %home_in.3, s32[128,128]{1,0:T(8,128)} %table_in.3, bf16[32,32,256]{2,1,0:T(8,128)(2,1)} %keys_in.3, bf16[32,32,256]{2,1,0:T(8,128)(2,1)} %values_in.3, bf16[1024,256]{1,0:T(8,128)(2,1)S(1)} %collective-permute-done.3.g1.refs_0_, ...), custom_call_target="tpu_custom_call" | custom-call | bytes 4194304 | tf_op jit(solution)/shard_map/pack/pallas_call | solution.py:94
  73.5 6.1 %all-to-all-done.got = bf16[128,72,128]{2,1,0:T(8,128)(2,1)} async-done(((bf16[128,72,128]{2,1,0:T(8,128)(2,1)}), bf16[128,72,128]{2,1,0:T(8,128)(2,1)}, u32[]{:S(2)}, u32[]{:S(2)}) %all-to-all-start) | async-done | bytes 2359328 | tf_op jit(solution)/shard_map/all_to_all | solution.py:313
  79.6 8.7 %all-to-all-start.1 = ((bf16[128,64,128]{2,1,0:T(8,128)(2,1)}), bf16[128,64,128]{2,1,0:T(8,128)(2,1)}, u32[]{:S(2)}, u32[]{:S(2)}) async-start(bf16[128,64,128]{2,1,0:T(8,128)(2,1)} %pack.3), calls=%async_computation.1 | async-start | bytes 4194304 | tf_op jit(solution)/shard_map/all_to_all | solution.py:333
  91.6 3.1 %collective-permute-start = (bf16[512,256]{1,0:T(8,128)(2,1)S(1)}, bf16[512,256]{1,0:T(8,128)(2,1)S(1)}, u32[]{:S(2)}, u32[]{:S(2)}) collective-permute-start(bf16[512,256]{1,0:T(8,128)(2,1)S(1)} %gather_fusion), channel_id=1, source_target_pairs={{0,1},{1,2},{2,3},{3,0},{4,5},{5,6},{6,7},{7,4},{8,9},{9,10},{10,1... | collective-permute-start | bytes 786440 | tf_op jit(solution)/shard_map/ppermute | solution.py:307
  94.7 4.2 %collective-permute-start.1 = (bf16[512,256]{1,0:T(8,128)(2,1)S(1)}, bf16[512,256]{1,0:T(8,128)(2,1)S(1)}, u32[]{:S(2)}, u32[]{:S(2)}) collective-permute-start(bf16[512,256]{1,0:T(8,128)(2,1)S(1)} %gather_fusion), channel_id=1, source_target_pairs={{0,2},{1,3},{2,0},{3,1},{4,6},{5,7},{6,4},{7,5},{8,10},{9,11},{10,... | collective-permute-start | bytes 786440 | tf_op jit(solution)/shard_map/ppermute | solution.py:307
  98.9 3.2 %collective-permute-start.2 = (bf16[512,256]{1,0:T(8,128)(2,1)S(1)}, bf16[512,256]{1,0:T(8,128)(2,1)S(1)}, u32[]{:S(2)}, u32[]{:S(2)}) collective-permute-start(bf16[512,256]{1,0:T(8,128)(2,1)S(1)} %gather_fusion), channel_id=1, source_target_pairs={{0,3},{1,0},{2,1},{3,2},{4,7},{5,4},{6,5},{7,6},{8,11},{9,8},{10,9... | collective-permute-start | bytes 786440 | tf_op jit(solution)/shard_map/ppermute | solution.py:307
  102.2 5.9 %collective-permute-done.1.r2 = bf16[512,256]{1,0:T(8,128)(2,1)S(1)} collective-permute-done((bf16[512,256]{1,0:T(8,128)(2,1)S(1)}, bf16[512,256]{1,0:T(8,128)(2,1)S(1)}, u32[]{:S(2)}, u32[]{:S(2)}) %collective-permute-start.1) | collective-permute-done | bytes 262176 | tf_op jit(solution)/shard_map/ppermute | solution.py:307
  110.2 6.5 %project.1 = (bf16[4,512,256]{2,1,0:T(8,128)(2,1)S(1)}, bf16[2,512,128]{2,1,0:T(8,128)(2,1)}, f32[2,512,128]{2,1,0:T(8,128)}) custom-call(bf16[512,256]{1,0:T(8,128)(2,1)} %copy-done.1, bf16[512,256]{1,0:T(8,128)(2,1)} %copy-done.12, bf16[512,256]{1,0:T(8,128)(2,1)} %copy-done.13, bf16[512,256]{1,0:T(8,128)(2,1)} %copy-done.14, bf16[1024,1024]{1,0:T(8,128)(2,1)} %bitcast.32, ...), custom_call_target="tpu_custom_call" | custom-call | flops 1879048192 | bytes 8388608 | tf_op jit(solution)/shard_map/project/pallas_call | solution.py:164
  116.7 4.0 %attend.2.a0 = bf16[1,512,128]{2,1,0:T(8,128)(2,1)S(1)} custom-call(bf16[2,512,128]{2,1,0:T(8,128)(2,1)} %get-tuple-element.8.query, bf16[128,72,128]{2,1,0:T(8,128)(2,1)} %all-to-all-done.got, f32[4,4096]{1,0:T(4,128)} %copy-done.4, f32[2,512,128]{2,1,0:T(8,128)} %get-tuple-element.9.own), custom_call_target="tpu_custom_call" | custom-call | flops 1073741824 | bytes 4194304 | tf_op jit(solution)/shard_map/attend/pallas_call | solution.py:220
  120.7 5.7 %collective-permute-start.6 = (bf16[1,512,128]{2,1,0:T(8,128)(2,1)S(1)}, bf16[1,512,128]{2,1,0:T(8,128)(2,1)S(1)}, u32[]{:S(2)}, u32[]{:S(2)}) collective-permute-start(bf16[1,512,128]{2,1,0:T(8,128)(2,1)S(1)} %attend.2.a0), channel_id=1, source_target_pairs={{0,1},{1,2},{2,3},{3,0},{4,5},{5,6},{6,7},{7,4},{8,9},{9,10},{10,1... | collective-permute-start | bytes 393224 | tf_op jit(solution)/shard_map/ppermute | solution.py:307
  126.4 2.7 %collective-permute-start.7 = (bf16[1,512,128]{2,1,0:T(8,128)(2,1)S(1)}, bf16[1,512,128]{2,1,0:T(8,128)(2,1)S(1)}, u32[]{:S(2)}, u32[]{:S(2)}) collective-permute-start(bf16[1,512,128]{2,1,0:T(8,128)(2,1)S(1)} %attend.2.a0), channel_id=1, source_target_pairs={{0,2},{1,3},{2,0},{3,1},{4,6},{5,7},{6,4},{7,5},{8,10},{9,11},{10,... | collective-permute-start | bytes 393224 | tf_op jit(solution)/shard_map/ppermute | solution.py:307
  129.1 3.5 %collective-permute-start.8 = (bf16[1,512,128]{2,1,0:T(8,128)(2,1)S(1)}, bf16[1,512,128]{2,1,0:T(8,128)(2,1)S(1)}, u32[]{:S(2)}, u32[]{:S(2)}) collective-permute-start(bf16[1,512,128]{2,1,0:T(8,128)(2,1)S(1)} %attend.2.a0), channel_id=1, source_target_pairs={{0,3},{1,0},{2,1},{3,2},{4,7},{5,4},{6,5},{7,6},{8,11},{9,8},{10,9... | collective-permute-start | bytes 393224 | tf_op jit(solution)/shard_map/ppermute | solution.py:307
  132.6 7.5 %all-to-all-done.1.got = bf16[128,64,128]{2,1,0:T(8,128)(2,1)} async-done(((bf16[128,64,128]{2,1,0:T(8,128)(2,1)}), bf16[128,64,128]{2,1,0:T(8,128)(2,1)}, u32[]{:S(2)}, u32[]{:S(2)}) %all-to-all-start.1) | async-done | bytes 2097184 | tf_op jit(solution)/shard_map/all_to_all | solution.py:333
  140.1 4.0 %attend.3 = bf16[4,512,128]{2,1,0:T(8,128)(2,1)S(1)} custom-call(bf16[2,512,128]{2,1,0:T(8,128)(2,1)} %get-tuple-element.8.query, bf16[128,64,128]{2,1,0:T(8,128)(2,1)} %all-to-all-done.1.got, f32[4,4096]{1,0:T(4,128)} %copy-done.4, f32[2,512,128]{2,1,0:T(8,128)} %get-tuple-element.9.own, bf16[1,512,128]{2,1,0:T(8,128)(2,1)S(1)} %collective-permute-done.6.refs_0_.a1, ...), custom_call_target="tpu_custom_call" | custom-call | flops 1073741824 | bytes 4194304 | tf_op jit(solution)/shard_map/attend/pallas_call | solution.py:220
  144.2 12.2 %all_to_all.15.last = bf16[4,512,128]{2,1,0:T(8,128)(2,1)S(1)} all-to-all(bf16[4,512,128]{2,1,0:T(8,128)(2,1)S(1)} %attend.3), channel_id=1, replica_groups=mesh['req'=128,'mp'=4] {'mp'}, dimensions={0} | all-to-all | bytes 1048576 | tf_op jit(solution)/shard_map/all_to_all | solution.py:348
  (70 shorter events, 18.3 us)
Async XLA Ops:
  3.4 19.0 %copy-start.5 = (bf16[1024,4,256]{2,1,0:T(4,128)(2,1)S(1)}, bf16[1024,4,256]{2,1,0:T(4,128)(2,1)}, u32[]{:S(2)}) copy-start(bf16[1024,4,256]{2,1,0:T(4,128)(2,1)} %param.12) | copy-start | bytes 6291460
  3.4 76.2 %all-to-all-start = ((bf16[128,72,128]{2,1,0:T(8,128)(2,1)}), bf16[128,72,128]{2,1,0:T(8,128)(2,1)}, u32[]{:S(2)}, u32[]{:S(2)}) async-start(bf16[128,72,128]{2,1,0:T(8,128)(2,1)} %pack.2), calls=%async_computation | async-start | bytes 4718592 | tf_op jit(solution)/shard_map/all_to_all | solution.py:313
  22.4 12.3 %copy-start.6 = (bf16[256,1024]{1,0:T(8,128)(2,1)S(1)}, bf16[256,1024]{1,0:T(8,128)(2,1)}, u32[]{:S(2)}) copy-start(bf16[256,1024]{1,0:T(8,128)(2,1)} %param.13) | copy-start | bytes 1572868
  22.4 18.3 %copy-start.9 = (s32[1,4,128]{2,1,0:T(4,128)S(1)}, s32[1,4,128]{2,1,0:T(4,128)}, u32[]{:S(2)}) copy-start(s32[1,4,128]{2,1,0:T(4,128)} %param.19) | copy-start | bytes 6148
  22.4 18.4 %copy-start.11 = (s32[128]{0:T(128)S(1)}, s32[128]{0:T(128)}, u32[]{:S(2)}) copy-start(s32[128]{0:T(128)} %home_in.3) | copy-start | bytes 1540
  24.0 45.9 %collective-permute-start.3 = (bf16[1024,256]{1,0:T(8,128)(2,1)}, bf16[1024,256]{1,0:T(8,128)(2,1)S(1)}, u32[]{:S(2)}, u32[]{:S(2)}) collective-permute-start(bf16[1024,256]{1,0:T(8,128)(2,1)} %bitcast.28), channel_id=1, source_target_pairs={{0,1},{1,2},{2,3},{3,0},{4,5},{5,6},{6,7},{7,4},{8,9},{9,10},{10,1... | collective-permute-start | bytes 1572872 | tf_op jit(solution)/shard_map/ppermute | solution.py:307
  27.1 42.8 %collective-permute-start.4 = (bf16[1024,256]{1,0:T(8,128)(2,1)}, bf16[1024,256]{1,0:T(8,128)(2,1)}, u32[]{:S(2)}, u32[]{:S(2)}) collective-permute-start(bf16[1024,256]{1,0:T(8,128)(2,1)} %bitcast.28), channel_id=1, source_target_pairs={{0,2},{1,3},{2,0},{3,1},{4,6},{5,7},{6,4},{7,5},{8,10},{9,11},{10,... | collective-permute-start | bytes 1572872 | tf_op jit(solution)/shard_map/ppermute | solution.py:307
  31.5 38.4 %collective-permute-start.5 = (bf16[1024,256]{1,0:T(8,128)(2,1)}, bf16[1024,256]{1,0:T(8,128)(2,1)}, u32[]{:S(2)}, u32[]{:S(2)}) collective-permute-start(bf16[1024,256]{1,0:T(8,128)(2,1)} %bitcast.28), channel_id=1, source_target_pairs={{0,3},{1,0},{2,1},{3,2},{4,7},{5,4},{6,5},{7,6},{8,11},{9,8},{10,9... | collective-permute-start | bytes 1572872 | tf_op jit(solution)/shard_map/ppermute | solution.py:307
  34.7 23.1 %collective-permute-start.11 = (bf16[256,256]{1,0:T(8,128)(2,1)S(1)}, bf16[256,256]{1,0:T(8,128)(2,1)S(1)}, u32[]{:S(2)}, u32[]{:S(2)}) collective-permute-start(bf16[256,256]{1,0:T(8,128)(2,1)S(1)} %get-tuple-element.13), channel_id=1, source_target_pairs={{0,3},{1,0},{2,1},{3,2},{4,7},{5,4},{6,5},{7,6},{8,11},{9,8},{10,9... | collective-permute-start | bytes 393224 | tf_op jit(solution)/shard_map/ppermute | solution.py:307
  36.7 28.8 %collective-permute-start.10 = (bf16[256,256]{1,0:T(8,128)(2,1)S(1)}, bf16[256,256]{1,0:T(8,128)(2,1)}, u32[]{:S(2)}, u32[]{:S(2)}) collective-permute-start(bf16[256,256]{1,0:T(8,128)(2,1)S(1)} %get-tuple-element.14), channel_id=1, source_target_pairs={{0,2},{1,3},{2,0},{3,1},{4,6},{5,7},{6,4},{7,5},{8,10},{9,11},{10,... | collective-permute-start | bytes 393224 | tf_op jit(solution)/shard_map/ppermute | solution.py:307
  44.7 25.2 %copy-start.4 = (f32[4,4096]{1,0:T(4,128)}, f32[4,4096]{1,0:T(4,128)S(1)}, u32[]{:S(2)}) copy-start(f32[4,4096]{1,0:T(4,128)S(1)} %broadcast_multiply_fusion.mask.refs_4_) | copy-start | bytes 196612
  57.8 8.7 %collective-permute-start.9 = (bf16[256,256]{1,0:T(8,128)(2,1)S(1)}, bf16[256,256]{1,0:T(8,128)(2,1)S(1)}, u32[]{:S(2)}, u32[]{:S(2)}) collective-permute-start(bf16[256,256]{1,0:T(8,128)(2,1)S(1)} %get-tuple-element.12), channel_id=1, source_target_pairs={{0,1},{1,2},{2,3},{3,0},{4,5},{5,6},{6,7},{7,4},{8,9},{9,10},{10,1... | collective-permute-start | bytes 393224 | tf_op jit(solution)/shard_map/ppermute | solution.py:307
  65.4 8.0 %copy-start = (bf16[128,8,4,256]{3,1,2,0:T(8,128)(2,1)}, bf16[128,8,4,256]{3,1,2,0:T(8,128)(2,1)S(1)}, u32[]{:S(2)}) copy-start(bf16[128,8,4,256]{3,1,2,0:T(8,128)(2,1)S(1)} %copy.21) | copy-start | bytes 6291460
  73.4 14.9 %copy-start.10 = (s32[1,512]{1,0:T(1,128)S(1)}, s32[1,512]{1,0:T(1,128)}, u32[]{:S(2)}) copy-start(s32[1,512]{1,0:T(1,128)} %param.11) | copy-start | bytes 6148
  79.6 60.5 %all-to-all-start.1 = ((bf16[128,64,128]{2,1,0:T(8,128)(2,1)}), bf16[128,64,128]{2,1,0:T(8,128)(2,1)}, u32[]{:S(2)}, u32[]{:S(2)}) async-start(bf16[128,64,128]{2,1,0:T(8,128)(2,1)} %pack.3), calls=%async_computation.1 | async-start | bytes 4194304 | tf_op jit(solution)/shard_map/all_to_all | solution.py:333
  91.6 17.9 %copy-start.1 = (bf16[512,256]{1,0:T(8,128)(2,1)}, bf16[512,256]{1,0:T(8,128)(2,1)S(1)}, u32[]{:S(2)}) copy-start(bf16[512,256]{1,0:T(8,128)(2,1)S(1)} %gather_fusion) | copy-start | bytes 786436
  91.6 10.6 %collective-permute-start = (bf16[512,256]{1,0:T(8,128)(2,1)S(1)}, bf16[512,256]{1,0:T(8,128)(2,1)S(1)}, u32[]{:S(2)}, u32[]{:S(2)}) collective-permute-start(bf16[512,256]{1,0:T(8,128)(2,1)S(1)} %gather_fusion), channel_id=1, source_target_pairs={{0,1},{1,2},{2,3},{3,0},{4,5},{5,6},{6,7},{7,4},{8,9},{9,10},{10,1... | collective-permute-start | bytes 786440 | tf_op jit(solution)/shard_map/ppermute | solution.py:307
  94.7 13.4 %collective-permute-start.1 = (bf16[512,256]{1,0:T(8,128)(2,1)S(1)}, bf16[512,256]{1,0:T(8,128)(2,1)S(1)}, u32[]{:S(2)}, u32[]{:S(2)}) collective-permute-start(bf16[512,256]{1,0:T(8,128)(2,1)S(1)} %gather_fusion), channel_id=1, source_target_pairs={{0,2},{1,3},{2,0},{3,1},{4,6},{5,7},{6,4},{7,5},{8,10},{9,11},{10,... | collective-permute-start | bytes 786440 | tf_op jit(solution)/shard_map/ppermute | solution.py:307
  98.9 10.6 %collective-permute-start.2 = (bf16[512,256]{1,0:T(8,128)(2,1)S(1)}, bf16[512,256]{1,0:T(8,128)(2,1)S(1)}, u32[]{:S(2)}, u32[]{:S(2)}) collective-permute-start(bf16[512,256]{1,0:T(8,128)(2,1)S(1)} %gather_fusion), channel_id=1, source_target_pairs={{0,3},{1,0},{2,1},{3,2},{4,7},{5,4},{6,5},{7,6},{8,11},{9,8},{10,9... | collective-permute-start | bytes 786440 | tf_op jit(solution)/shard_map/ppermute | solution.py:307
  102.1 7.3 %copy-start.12 = (bf16[512,256]{1,0:T(8,128)(2,1)}, bf16[512,256]{1,0:T(8,128)(2,1)S(1)}, u32[]{:S(2)}) copy-start(bf16[512,256]{1,0:T(8,128)(2,1)S(1)} %collective-permute-done.r1) | copy-start | bytes 786436
  120.7 35.7 %copy-start.2 = (bf16[512,256]{1,0:T(8,128)(2,1)S(1)}, bf16[512,256]{1,0:T(8,128)(2,1)}, u32[]{:S(2)}) copy-start(bf16[512,256]{1,0:T(8,128)(2,1)} %copy-done.1) | copy-start | bytes 786436
  120.7 19.5 %collective-permute-start.6 = (bf16[1,512,128]{2,1,0:T(8,128)(2,1)S(1)}, bf16[1,512,128]{2,1,0:T(8,128)(2,1)S(1)}, u32[]{:S(2)}, u32[]{:S(2)}) collective-permute-start(bf16[1,512,128]{2,1,0:T(8,128)(2,1)S(1)} %attend.2.a0), channel_id=1, source_target_pairs={{0,1},{1,2},{2,3},{3,0},{4,5},{5,6},{6,7},{7,4},{8,9},{9,10},{10,1... | collective-permute-start | bytes 393224 | tf_op jit(solution)/shard_map/ppermute | solution.py:307
  126.4 13.8 %collective-permute-start.7 = (bf16[1,512,128]{2,1,0:T(8,128)(2,1)S(1)}, bf16[1,512,128]{2,1,0:T(8,128)(2,1)S(1)}, u32[]{:S(2)}, u32[]{:S(2)}) collective-permute-start(bf16[1,512,128]{2,1,0:T(8,128)(2,1)S(1)} %attend.2.a0), channel_id=1, source_target_pairs={{0,2},{1,3},{2,0},{3,1},{4,6},{5,7},{6,4},{7,5},{8,10},{9,11},{10,... | collective-permute-start | bytes 393224 | tf_op jit(solution)/shard_map/ppermute | solution.py:307
  129.1 11.1 %collective-permute-start.8 = (bf16[1,512,128]{2,1,0:T(8,128)(2,1)S(1)}, bf16[1,512,128]{2,1,0:T(8,128)(2,1)S(1)}, u32[]{:S(2)}, u32[]{:S(2)}) collective-permute-start(bf16[1,512,128]{2,1,0:T(8,128)(2,1)S(1)} %attend.2.a0), channel_id=1, source_target_pairs={{0,3},{1,0},{2,1},{3,2},{4,7},{5,4},{6,5},{7,6},{8,11},{9,8},{10,9... | collective-permute-start | bytes 393224 | tf_op jit(solution)/shard_map/ppermute | solution.py:307
  (5 other events, 14.3 us)
